TPU v7x, 32 devices: a whole 2x2x4 slice. The times are simulated.
32 devices in a mesh: group: 4 (over x, core), member: 8 (over z, y).
Axes of the slice: x: 2, y: 2, z: 4, core: 2. Of those that a mesh axis runs over, the one named last changes fastest.
Arguments:
- features: bfloat16 [16384, 512], P(('group', 'member')), may hold values from -6 to 6
- cotangent: bfloat16 [16384, 512], P(('group', 'member')), may hold values from -6 to 6
- w_self: bfloat16 [512, 512], replicated, may hold values from -0.25 to 0.25
- w_neigh: bfloat16 [512, 512], replicated, may hold values from -0.25 to 0.25
- bias: float32 [512], replicated, may hold values from -4 to 4
- neighbours: int32 [16384, 16], P(('group', 'member')), may hold values from 0 to 639
- neigh_count: int32 [16384], P(('group', 'member')), may hold values from 1 to 16
- serve_rows: int32 [32, 128], P(('group', 'member')), may hold values from 0 to 511
Outputs:
- grad_features: float32 [16384, 512], P(('group', 'member'))
- grad_self: float32 [512, 512], replicated
- grad_neigh: float32 [512, 512], replicated
- grad_bias: float32 [512], replicated
All inputs are finite; a program needn't handle non-finite values.
Results may differ from a plain program's by a relative error of at most 0.0055.
Values may be sent and summed in bfloat16 or wider, within the bound.
No kernel may reach another device: no remote copies, remote signals or barrier semaphores. Data moves between devices by JAX's collectives and lax.ppermute only.
A program may use at most 64 MiB of HBM per device.

v0:
```python
import math

import jax
import jax.numpy as jnp
from jax import lax
from jax.sharding import PartitionSpec as P


def block_length():
    return 256


def local(features, cotangent, w_self, w_neigh, bias, neighbours, neigh_count, serve_rows):
    own_rows, feat_width = features.shape
    fanout = neighbours.shape[1]
    groups = lax.axis_size("group")
    members = lax.axis_size("member")
    slot_count = serve_rows.shape[1]
    per_peer = slot_count // (groups * members)
    serve_flat = serve_rows.reshape(slot_count)
    outgoing = jnp.take(features, serve_flat, axis=0).reshape(groups, members, per_peer, feat_width)
    incoming = lax.all_to_all(
        lax.all_to_all(outgoing, "group", split_axis=0, concat_axis=0, tiled=True),
        "member",
        split_axis=1,
        concat_axis=1,
        tiled=True,
    )
    lookup = jnp.concatenate([features, incoming.reshape(slot_count, feat_width)], axis=0)
    block_size = block_length()
    block_count = own_rows // block_size
    index_blocks = neighbours.reshape(block_count, block_size, fanout)
    count_blocks = neigh_count.reshape(block_count, block_size)
    positions = jnp.arange(fanout, dtype=jnp.int32)

    def aggregate(blocks_pair):
        index_block, count_block = blocks_pair
        in_use = (positions[None, :] < count_block[:, None]).astype(jnp.bfloat16)
        gathered = jnp.take(lookup, index_block, axis=0)
        summed = jnp.einsum("bk,bkw->bw", in_use, gathered, preferred_element_type=jnp.float32)
        return (summed / count_block[:, None].astype(jnp.float32)).astype(jnp.bfloat16)

    aggregated = lax.map(aggregate, (index_blocks, count_blocks)).reshape(own_rows, feat_width)
    pre = jnp.dot(features, w_self, preferred_element_type=jnp.float32)
    pre = pre + jnp.dot(aggregated, w_neigh, preferred_element_type=jnp.float32) + bias
    sigmoid_pre = jax.nn.sigmoid(pre)
    pre_grad = (
        cotangent.astype(jnp.float32) * sigmoid_pre * (1.0 + pre * (1.0 - sigmoid_pre))
    ).astype(jnp.bfloat16)
    local_self = jnp.einsum("nd,ne->de", features, pre_grad, preferred_element_type=jnp.float32)
    local_neigh = jnp.einsum("nd,ne->de", aggregated, pre_grad, preferred_element_type=jnp.float32)
    local_bias = jnp.sum(pre_grad.astype(jnp.float32), axis=0)
    summed_grads = lax.psum((local_self, local_neigh, local_bias), ("group", "member"))
    factor = 1.0 / math.sqrt(own_rows * groups * members)
    agg_grad = jnp.einsum("ne,de->nd", pre_grad, w_neigh, preferred_element_type=jnp.float32)
    message = (agg_grad / neigh_count[:, None].astype(jnp.float32)).astype(jnp.bfloat16)
    message_blocks = message.reshape(block_count, block_size, feat_width)
    sink = own_rows + slot_count

    def spread(grad_table, inputs):
        index_block, count_block, message_block = inputs
        in_use = positions[None, :] < count_block[:, None]
        target = jnp.where(in_use, index_block, sink).reshape(-1)
        values = jnp.broadcast_to(
            message_block.astype(jnp.float32)[:, None, :], (block_size, fanout, feat_width)
        )
        return (grad_table.at[target].add(values.reshape(-1, feat_width)), None)

    start_table = jnp.zeros((sink + 1, feat_width), jnp.float32)
    grad_table, _ = lax.scan(spread, start_table, (index_blocks, count_blocks, message_blocks))
    remote_grad = (
        grad_table[own_rows:sink]
        .astype(jnp.bfloat16)
        .reshape(groups, members, per_peer, feat_width)
    )
    returned = lax.all_to_all(
        lax.all_to_all(remote_grad, "group", split_axis=0, concat_axis=0, tiled=True),
        "member",
        split_axis=1,
        concat_axis=1,
        tiled=True,
    )
    owner_sum = (
        jnp.zeros((own_rows, feat_width), jnp.float32)
        .at[serve_flat]
        .add(returned.reshape(slot_count, feat_width).astype(jnp.float32))
    )
    self_grad = jnp.einsum("ne,de->nd", pre_grad, w_self, preferred_element_type=jnp.float32)
    grad_features = self_grad + grad_table[:own_rows] + owner_sum
    return (
        grad_features,
        summed_grads[0] * factor,
        summed_grads[1] * factor,
        summed_grads[2] * factor,
    )


def solution(mesh):
    placed = (
        P(("group", "member"), None),
        P(("group", "member"), None),
        P(),
        P(),
        P(),
        P(("group", "member"), None),
        P(("group", "member")),
        P(("group", "member"), None),
    )
    return jax.shard_map(
        local,
        mesh=mesh,
        in_specs=placed,
        out_specs=(P(("group", "member"), None), P(), P(), P()),
        check_vma=False,
    )
```

profile of v0, /device:TPU:0, one launch (start us, length us, event | category | flops | bytes accessed | tf_op | source)
XLA Modules:
  0.0 228.5 jit_solution(11548430528020139316)
XLA Ops:
  8.4 2.0 gather_fusion.1
  13.2 4.2 %all-to-all-start = ((bf16[4,8,4,512]{3,2,1,0:T(4,128)(2,1)}), bf16[4,8,4,512]{3,2,1,0:T(4,128)(2,1)S(1)}, u32[]{:S(2)}, u32[]{:S(2)}) async-start(bf16[4,8,4,512]{3,2,1,0:T(4,128)(2,1)} %broadcast_select_fusion), calls=%async_computation | async-start | bytes 262144 | tf_op jit(solution)/shard_map/all_to_all | solution.py:23
  19.7 2.4 %all-to-all-done = bf16[4,8,4,512]{3,2,1,0:T(4,128)(2,1)S(1)} async-done(((bf16[4,8,4,512]{3,2,1,0:T(4,128)(2,1)}), bf16[4,8,4,512]{3,2,1,0:T(4,128)(2,1)S(1)}, u32[]{:S(2)}, u32[]{:S(2)}) %all-to-all-start) | async-done | bytes 131104 | tf_op jit(solution)/shard_map/all_to_all | solution.py:23
  22.8 6.4 %all-to-all-start.1 = ((bf16[4,8,4,512]{3,2,0,1:T(4,128)(2,1)}), bf16[4,8,4,512]{3,2,0,1:T(4,128)(2,1)S(1)}, u32[]{:S(2)}, u32[]{:S(2)}) async-start(bf16[4,8,4,512]{3,2,0,1:T(4,128)(2,1)} %copy.57), calls=%async_computation.1 | async-start | bytes 262144 | tf_op jit(solution)/shard_map/all_to_all | solution.py:22
  29.2 2.6 %fusion.15 = f32[512,512]{1,0:T(8,128)} fusion(bf16[512,512]{1,0:T(8,128)(2,1)} %param.12, bf16[512,512]{1,0:T(8,128)(2,1)} %param.14), kind=kOutput, calls=%fused_computation.47 | convolution fusion | flops 268435456 | bytes 2097152 | tf_op jit(solution)/shard_map/dot_general | solution.py:44
  31.8 4.7 %all-to-all-done.1 = bf16[4,8,4,512]{3,2,0,1:T(4,128)(2,1)S(1)} async-done(((bf16[4,8,4,512]{3,2,0,1:T(4,128)(2,1)}), bf16[4,8,4,512]{3,2,0,1:T(4,128)(2,1)S(1)}, u32[]{:S(2)}, u32[]{:S(2)}) %all-to-all-start.1) | async-done | bytes 131104 | tf_op jit(solution)/shard_map/all_to_all | solution.py:22
  36.6 41.2 %while.22 = (s32[]{:T(128)}, bf16[2,256,512]{2,1,0:T(8,128)(2,1)S(1)}, s32[2,256]{1,0:T(2,128)S(1)}, s32[2,256,16]{2,1,0:T(8,128)S(1)}, bf16[640,512]{1,0:T(8,128)(2,1)S(1)}, /*index=5*/s32[]{:T(128)}) while((s32[]{:T(128)}, bf16[2,256,512]{2,1,0:T(8,128)(2,1)S(1)}, s32[2,256]{1,0:T(2,128)S(1)}, s32[2,256,16]{2,1,0:T(8,128)S(1)}, ...), condition=%wide.region_1.2_spmd.clone, body=%wide.region_0.1_spmd.clone.sunk | while | flops 6598914 | bytes 14047325 | solution.py:43
  36.8 17.3 %gather_fusion = bf16[4096,512]{1,0:T(8,128)(2,1)} fusion(bf16[640,512]{1,0:T(8,128)(2,1)S(1)} %get-tuple-element.291, s32[4096]{0:T(1024)S(1)} %broadcast_clamp_fusion.2), kind=kCustom, calls=%fused_computation.clone.clone.1 | custom fusion | bytes 8404992 | tf_op jit(solution)/shard_map/while/body/eval_jaxpr/jit(_take)/gather | solution.py:39
  54.3 2.8 %fusion.36 = f32[256,1,512]{2,1,0:T(1,128)S(1)} fusion(bf16[256,16,512]{2,1,0:T(8,128)(2,1)} %bitcast.70, pred[256,16]{1,0:T(8,128)(4,1)S(1)} %compare_and_fusion.3, pred[256,16,1]{1,0,2:T(32,128)(4,1)S(1)} %fusion.35), kind=kOutput, calls=%fused_computation.6.clone.1 | convolution fusion | flops 6291456 | bytes 4726784 | tf_op jit(solution)/shard_map/while/body/eval_jaxpr/bk,bkw->bw/dot_general | solution.py:40
  57.4 17.3 %gather_fusion = bf16[4096,512]{1,0:T(8,128)(2,1)} fusion(bf16[640,512]{1,0:T(8,128)(2,1)S(1)} %get-tuple-element.291, s32[4096]{0:T(1024)S(1)} %broadcast_clamp_fusion.2), kind=kCustom, calls=%fused_computation.clone.clone.1 | custom fusion | bytes 8404992 | tf_op jit(solution)/shard_map/while/body/eval_jaxpr/jit(_take)/gather | solution.py:39
  74.9 2.8 %fusion.36 = f32[256,1,512]{2,1,0:T(1,128)S(1)} fusion(bf16[256,16,512]{2,1,0:T(8,128)(2,1)} %bitcast.70, pred[256,16]{1,0:T(8,128)(4,1)S(1)} %compare_and_fusion.3, pred[256,16,1]{1,0,2:T(32,128)(4,1)S(1)} %fusion.35), kind=kOutput, calls=%fused_computation.6.clone.1 | convolution fusion | flops 6291456 | bytes 4726784 | tf_op jit(solution)/shard_map/while/body/eval_jaxpr/bk,bkw->bw/dot_general | solution.py:40
  77.9 2.7 %convert_reduce_fusion = (f32[512]{0:T(512)}, bf16[512,512]{1,0:T(8,128)(2,1)S(1)}) fusion(f32[512]{0:T(512)S(1)} %copy-done.6, f32[512,512]{1,0:T(8,128)} %fusion.15, bf16[512,512]{1,0:T(8,128)(2,1)S(1)} %bitcast.74, bf16[512,512]{1,0:T(8,128)(2,1)S(1)} %copy-done, bf16[512,512]{1,0:T(8,128)(2,1)} %param.13), kind=kOutput, calls=%fused_computation.33 | convolution fusion | flops 272104960 | bytes 3149824 | tf_op jit(solution)/shard_map/dot_general | solution.py:45
  84.2 61.2 %while.23 = (s32[]{:T(128)}, f32[641,512]{1,0:T(8,128)S(1)}, s32[2,256]{1,0:T(2,128)S(1)}, s32[2,256,16]{2,1,0:T(8,128)S(1)}, bf16[2,256,512]{2,1,0:T(8,128)(2,1)S(1)}, /*index=5*/s32[]{:T(128)}) while((s32[]{:T(128)}, f32[641,512]{1,0:T(8,128)S(1)}, s32[2,256]{1,0:T(2,128)S(1)}, s32[2,256,16]{2,1,0:T(8,128)S(1)}, ...), condition=%wide.region_4.5_spmd.clone, body=%wide.region_2.4_spmd.clone.sunk | while | flops 2248706 | bytes 34999384 | solution.py:70
  84.7 4.3 %broadcast_in_dim.77 = f32[256,16,512]{2,1,0:T(8,128)} broadcast(f32[256,512]{1,0:T(8,128)S(1)} %bitcast_convert_fusion.2), dimensions={0,2} | broadcast | bytes 8912896 | tf_op jit(solution)/shard_map/while/body/eval_jaxpr/broadcast_in_dim | solution.py:64
  89.0 25.8 %scatter_fusion = f32[641,512]{1,0:T(8,128)S(1)} fusion(f32[641,512]{1,0:T(8,128)S(1)} %get-tuple-element.300, s32[4096]{0:T(1024)S(1)} %bitcast.73, f32[4096,512]{1,0:T(8,128)} %bitcast.69), kind=kCustom, calls=%fused_computation.2.clone.clone.1 | custom fusion | flops 2097152 | bytes 25182208 | tf_op jit(solution)/shard_map/while/body/eval_jaxpr/scatter-add | solution.py:67
  115.3 4.3 %broadcast_in_dim.77 = f32[256,16,512]{2,1,0:T(8,128)} broadcast(f32[256,512]{1,0:T(8,128)S(1)} %bitcast_convert_fusion.2), dimensions={0,2} | broadcast | bytes 8912896 | tf_op jit(solution)/shard_map/while/body/eval_jaxpr/broadcast_in_dim | solution.py:64
  119.6 25.8 %scatter_fusion = f32[641,512]{1,0:T(8,128)S(1)} fusion(f32[641,512]{1,0:T(8,128)S(1)} %get-tuple-element.300, s32[4096]{0:T(1024)S(1)} %bitcast.73, f32[4096,512]{1,0:T(8,128)} %bitcast.69), kind=kCustom, calls=%fused_computation.2.clone.clone.1 | custom fusion | flops 2097152 | bytes 25182208 | tf_op jit(solution)/shard_map/while/body/eval_jaxpr/scatter-add | solution.py:67
  145.5 7.0 %all_to_all.20 = bf16[4,8,4,512]{3,2,1,0:T(4,128)(2,1)S(1)} all-to-all(bf16[4,8,4,512]{3,2,1,0:T(4,128)(2,1)S(1)} %reshape.183), channel_id=1, replica_groups=mesh['group'=4,'member'=8] {'group'}, dimensions={0} | all-to-all | bytes 262144 | tf_op jit(solution)/shard_map/all_to_all | solution.py:77
  153.2 3.4 %all-to-all-start.3 = ((bf16[4,8,4,512]{3,2,0,1:T(4,128)(2,1)}), bf16[4,8,4,512]{3,2,0,1:T(4,128)(2,1)S(1)}, u32[]{:S(2)}, u32[]{:S(2)}) async-start(bf16[4,8,4,512]{3,2,0,1:T(4,128)(2,1)} %copy.61), calls=%async_computation.3 | async-start | bytes 262144 | tf_op jit(solution)/shard_map/all_to_all | solution.py:76
  158.1 40.5 %psum.23 = f32[512]{0:T(512)S(1)} all-reduce(f32[512]{0:T(512)} %get-tuple-element.209), channel_id=1, replica_groups=mesh['group'=4,'member'=8] {'group','member'}, use_global_device_ids=true, to_apply=%region_9.10 | all-reduce | flops 512 | bytes 4096 | tf_op jit(solution)/shard_map/psum | solution.py:53
  199.5 1.9 scatter_fusion.1
  201.4 13.6 %all-reduce.3.cloned.1.call-done = (f32[512,512]{0,1:T(8,128)}, f32[512,512]{0,1:T(8,128)}) async-done(((f32[512,512]{0,1:T(8,128)}, f32[512,512]{0,1:T(8,128)}), (f32[512,512]{0,1:T(8,128)}, f32[512,512]{0,1:T(8,128)})) %all-reduce.3.cloned.1.call-update) | async-done | bytes 2097168 | tf_op jit(solution)/shard_map/psum | solution.py:53
  215.0 2.7 %broadcast_multiply_fusion = (f32[512,512]{0,1:T(8,128)S(1)}, f32[512,512]{0,1:T(8,128)}) fusion(f32[512,512]{0,1:T(8,128)} %get-tuple-element.208, f32[512,512]{0,1:T(8,128)} %get-tuple-element.207), kind=kLoop, calls=%fused_computation.36 | loop fusion | flops 524288 | bytes 4194304 | tf_op jit(solution)/shard_map/mul | solution.py:93
  217.8 2.5 %copy.65 = f32[512,512]{1,0:T(8,128)} copy(f32[512,512]{0,1:T(8,128)} %get-tuple-element.212) | data formatting | bytes 2097152
  (76 shorter events, 16.9 us)
Async XLA Ops:
  7.2 70.7 %copy-start = (bf16[512,512]{1,0:T(8,128)(2,1)S(1)}, bf16[512,512]{1,0:T(8,128)(2,1)}, u32[]{:S(2)}) copy-start(bf16[512,512]{1,0:T(8,128)(2,1)} %param.15) | copy-start | bytes 1572868
  7.2 29.4 %copy-start.1 = (bf16[512,512]{1,0:T(8,128)(2,1)S(1)}, bf16[512,512]{1,0:T(8,128)(2,1)}, u32[]{:S(2)}) copy-start(bf16[512,512]{1,0:T(8,128)(2,1)} %param.12) | copy-start | bytes 1572868
  7.9 0.5 copy-start.5
  13.2 8.8 %all-to-all-start = ((bf16[4,8,4,512]{3,2,1,0:T(4,128)(2,1)}), bf16[4,8,4,512]{3,2,1,0:T(4,128)(2,1)S(1)}, u32[]{:S(2)}, u32[]{:S(2)}) async-start(bf16[4,8,4,512]{3,2,1,0:T(4,128)(2,1)} %broadcast_select_fusion), calls=%async_computation | async-start | bytes 262144 | tf_op jit(solution)/shard_map/all_to_all | solution.py:23
  22.8 13.7 %all-to-all-start.1 = ((bf16[4,8,4,512]{3,2,0,1:T(4,128)(2,1)}), bf16[4,8,4,512]{3,2,0,1:T(4,128)(2,1)S(1)}, u32[]{:S(2)}, u32[]{:S(2)}) async-start(bf16[4,8,4,512]{3,2,0,1:T(4,128)(2,1)} %copy.57), calls=%async_computation.1 | async-start | bytes 262144 | tf_op jit(solution)/shard_map/all_to_all | solution.py:22
  29.1 185.9 %all-reduce.3.cloned.1.call-start = ((), (), s32[]{:S(2)}) async-start(), calls=%async_computation.4 | async-start | bytes 4194304 | tf_op jit(solution)/shard_map/psum | solution.py:53
  36.6 41.2 %copy-start.6 = (f32[512]{0:T(512)S(1)}, f32[512]{0:T(512)}, u32[]{:S(2)}) copy-start(f32[512]{0:T(512)} %param.16) | copy-start | bytes 6148
  80.6 3.4 %copy-start.3 = (bf16[512,512]{1,0:T(8,128)(2,1)}, bf16[512,512]{1,0:T(8,128)(2,1)S(1)}, u32[]{:S(2)}) copy-start(bf16[512,512]{1,0:T(8,128)(2,1)S(1)} %get-tuple-element.210) | copy-start | bytes 1572868
  84.2 72.4 %copy-start.4 = (bf16[512,512]{1,0:T(8,128)(2,1)S(1)}, bf16[512,512]{1,0:T(8,128)(2,1)}, u32[]{:S(2)}) copy-start(bf16[512,512]{1,0:T(8,128)(2,1)} %copy-done.3) | copy-start | bytes 1572868
  153.2 45.9 %all-to-all-start.3 = ((bf16[4,8,4,512]{3,2,0,1:T(4,128)(2,1)}), bf16[4,8,4,512]{3,2,0,1:T(4,128)(2,1)S(1)}, u32[]{:S(2)}, u32[]{:S(2)}) async-start(bf16[4,8,4,512]{3,2,0,1:T(4,128)(2,1)} %copy.61), calls=%async_computation.3 | async-start | bytes 262144 | tf_op jit(solution)/shard_map/all_to_all | solution.py:76
  201.4 20.2 %copy-start.2 = (f32[512,512]{1,0:T(8,128)}, f32[512,512]{1,0:T(8,128)S(1)}, u32[]{:S(2)}) copy-start(f32[512,512]{1,0:T(8,128)S(1)} %scatter_fusion.1) | copy-start | bytes 3145732
Sparse Core Ops, SparseCore 0:
  84.1 130.8 all-reduce.2
where the time goes:
time: 229 us; the launch traced here: 228 us
  other arithmetic  61.4 us (27%)
  local copies, waits for them, and re-layouts  54.5 us (24%)
  blocking collectives  47.5 us (21%)
  waiting for transfers between devices  20.7 us (9%)
  matrix products  15.8 us (7%)
  between operations  14.2 us (6%)
  starting transfers between devices  14 us (6%)
    scatter-add x2, other arithmetic, spread(): return (grad_table.at[target].add(values.reshape(-1, feat_width)), None)  51.6 us
    psum x1, blocking collectives, local(): lax.psum((local_self, local_neigh, local_bias), ('group', 'member'))  40.5 us
    gather x2, local copies, waits for them, and re-layouts, aggregate(): gathered = jnp.take(lookup, index_block, axis=0)  34.7 us
    psum x1, waiting for transfers between devices, local(): lax.psum((local_self, local_neigh, local_bias), ('group', 'member'))  13.6 us
    broadcast_in_dim x2, local copies, waits for them, and re-layouts, spread(): jnp.broadcast_to(message_block.astype(jnp.float32)[:, None, :], (block_si...  8.59 us
    all_to_all x1, blocking collectives, local(): lax.all_to_all(remote_grad, 'group', split_axis=0, concat_axis=0, tiled=T...  7.02 us
    all_to_all x1, starting transfers between devices, local(): lax.all_to_all(lax.all_to_all(outgoing, 'group', split_axis=0, concat_axi...  6.37 us
    unnamed x18, local copies, waits for them, and re-layouts  5.76 us
  transfers between devices with their start and end apart: 4, of which 3 were waited for; matrix products, arithmetic and copies ran while one was open for 31% of the time, Pallas kernels for 0%

commit v1 on v0

v1 whole, which is shorter than its diff:
```python
import functools
import math

import jax
import jax.numpy as jnp
from jax import lax
from jax.experimental import pallas as pl
from jax.experimental.pallas import tpu as pltpu
from jax.sharding import Mesh
from jax.sharding import PartitionSpec as P

BF16 = jnp.bfloat16
F32 = jnp.float32


def product(left, right, left_dim, right_dim):
    return lax.dot_general(
        left, right, (((left_dim,), (right_dim,)), ((), ())), preferred_element_type=F32
    )


def call(body, outs, scratch=(), flops=0, moved=0, smem=0, name=None):
    def run(*operands):
        return pl.pallas_call(
            body,
            out_shape=outs,
            in_specs=[
                pl.BlockSpec(memory_space=pltpu.SMEM if at < smem else pltpu.VMEM)
                for at in range(len(operands))
            ],
            out_specs=jax.tree.map(lambda _: pl.BlockSpec(memory_space=pltpu.VMEM), outs),
            scratch_shapes=list(scratch),
            compiler_params=pltpu.CompilerParams(vmem_limit_bytes=40 * 1024 * 1024),
            cost_estimate=pl.CostEstimate(flops=flops, bytes_accessed=moved, transcendentals=0),
            name=name,
        )(*operands)

    return run


def serve_kernel(serve_ref, features_ref, out_ref):
    own_rows = features_ref.shape[0]
    slots = serve_ref.shape[1]
    row = lax.broadcasted_iota(jnp.int32, (own_rows, slots), 0)
    picks = (row == serve_ref[...]).astype(F32).astype(BF16)
    rows = product(picks, features_ref[...], 0, 0)
    out_ref[...] = rows.reshape(out_ref.shape).astype(BF16)


def own_kernel(
    neighbours_ref, count_ref, features_ref, w_self_ref, bias_ref,
    counts_ref, inverse_ref, own_sum_ref, pre_ref, live_ref,
):
    own_rows, fanout = neighbours_ref.shape
    table_rows = counts_ref.shape[0]
    count = count_ref[...]
    position = lax.broadcasted_iota(jnp.int32, (fanout, own_rows), 0)
    live_ref[...] = jnp.where(position < count, neighbours_ref[...].T, -1)
    inverse_ref[...] = jnp.broadcast_to(1.0 / count.astype(F32), (128, own_rows)).T
    step = 32

    def fill(at, carry):
        start = pl.multiple_of(at * step, step)
        row = lax.broadcasted_iota(jnp.int32, (step, own_rows), 0) + start
        total = jnp.zeros((step, own_rows), F32)
        for k in range(fanout):
            total = total + jnp.where(row == live_ref[k : k + 1, :], 1.0, 0.0)
        counts_ref[pl.ds(start, step), :] = total.astype(BF16)
        return carry

    lax.fori_loop(0, table_rows // step, fill, 0)
    features = features_ref[...]
    own_sum_ref[...] = product(counts_ref[:own_rows, :], features, 0, 0)
    pre_ref[...] = product(features, w_self_ref[...], 1, 0) + bias_ref[...]


def spread_wide(inverse, width):
    return jnp.concatenate([inverse] * (width // 128), axis=1)


def main_kernel(
    core_ref, incoming_ref, counts_ref, inverse_ref, own_sum_ref, pre_ref, features_ref, cotangent_ref, w_neigh_ref,
    send_ref, keep_ref, keep_rows_ref, bias_ref, pre_grad_ref, message_ref, rows_ref,
):
    own_rows, width = features_ref.shape
    slots = rows_ref.shape[0]
    first = core_ref[0] == 0
    inverse = spread_wide(inverse_ref[...], width)
    slot_counts = counts_ref[own_rows:, :]
    incoming = incoming_ref[...].astype(F32).reshape(slots, width).astype(BF16)
    summed = own_sum_ref[...] + product(slot_counts, incoming, 0, 0)
    aggregated = (summed * inverse).astype(BF16)
    pre = pre_ref[...] + product(aggregated, w_neigh_ref[...], 1, 0)
    sigmoid_pre = jax.nn.sigmoid(pre)
    pre_grad = (
        cotangent_ref[...].astype(F32) * sigmoid_pre * (1.0 + pre * (1.0 - sigmoid_pre))
    ).astype(BF16)
    pre_grad_ref[...] = pre_grad
    features = features_ref[...]
    keep_ref[...] = product(jnp.where(first, features, aggregated), pre_grad, 0, 0)
    send_ref[:own_rows, :] = product(
        jnp.where(first, aggregated, features), pre_grad, 0, 0
    ).astype(BF16)
    message = (product(pre_grad, w_neigh_ref[...], 1, 1) * inverse).astype(BF16)
    message_ref[...] = message
    rows_ref[...] = product(slot_counts, message, 1, 0)
    half = slots // 2
    blocks, length = keep_rows_ref.shape[0], keep_rows_ref.shape[1]
    for at in range(blocks):
        mine = pl.multiple_of((at * 2 + core_ref[0]) * length, length)
        other = pl.multiple_of((at * 2 + 1 - core_ref[0]) * length, length)
        keep_rows_ref[at] = rows_ref[pl.ds(mine, length), :].astype(BF16)
        send_ref[own_rows + at * length : own_rows + (at + 1) * length, :] = rows_ref[
            pl.ds(other, length), :
        ].astype(BF16)
    bias = jnp.sum(pre_grad.astype(F32), axis=0, keepdims=True).astype(BF16)
    bias_ref[...] = jnp.broadcast_to(bias, bias_ref.shape)
    send_ref[own_rows + half :, :] = jnp.broadcast_to(bias, bias_ref.shape)


def pack_kernel(order, received_ref, keep_ref, keep_rows_ref, bias_ref, out_ref):
    width = keep_ref.shape[1]
    peers, length = out_ref.shape[0], out_ref.shape[1]
    blocks, block_rows = keep_rows_ref.shape[0], keep_rows_ref.shape[1]
    half = blocks * block_rows
    own_rows = keep_ref.shape[0]
    share = own_rows // peers
    cap = half // peers
    keep_rows = keep_rows_ref[...].astype(F32).reshape(half, width)
    other_rows = received_ref[own_rows : own_rows + half, :].astype(F32)
    bias = (
        bias_ref[...].astype(F32) + received_ref[own_rows + half :, :].astype(F32)
    )
    summed = keep_ref[...] + received_ref[:own_rows, :].astype(F32)
    for peer in range(peers):
        at = order[peer] * share
        parts = [
            summed[at : at + share],
            keep_rows[peer * cap : (peer + 1) * cap],
            other_rows[peer * cap : (peer + 1) * cap],
            bias[: length - share - 2 * cap],
        ]
        out_ref[peer] = jnp.concatenate(parts, axis=0).astype(BF16)


def own_grad_kernel(pre_grad_ref, w_self_ref, counts_ref, message_ref, out_ref):
    own_rows = pre_grad_ref.shape[0]
    out_ref[...] = product(pre_grad_ref[...], w_self_ref[...], 1, 1) + product(
        counts_ref[:own_rows, :], message_ref[...], 1, 0
    )


def sum_kernel(factor, share, cap, payload_ref, out_ref, bias_ref):
    out = jnp.sum(payload_ref[:, :share, :].astype(F32), axis=0).astype(BF16)
    for copy in range(out_ref.shape[0]):
        out_ref[copy] = out
    at = share + 2 * cap
    tail = payload_ref[:, share:, :].astype(F32)
    bias_ref[...] = jnp.sum(tail[:, at - share, :], axis=0, keepdims=True) * factor


def owner_kernel(share, cap, core_ref, serve_ref, payload_ref, base_ref, out_ref):
    own_rows, width = base_ref.shape
    slots = serve_ref.shape[1]
    peers = payload_ref.shape[0]
    blocks = serve_ref.shape[0]
    tail = payload_ref[:, share:, :].astype(F32)
    half = peers * cap
    mine = tail[:, :cap, :].reshape(half, width)
    other = tail[:, cap : 2 * cap, :].reshape(half, width)
    first = core_ref[0] == 0
    rows = jnp.concatenate(
        [jnp.where(first, mine, other), jnp.where(first, other, mine)], axis=0
    ).astype(BF16)
    row = lax.broadcasted_iota(jnp.int32, (own_rows, slots), 0)
    picks = (row == serve_ref[...]).astype(F32).astype(BF16)
    out_ref[...] = base_ref[...] + product(picks, rows, 1, 0)


def finish_kernel(factor, core_ref, mine_ref, other_ref, self_ref, neigh_ref):
    first = core_ref[0] == 0
    mine, other = mine_ref[...], other_ref[...]
    self_ref[...] = jnp.where(first, mine, other).astype(F32) * factor
    neigh_ref[...] = jnp.where(first, other, mine).astype(F32) * factor


def local(features, cotangent, w_self, w_neigh, bias, neighbours, neigh_count, serve_rows):
    own_rows, width = features.shape
    fanout = neighbours.shape[1]
    across = lax.axis_size("across")
    outer, inner = lax.axis_size("outer"), lax.axis_size("inner")
    members = outer * inner
    peers = across * members
    devices = 2 * peers
    slots = serve_rows.shape[1]
    cap = slots // devices
    half = slots // 2
    table_rows = own_rows + slots
    share = own_rows // peers
    length = -(-(share + 2 * cap + 1) // 16) * 16
    everyone = ("across", "core", "outer", "inner")
    plane = ("across", "outer", "inner")
    core = lax.axis_index("core").astype(jnp.int32).reshape(1)
    swap = [(0, 1), (1, 0)]
    factor = 1.0 / math.sqrt(own_rows * devices)
    shape = jax.ShapeDtypeStruct
    cube = 2 * own_rows * own_rows * width

    outgoing = call(
        serve_kernel, shape((devices, cap, width), BF16), flops=cube // 4, moved=1 << 20, name="serve"
    )(serve_rows, features)
    incoming = lax.all_to_all(outgoing, everyone, 0, 0, tiled=True)
    counts, inverse, own_sum, pre = call(
        own_kernel,
        (
            shape((table_rows, own_rows), BF16),
            shape((own_rows, 128), F32),
            shape((own_rows, width), F32),
            shape((own_rows, width), F32),
        ),
        scratch=[pltpu.VMEM((fanout, own_rows), jnp.int32)],
        flops=20 * cube,
        moved=4 << 20,
        name="own_aggregate",
    )(neighbours, neigh_count.reshape(1, own_rows), features, w_self, bias.reshape(1, width))
    send, keep, keep_rows, own_bias, pre_grad, message = call(
        main_kernel,
        (
            shape((own_rows + half + 16, width), BF16),
            shape((own_rows, width), F32),
            shape((across, members * cap, width), BF16),
            shape((16, width), BF16),
            shape((own_rows, width), BF16),
            shape((own_rows, width), BF16),
        ),
        scratch=[pltpu.VMEM((slots, width), F32)],
        flops=5 * cube,
        moved=8 << 20,
        smem=1,
        name="layer_grad",
    )(core, incoming, counts, inverse, own_sum, pre, features, cotangent, w_neigh)
    received = lax.ppermute(send, "core", swap)
    order = [
        (a * inner + i) * outer + o
        for a in range(across) for o in range(outer) for i in range(inner)
    ]
    payload = call(
        functools.partial(pack_kernel, order),
        shape((peers, length, width), BF16),
        flops=cube // 4,
        moved=4 << 20,
        name="pack",
    )(received, keep, keep_rows, own_bias)
    arrived = lax.all_to_all(payload, plane, 0, 0, tiled=True)
    base = call(
        own_grad_kernel, shape((own_rows, width), F32), flops=2 * cube, moved=4 << 20, name="own_grad"
    )(pre_grad, w_self, counts, message)
    summed, bias_sum = call(
        functools.partial(sum_kernel, factor, share, cap),
        (shape((outer, share, width), BF16), shape((1, width), F32)),
        flops=cube // 8,
        moved=1 << 20,
        name="sum_shares",
    )(arrived)
    column = lax.all_to_all(summed, "outer", 0, 0, tiled=True).reshape(outer * share, width)
    mine = lax.all_gather(column, ("across", "inner"), axis=0, tiled=True)
    serve_order = serve_rows.reshape(across, 2, members * cap).transpose(1, 0, 2).reshape(1, slots)
    grad_features = call(
        functools.partial(owner_kernel, share, cap),
        shape((own_rows, width), F32),
        flops=cube // 4,
        moved=3 << 20,
        smem=1,
        name="owner_sum",
    )(core, serve_order, arrived, base)
    other = lax.ppermute(mine, "core", swap)
    grad_self, grad_neigh = call(
        functools.partial(finish_kernel, factor),
        (shape((own_rows, width), F32), shape((own_rows, width), F32)),
        flops=cube // 8,
        moved=3 << 20,
        smem=1,
        name="finish",
    )(core, mine, other)
    return grad_features, grad_self, grad_neigh, bias_sum.reshape(width)


def solution(mesh):
    groups, members = mesh.shape["group"], mesh.shape["member"]
    outer = 2
    while outer * outer < members:
        outer *= 2
    fine = Mesh(
        mesh.devices.reshape(groups // 2, 2, outer, members // outer),
        ("across", "core", "outer", "inner"),
    )
    nodes = ("across", "core", "outer", "inner")
    rows = P(nodes, None)
    return jax.shard_map(
        local,
        mesh=fine,
        in_specs=(rows, rows, P(), P(), P(), rows, P(nodes), rows),
        out_specs=(rows, P(), P(), P()),
        check_vma=False,
    )
```

time: 229 us -> 80.1 us (0.35)
  other arithmetic: 61.4 us -> 0.66 us
  local copies, waits for them, and re-layouts: 54.5 us -> 10.5 us
  waiting for transfers between devices: 20.7 us -> 3 us
  matrix products: 15.8 us -> 0 us
  between operations: 14.2 us -> 0.77 us
  Pallas kernels: 0 us -> 11.2 us
  starting transfers between devices: 14 us -> 7.55 us
    scatter-add x3 -> x0, other arithmetic: 53.5 us -> none  [the longest x2 51.6 us: spread(): return (grad_table.at[target].add(values.reshape(-1, feat_width)), None)]
    psum x1 -> x0, blocking collectives: 40.5 us -> none  [local(): lax.psum((local_self, local_neigh, local_bias), ('group', 'member'))]
    gather x4 -> x0, local copies, waits for them, and re-layouts: 36.7 us -> none  [the longest x2 34.7 us: aggregate(): gathered = jnp.take(lookup, index_block, axis=0)]
    all_to_all x1 -> x2, blocking collectives: 7.02 us -> 36 us  [the longest x1 27.2 us: local(): arrived = lax.all_to_all(payload, plane, 0, 0, tiled=True)]
    dot_general x8 -> x0, matrix products: 15.8 us -> none  [the longest x2 5.62 us: aggregate(): jnp.einsum('bk,bkw->bw', in_use, gathered, preferred_element_type=jnp.flo...]
    psum x1 -> x0, waiting for transfers between devices: 13.6 us -> none  [local(): lax.psum((local_self, local_neigh, local_bias), ('group', 'member'))]
    pallas_call x0 -> x8, Pallas kernels: none -> 11.2 us  [run(): pl.pallas_call(body, out_shape=outs, in_specs=[pl.BlockSpec(memory_space=...]
    all_gather x0 -> x1, blocking collectives: none -> 9.78 us  [local(): mine = lax.all_gather(column, ('across', 'inner'), axis=0, tiled=True)]
  transfers between devices with their start and end apart: 4 -> 3, of which waited for: 3 -> 2; matrix products, arithmetic and copies ran while one was open for 31% -> 3% of each run, Pallas kernels for 0% -> 6%
where the time goes in v1:
time: 80.1 us; the launch traced here: 79.5 us
  blocking collectives  45.7 us (57%)
  Pallas kernels  11.2 us (14%)
  local copies, waits for them, and re-layouts  10.5 us (13%)
  starting transfers between devices  7.55 us (9%)
  waiting for transfers between devices  3 us (4%)
    all_to_all x1, blocking collectives, local(): arrived = lax.all_to_all(payload, plane, 0, 0, tiled=True)  27.2 us
    pallas_call x8, Pallas kernels, run(): pl.pallas_call(body, out_shape=outs, in_specs=[pl.BlockSpec(memory_space=...  11.2 us
    unnamed x28, local copies, waits for them, and re-layouts  10.3 us
    all_gather x1, blocking collectives, local(): mine = lax.all_gather(column, ('across', 'inner'), axis=0, tiled=True)  9.78 us
    all_to_all x1, blocking collectives, local(): lax.all_to_all(summed, 'outer', 0, 0, tiled=True)  8.79 us
    all_to_all x1, starting transfers between devices, local(): incoming = lax.all_to_all(outgoing, everyone, 0, 0, tiled=True)  7.3 us
    ppermute x1, waiting for transfers between devices, local(): received = lax.ppermute(send, 'core', swap)  1.91 us
  transfers between devices with their start and end apart: 3, of which 2 were waited for; matrix products, arithmetic and copies ran while one was open for 3% of the time, Pallas kernels for 6%

profile of v1, /device:TPU:0, one launch (start us, length us, event | category | flops | bytes accessed | tf_op | source)
XLA Modules:
  0.0 79.5 jit_solution(504746659491242838)
XLA Ops:
  0.7 1.1 %copy-done.1 = bf16[512,512]{1,0:T(8,128)(2,1)S(1)} copy-done((bf16[512,512]{1,0:T(8,128)(2,1)S(1)}, bf16[512,512]{1,0:T(8,128)(2,1)}, u32[]{:S(2)}) %copy-start.1) | copy-done | bytes 524312
  1.7 0.7 copy-done.3
  2.4 0.9 %serve.1 = bf16[32,4,512]{2,1,0:T(4,128)(2,1)} custom-call(s32[1,128]{1,0:T(1,128)S(1)} %copy-done.3, bf16[512,512]{1,0:T(8,128)(2,1)S(1)} %copy-done.1), custom_call_target="tpu_custom_call" | custom-call | flops 67108864 | bytes 1048576 | tf_op jit(solution)/shard_map/serve/pallas_call | solution.py:24
  3.3 7.3 %all-to-all-start = ((bf16[32,4,512]{2,1,0:T(4,128)(2,1)}), bf16[32,4,512]{2,1,0:T(4,128)(2,1)S(1)}, u32[]{:S(2)}, u32[]{:S(2)}) async-start(bf16[32,4,512]{2,1,0:T(4,128)(2,1)} %serve.1), calls=%async_computation | async-start | bytes 262144 | tf_op jit(solution)/shard_map/all_to_all | solution.py:212
  10.6 0.9 %copy.13.neighbours_ref = s32[512,16]{1,0:T(8,128)S(1)} copy(s32[512,16]{0,1:T(8,128)} %param.13) | data formatting | bytes 65536 | tf_op args[5]
  11.6 0.6 copy-done.7
  12.2 3.1 %own_aggregate.1 = (bf16[640,512]{1,0:T(8,128)(2,1)S(1)}, f32[512,128]{1,0:T(8,128)S(1)}, f32[512,512]{1,0:T(8,128)S(1)}, f32[512,512]{1,0:T(8,128)S(1)}) custom-call(s32[512,16]{1,0:T(8,128)S(1)} %copy.13.neighbours_ref, s32[1,512]{1,0:T(1,128)S(1)} %bitcast.6, bf16[512,512]{1,0:T(8,128)(2,1)S(1)} %copy-done.2, bf16[512,512]{1,0:T(8,128)(2,1)S(1)} %copy-done, ...), custom_call_target="tpu_custom_call" | custom-call | flops 5368709120 | bytes 4194304 | tf_op jit(solution)/shard_map/own_aggregate/pallas_call | solution.py:24
  15.3 1.0 %copy-done.9 = f32[512,512]{1,0:T(8,128)} copy-done((f32[512,512]{1,0:T(8,128)}, f32[512,512]{1,0:T(8,128)S(1)}, u32[]{:S(2)}) %copy-start.9) | copy-done | bytes 1048600
  16.3 1.0 %copy-done.11 = f32[512,512]{1,0:T(8,128)} copy-done((f32[512,512]{1,0:T(8,128)}, f32[512,512]{1,0:T(8,128)S(1)}, u32[]{:S(2)}) %copy-start.11) | copy-done | bytes 1048600
  17.3 1.1 %all-to-all-done.incoming_ref = bf16[32,4,512]{2,1,0:T(4,128)(2,1)S(1)} async-done(((bf16[32,4,512]{2,1,0:T(4,128)(2,1)}), bf16[32,4,512]{2,1,0:T(4,128)(2,1)S(1)}, u32[]{:S(2)}, u32[]{:S(2)}) %all-to-all-start) | async-done | bytes 131104 | tf_op jit(solution)/shard_map/all_to_all | solution.py:212
  18.4 1.0 %copy-done.5 = bf16[512,512]{1,0:T(8,128)(2,1)S(1)} copy-done((bf16[512,512]{1,0:T(8,128)(2,1)S(1)}, bf16[512,512]{1,0:T(8,128)(2,1)}, u32[]{:S(2)}) %copy-start.5) | copy-done | bytes 524312
  19.4 1.0 %copy-done.6 = bf16[512,512]{1,0:T(8,128)(2,1)S(1)} copy-done((bf16[512,512]{1,0:T(8,128)(2,1)S(1)}, bf16[512,512]{1,0:T(8,128)(2,1)}, u32[]{:S(2)}) %copy-start.6) | copy-done | bytes 524312
  20.5 1.2 %copy-done.10 = f32[512,512]{1,0:T(8,128)S(1)} copy-done((f32[512,512]{1,0:T(8,128)S(1)}, f32[512,512]{1,0:T(8,128)}, u32[]{:S(2)}) %copy-start.10) | copy-done | bytes 1048600
  21.7 1.2 %copy-done.12 = f32[512,512]{1,0:T(8,128)S(1)} copy-done((f32[512,512]{1,0:T(8,128)S(1)}, f32[512,512]{1,0:T(8,128)}, u32[]{:S(2)}) %copy-start.12) | copy-done | bytes 1048600
  22.9 2.0 %layer_grad.1 = (bf16[592,512]{1,0:T(8,128)(2,1)S(1)}, f32[512,512]{1,0:T(8,128)S(1)}, bf16[2,32,512]{2,1,0:T(8,128)(2,1)S(1)}, bf16[16,512]{1,0:T(8,128)(2,1)S(...) custom-call(s32[1]{0:T(128)} %bitcast.core_ref, bf16[32,4,512]{2,1,0:T(4,128)(2,1)S(1)} %all-to-all-done.incoming_ref, ...), custom_call_target="tpu_custom_call" | custom-call | flops 1342177280 | bytes 8388608 | tf_op jit(solution)/shard_map/layer_grad/pallas_call | solution.py:24
  25.1 1.9 %collective-permute-done.received_ref = bf16[592,512]{1,0:T(8,128)(2,1)S(1)} collective-permute-done((bf16[592,512]{1,0:T(8,128)(2,1)S(1)}, bf16[592,512]{1,0:T(8,128)(2,1)S(1)}, u32[]{:S(2)}, u32[]{:S(2)}) %collective-permute-start) | collective-permute-done | bytes 606240 | tf_op jit(solution)/shard_map/ppermute | solution.py:242
  27.1 27.2 %all_to_all.15.payload_ref = bf16[16,48,512]{2,1,0:T(8,128)(2,1)S(1)} all-to-all(bf16[16,48,512]{2,1,0:T(8,128)(2,1)S(1)} %pack.1), channel_id=1, replica_groups=mesh['across'=2,'core'=2,'outer'=4,'inner'=2] {'across','outer','inner'}, dimensions={0} | all-to-all | bytes 1572864 | tf_op jit(solution)/shard_map/all_to_all | solution.py:254
  54.3 0.6 sum_shares.1
  54.9 8.8 %all_to_all.16 = bf16[4,32,512]{2,1,0:T(8,128)(2,1)S(1)} all-to-all(bf16[4,32,512]{2,1,0:T(8,128)(2,1)S(1)} %get-tuple-element.28), channel_id=1, replica_groups=mesh['across'=2,'core'=2,'outer'=4,'inner'=2] {'outer'}, dimensions={0} | all-to-all | bytes 262144 | tf_op jit(solution)/shard_map/all_to_all | solution.py:265
  63.7 9.8 %all_gather.3.mine_ref = bf16[512,512]{1,0:T(8,128)(2,1)S(1)} all-gather(bf16[128,512]{1,0:T(8,128)(2,1)S(1)} %bitcast.8), channel_id=1, replica_groups=mesh['across'=2,'core'=2,'outer'=4,'inner'=2] {'across','inner'}, dimensions={0}, use_global_device_ids=true | all-gather | bytes 655360 | tf_op jit(solution)/shard_map/all_gather | solution.py:266
  74.2 0.7 reduce.3
  75.0 0.7 own_grad.1.base_ref
  75.7 1.3 %owner_sum.1 = f32[512,512]{1,0:T(8,128)} custom-call(s32[1]{0:T(128)} %bitcast.core_ref, s32[1,128]{1,0:T(1,128)S(1)} %reshape.31.serve_ref, bf16[16,48,512]{2,1,0:T(8,128)(2,1)S(1)} %all_to_all.15.payload_ref, f32[512,512]{1,0:T(8,128)S(1)} %own_grad.1.base_ref), custom_call_target="tpu_custom_call" | custom-call | flops 67108864 | bytes 3145728 | tf_op jit(solution)/shard_map/owner_sum/pallas_call | solution.py:24
  77.0 2.5 %finish.1 = (f32[512,512]{1,0:T(8,128)}, f32[512,512]{1,0:T(8,128)}) custom-call(s32[1]{0:T(128)} %bitcast.core_ref, bf16[512,512]{1,0:T(8,128)(2,1)S(1)} %all_gather.3.mine_ref, bf16[512,512]{1,0:T(8,128)(2,1)} %collective-permute-done.1.other_ref), custom_call_target="tpu_custom_call" | custom-call | flops 33554432 | bytes 3145728 | tf_op jit(solution)/shard_map/finish/pallas_call | solution.py:24
  (25 shorter events, 1.2 us)
Async XLA Ops:
  0.6 10.9 %copy-start = (bf16[512,512]{1,0:T(8,128)(2,1)S(1)}, bf16[512,512]{1,0:T(8,128)(2,1)}, u32[]{:S(2)}) copy-start(bf16[512,512]{1,0:T(8,128)(2,1)} %w_self_ref.3) | copy-start | bytes 1572868
  0.6 1.1 %copy-start.1 = (bf16[512,512]{1,0:T(8,128)(2,1)S(1)}, bf16[512,512]{1,0:T(8,128)(2,1)}, u32[]{:S(2)}) copy-start(bf16[512,512]{1,0:T(8,128)(2,1)} %features_ref.5) | copy-start | bytes 1572868
  1.7 0.7 copy-start.3
  2.4 9.2 %copy-start.2 = (bf16[512,512]{1,0:T(8,128)(2,1)S(1)}, bf16[512,512]{1,0:T(8,128)(2,1)}, u32[]{:S(2)}) copy-start(bf16[512,512]{1,0:T(8,128)(2,1)} %features_ref.5) | copy-start | bytes 1572868
  3.3 15.0 %all-to-all-start = ((bf16[32,4,512]{2,1,0:T(4,128)(2,1)}), bf16[32,4,512]{2,1,0:T(4,128)(2,1)S(1)}, u32[]{:S(2)}, u32[]{:S(2)}) async-start(bf16[32,4,512]{2,1,0:T(4,128)(2,1)} %serve.1), calls=%async_computation | async-start | bytes 262144 | tf_op jit(solution)/shard_map/all_to_all | solution.py:212
  10.6 0.9 %copy-start.8 = (f32[512]{0:T(512)S(1)}, f32[512]{0:T(512)}, u32[]{:S(2)}) copy-start(f32[512]{0:T(512)} %param.12) | copy-start | bytes 6148
  11.5 0.7 copy-start.7
  15.3 1.0 %copy-start.9 = (f32[512,512]{1,0:T(8,128)}, f32[512,512]{1,0:T(8,128)S(1)}, u32[]{:S(2)}) copy-start(f32[512,512]{1,0:T(8,128)S(1)} %get-tuple-element.20.own_sum_ref) | copy-start | bytes 3145732
  16.3 1.0 %copy-start.11 = (f32[512,512]{1,0:T(8,128)}, f32[512,512]{1,0:T(8,128)S(1)}, u32[]{:S(2)}) copy-start(f32[512,512]{1,0:T(8,128)S(1)} %get-tuple-element.21.pre_ref) | copy-start | bytes 3145732
  18.4 1.0 %copy-start.5 = (bf16[512,512]{1,0:T(8,128)(2,1)S(1)}, bf16[512,512]{1,0:T(8,128)(2,1)}, u32[]{:S(2)}) copy-start(bf16[512,512]{1,0:T(8,128)(2,1)} %cotangent_ref.1) | copy-start | bytes 1572868
  19.4 1.0 %copy-start.6 = (bf16[512,512]{1,0:T(8,128)(2,1)S(1)}, bf16[512,512]{1,0:T(8,128)(2,1)}, u32[]{:S(2)}) copy-start(bf16[512,512]{1,0:T(8,128)(2,1)} %w_neigh_ref.1) | copy-start | bytes 1572868
  20.5 1.2 %copy-start.10 = (f32[512,512]{1,0:T(8,128)S(1)}, f32[512,512]{1,0:T(8,128)}, u32[]{:S(2)}) copy-start(f32[512,512]{1,0:T(8,128)} %copy-done.9) | copy-start | bytes 3145732
  21.7 1.2 %copy-start.12 = (f32[512,512]{1,0:T(8,128)S(1)}, f32[512,512]{1,0:T(8,128)}, u32[]{:S(2)}) copy-start(f32[512,512]{1,0:T(8,128)} %copy-done.11) | copy-start | bytes 3145732
  24.9 2.1 %collective-permute-start = (bf16[592,512]{1,0:T(8,128)(2,1)S(1)}, bf16[592,512]{1,0:T(8,128)(2,1)S(1)}, u32[]{:S(2)}, u32[]{:S(2)}) collective-permute-start(bf16[592,512]{1,0:T(8,128)(2,1)S(1)} %get-tuple-element.22), channel_id=1, source_target_pairs={{0,8},{8,0},{1,9},{9,1},{2,10},{10,2},{3,11},{11,3},{4,12},{12,4},... | collective-permute-start | bytes 1818632 | tf_op jit(solution)/shard_map/ppermute | solution.py:242
  73.5 0.7 copy-start.4
  73.5 3.5 %collective-permute-start.1 = (bf16[512,512]{1,0:T(8,128)(2,1)S(1)}, bf16[512,512]{1,0:T(8,128)(2,1)}, u32[]{:S(2)}, u32[]{:S(2)}) collective-permute-start(bf16[512,512]{1,0:T(8,128)(2,1)S(1)} %all_gather.3.mine_ref), channel_id=1, source_target_pairs={{0,8},{8,0},{1,9},{9,1},{2,10},{10,2},{3,11},{11,3},{4,12},{12,4},... | collective-permute-start | bytes 1572872 | tf_op jit(solution)/shard_map/ppermute | solution.py:276

commit v2 on v1

v2 whole, which is shorter than its diff:
```python
import functools
import math

import jax
import jax.numpy as jnp
from jax import lax
from jax.experimental import pallas as pl
from jax.experimental.pallas import tpu as pltpu
from jax.sharding import Mesh
from jax.sharding import PartitionSpec as P

BF16 = jnp.bfloat16
F32 = jnp.float32
SMEM, VMEM, HBM = pltpu.SMEM, pltpu.VMEM, pltpu.HBM
shape = jax.ShapeDtypeStruct


def product(left, right, left_dim, right_dim):
    return lax.dot_general(
        left, right, (((left_dim,), (right_dim,)), ((), ())), preferred_element_type=F32
    )


def call(name, body, ins, outs, scratch=(), copies=0, flops=0, moved=0, aliases=None):
    scratch = list(scratch)
    if copies:
        scratch.append(pltpu.SemaphoreType.DMA((copies,)))
    return pl.pallas_call(
        body,
        out_shape=tuple(out for out, _ in outs),
        in_specs=[pl.BlockSpec(memory_space=memory) for memory in ins],
        out_specs=tuple(pl.BlockSpec(memory_space=memory) for _, memory in outs),
        scratch_shapes=scratch,
        input_output_aliases=aliases or {},
        compiler_params=pltpu.CompilerParams(vmem_limit_bytes=48 * 1024 * 1024),
        cost_estimate=pl.CostEstimate(flops=flops, bytes_accessed=moved, transcendentals=0),
        name=name,
    )


def start_all(sems, *pairs):
    copies = [pltpu.make_async_copy(a, b, sems.at[at]) for at, (a, b) in enumerate(pairs)]
    for copy in copies:
        copy.start()
    return copies


def serve_kernel(serve_hbm, features_hbm, out_ref, serve_ref, features_ref, sems):
    copies = start_all(sems, (serve_hbm, serve_ref), (features_hbm, features_ref))
    own_rows = features_ref.shape[0]
    slots = serve_ref.shape[1]
    copies[0].wait()
    row = lax.broadcasted_iota(jnp.int32, (own_rows, slots), 0)
    picks = (row == serve_ref[...]).astype(F32).astype(BF16)
    copies[1].wait()
    rows = product(picks, features_ref[...], 0, 0)
    out_ref[...] = rows.reshape(out_ref.shape).astype(BF16)


def own_kernel(
    dims, place_ref, neighbours_hbm, count_hbm, serve_hbm, features_hbm, w_self_hbm, bias_hbm,
    counts_hbm, inverse_hbm, own_sum_hbm, pre_hbm, order_hbm,
    neighbours_ref, count_ref, serve_ref, features_ref, w_self_ref, bias_ref,
    counts_ref, inverse_ref, own_sum_ref, pre_ref, order_ref, live_ref, sems,
):
    ins = start_all(
        sems,
        (neighbours_hbm, neighbours_ref),
        (count_hbm, count_ref),
        (features_hbm, features_ref),
        (w_self_hbm, w_self_ref),
        (bias_hbm, bias_ref),
        (serve_hbm, serve_ref),
    )

    def send(at, source, target):
        copy = pltpu.make_async_copy(source, target, sems.at[len(ins) + at])
        copy.start()
        return copy

    fanout, own_rows = neighbours_ref.shape
    table_rows = counts_ref.shape[0]
    for copy in ins[:2]:
        copy.wait()
    count = count_ref[...]
    position = lax.broadcasted_iota(jnp.int32, (fanout, own_rows), 0)
    live_ref[...] = jnp.where(position < count, neighbours_ref[...], -1)
    inverse_ref[...] = jnp.broadcast_to(1.0 / count.astype(F32), (128, own_rows)).T
    outs = [send(0, inverse_ref, inverse_hbm)]
    step = 32

    def fill(at, carry):
        start = pl.multiple_of(at * step, step)
        row = lax.broadcasted_iota(jnp.int32, (step, own_rows), 0) + start
        total = jnp.zeros((step, own_rows), F32)
        for k in range(fanout):
            total = total + jnp.where(row == live_ref[k : k + 1, :], 1.0, 0.0)
        counts_ref[pl.ds(start, step), :] = total.astype(BF16)
        return carry

    lax.fori_loop(0, table_rows // step, fill, 0)
    outs.append(send(1, counts_ref, counts_hbm))
    ins[2].wait()
    features = features_ref[...]
    own_sum_ref[...] = product(counts_ref[:own_rows, :], features, 0, 0)
    outs.append(send(2, own_sum_ref, own_sum_hbm))
    ins[3].wait()
    ins[4].wait()
    pre_ref[...] = product(features, w_self_ref[...], 1, 0) + bias_ref[...]
    outs.append(send(3, pre_ref, pre_hbm))
    ins[5].wait()
    across, near, cap = dims
    slots = serve_ref.shape[1]
    to = lax.broadcasted_iota(jnp.int32, (slots, slots), 1)
    slot = to % cap
    core = (to // cap % 2 + place_ref[0]) % 2
    n = to // (2 * cap) % near
    a = to // (2 * cap * near) % across
    wide = (to // (2 * cap * near * across) + place_ref[1]) % 2
    source = (((a * 2 + core) * 2 + wide) * near + n) * cap + slot
    at = lax.broadcasted_iota(jnp.int32, (slots, slots), 0)
    moves = (at == source).astype(F32).astype(BF16)
    serve = serve_ref[...]
    high = (serve // 32).astype(F32).astype(BF16)
    low = (serve % 32).astype(F32).astype(BF16)
    order_ref[...] = (
        product(high, moves, 1, 0) * 32.0 + product(low, moves, 1, 0)
    ).astype(jnp.int32)
    outs.append(send(4, order_ref, order_hbm))
    for copy in outs:
        copy.wait()


def spread_wide(inverse, width):
    return jnp.concatenate([inverse] * (width // 128), axis=1)


def main_kernel(
    place_ref, incoming_ref, counts_hbm, inverse_hbm, own_sum_hbm, pre_hbm, features_hbm, cotangent_hbm, w_neigh_hbm,
    send_ref, keep_ref, keep_rows_ref, bias_ref, pre_grad_ref, message_ref,
    counts_ref, inverse_ref, own_sum_ref, pre_ref, features_ref, cotangent_ref, w_neigh_ref, rows_ref, sems,
):
    own_rows, width = features_ref.shape
    slots = rows_ref.shape[0]
    copies = start_all(
        sems,
        (counts_hbm.at[pl.ds(own_rows, slots), :], counts_ref),
        (own_sum_hbm, own_sum_ref),
        (inverse_hbm, inverse_ref),
        (w_neigh_hbm, w_neigh_ref),
        (pre_hbm, pre_ref),
        (cotangent_hbm, cotangent_ref),
        (features_hbm, features_ref),
    )
    first = place_ref[0] == 0
    incoming = incoming_ref[...].astype(F32).reshape(slots, width).astype(BF16)
    copies[0].wait()
    slot_counts = counts_ref[...]
    fetched = product(slot_counts, incoming, 0, 0)
    copies[1].wait()
    copies[2].wait()
    inverse = spread_wide(inverse_ref[...], width)
    aggregated = ((own_sum_ref[...] + fetched) * inverse).astype(BF16)
    copies[3].wait()
    mixed = product(aggregated, w_neigh_ref[...], 1, 0)
    copies[4].wait()
    pre = pre_ref[...] + mixed
    sigmoid_pre = jax.nn.sigmoid(pre)
    copies[5].wait()
    pre_grad = (
        cotangent_ref[...].astype(F32) * sigmoid_pre * (1.0 + pre * (1.0 - sigmoid_pre))
    ).astype(BF16)
    pre_grad_ref[...] = pre_grad
    copies[6].wait()
    features = features_ref[...]
    keep_ref[...] = product(jnp.where(first, features, aggregated), pre_grad, 0, 0)
    send_ref[:own_rows, :] = product(
        jnp.where(first, aggregated, features), pre_grad, 0, 0
    ).astype(BF16)
    message = (product(pre_grad, w_neigh_ref[...], 1, 1) * inverse).astype(BF16)
    message_ref[...] = message
    rows_ref[...] = product(slot_counts, message, 1, 0)
    half = slots // 2
    blocks, length = keep_rows_ref.shape[0], keep_rows_ref.shape[1]
    for at in range(blocks):
        mine = pl.multiple_of((at * 2 + place_ref[0]) * length, length)
        other = pl.multiple_of((at * 2 + 1 - place_ref[0]) * length, length)
        keep_rows_ref[at] = rows_ref[pl.ds(mine, length), :].astype(BF16)
        send_ref[own_rows + at * length : own_rows + (at + 1) * length, :] = rows_ref[
            pl.ds(other, length), :
        ].astype(BF16)
    bias = jnp.sum(pre_grad.astype(F32), axis=0, keepdims=True).astype(BF16)
    bias_ref[...] = jnp.broadcast_to(bias, bias_ref.shape)
    send_ref[own_rows + half :, :] = jnp.broadcast_to(bias, bias_ref.shape)


def own_grad_kernel(
    pre_grad_ref, message_ref, w_self_hbm, counts_hbm, out_hbm, w_self_ref, counts_ref, out_ref, sems
):
    own_rows = pre_grad_ref.shape[0]
    copies = start_all(
        sems, (w_self_hbm, w_self_ref), (counts_hbm.at[pl.ds(0, own_rows), :], counts_ref)
    )
    copies[0].wait()
    out_ref[...] = product(pre_grad_ref[...], w_self_ref[...], 1, 1)
    copies[1].wait()
    out_ref[...] += product(counts_ref[...], message_ref[...], 1, 0)
    copy = pltpu.make_async_copy(out_ref, out_hbm, sems.at[2])
    copy.start()
    copy.wait()


def pack_kernel(dims, received_ref, keep_ref, keep_rows_ref, bias_ref, after_hbm, out_ref):
    across, near, cap = dims
    own_rows, width = keep_ref.shape
    peers, length = out_ref.shape[0], out_ref.shape[1]
    half = 2 * peers * cap
    share = own_rows // peers
    keep_rows = keep_rows_ref[...].astype(F32).reshape(half, width)
    other_rows = received_ref[own_rows : own_rows + half, :].astype(F32)
    bias = bias_ref[...].astype(F32) + received_ref[own_rows + half :, :].astype(F32)
    summed = keep_ref[...] + received_ref[:own_rows, :].astype(F32)
    for peer in range(peers):
        parts = [summed[peer * share : (peer + 1) * share]]
        for wide in range(2):
            at = ((peer // near * 2 + wide) * near + peer % near) * cap
            parts += [keep_rows[at : at + cap], other_rows[at : at + cap]]
        parts.append(bias[: length - share - 4 * cap])
        out_ref[peer] = jnp.concatenate(parts, axis=0).astype(BF16)


def sum_kernel(cap, share, place_ref, payload_ref, keep_ref, send_ref):
    peers, length, width = payload_ref.shape
    pair = 2 * cap
    count = peers * pair
    payload = payload_ref[...].astype(F32)
    grads = jnp.sum(payload[:, :share, :], axis=0).astype(BF16)
    tail = payload[:, share + 2 * pair :, :]
    bias = jnp.broadcast_to(
        jnp.sum(tail[:, 0:1, :], axis=0), (keep_ref.shape[0] - share - count, width)
    ).astype(BF16)
    first = place_ref[1] == 0
    lower = payload[:, share : share + pair, :].reshape(count, width)
    upper = payload[:, share + pair : share + 2 * pair, :].reshape(count, width)
    for ref, rows in (
        (keep_ref, jnp.where(first, lower, upper)),
        (send_ref, jnp.where(first, upper, lower)),
    ):
        ref[:share, :] = grads
        ref[share : share + count, :] = rows.astype(BF16)
        ref[share + count :, :] = bias


def total_kernel(factor, keep_ref, received_ref, out_ref, bias_ref):
    peers, share, width = out_ref.shape
    total = (keep_ref[:share, :].astype(F32) + received_ref[:share, :].astype(F32)).astype(BF16)
    for peer in range(peers):
        out_ref[peer] = total
    last = keep_ref.shape[0] - 16
    bias = keep_ref[last:, :].astype(F32) + received_ref[last:, :].astype(F32)
    bias_ref[...] = bias[:1] * factor


def owner_kernel(share, order_hbm, keep_ref, received_ref, base_hbm, out_hbm, order_ref, base_ref, sems):
    copies = start_all(sems, (order_hbm, order_ref), (base_hbm, base_ref))
    own_rows = base_ref.shape[0]
    slots = order_ref.shape[1]
    half = slots // 2
    rows = jnp.concatenate(
        [keep_ref[share : share + half, :], received_ref[share : share + half, :]], axis=0
    )
    copies[0].wait()
    row = lax.broadcasted_iota(jnp.int32, (own_rows, slots), 0)
    picks = (row == order_ref[...]).astype(F32).astype(BF16)
    added = product(picks, rows, 1, 0)
    copies[1].wait()
    base_ref[...] += added
    copy = pltpu.make_async_copy(base_ref, out_hbm, sems.at[2])
    copy.start()
    copy.wait()


def finish_kernel(factor, which, place_ref, half_ref, *refs):
    self_hbm, neigh_hbm, wide_ref, sems = refs[-4:]
    wide_ref[...] = half_ref[...].astype(F32) * factor
    matrix = (place_ref[0] + which) % 2

    @pl.when(matrix == 0)
    def _():
        pltpu.sync_copy(wide_ref, self_hbm)

    @pl.when(matrix == 1)
    def _():
        pltpu.sync_copy(wide_ref, neigh_hbm)


def local(features, cotangent, w_self, w_neigh, bias, neighbours, neigh_count, serve_rows):
    own_rows, width = features.shape
    fanout = neighbours.shape[1]
    across, near = lax.axis_size("across"), lax.axis_size("near")
    peers = across * near
    devices = 4 * peers
    slots = serve_rows.shape[1]
    cap = slots // devices
    half = slots // 2
    table_rows = own_rows + slots
    share = own_rows // peers
    length = -(-(share + 4 * cap + 1) // 8) * 8
    everyone = ("across", "core", "wide", "near")
    cube = ("across", "near")
    dims = (across, near, cap)
    place = jnp.stack([lax.axis_index("core"), lax.axis_index("wide")]).astype(jnp.int32)
    swap = [(0, 1), (1, 0)]
    factor = 1.0 / math.sqrt(own_rows * devices)
    work = 2 * own_rows * own_rows * width
    square16 = shape((own_rows, width), BF16)
    square32 = shape((own_rows, width), F32)

    (outgoing,) = call(
        "serve", serve_kernel, (HBM, HBM), ((shape((devices, cap, width), BF16), VMEM),),
        scratch=[VMEM((1, slots), jnp.int32), VMEM((own_rows, width), BF16)],
        copies=2, flops=work // 4, moved=1 << 20,
    )(serve_rows, features)
    incoming = lax.all_to_all(outgoing, everyone, 0, 0, tiled=True)
    results = (
        shape((table_rows, own_rows), BF16),
        shape((own_rows, 128), F32),
        square32,
        square32,
        shape((1, slots), jnp.int32),
    )
    counts, inverse, own_sum, pre, order = call(
        "own_aggregate", functools.partial(own_kernel, dims),
        (SMEM,) + (HBM,) * 6, tuple((result, HBM) for result in results),
        scratch=[
            VMEM((fanout, own_rows), jnp.int32),
            VMEM((1, own_rows), jnp.int32),
            VMEM((1, slots), jnp.int32),
            VMEM((own_rows, width), BF16),
            VMEM((width, width), BF16),
            VMEM((1, width), F32),
            *(VMEM(result.shape, result.dtype) for result in results),
            VMEM((fanout, own_rows), jnp.int32),
        ],
        copies=11, flops=20 * work, moved=4 << 20,
    )(
        place, neighbours.T, neigh_count.reshape(1, own_rows), serve_rows, features, w_self,
        bias.reshape(1, width),
    )
    send, keep, keep_rows, own_bias, pre_grad, message = call(
        "layer_grad", main_kernel, (SMEM, VMEM) + (HBM,) * 7,
        (
            (shape((own_rows + half + 16, width), BF16), VMEM),
            (square32, VMEM),
            (shape((across, 2 * near * cap, width), BF16), VMEM),
            (shape((16, width), BF16), VMEM),
            (square16, VMEM),
            (square16, VMEM),
        ),
        scratch=[
            VMEM((slots, own_rows), BF16),
            VMEM((own_rows, 128), F32),
            VMEM((own_rows, width), F32),
            VMEM((own_rows, width), F32),
            VMEM((own_rows, width), BF16),
            VMEM((own_rows, width), BF16),
            VMEM((width, width), BF16),
            VMEM((slots, width), F32),
        ],
        copies=7, flops=5 * work, moved=8 << 20,
    )(place, incoming, counts, inverse, own_sum, pre, features, cotangent, w_neigh)
    received = lax.ppermute(send, "core", swap)
    (base,) = call(
        "own_grad", own_grad_kernel, (VMEM, VMEM, HBM, HBM), ((square32, HBM),),
        scratch=[
            VMEM((width, width), BF16), VMEM((own_rows, own_rows), BF16), VMEM((own_rows, width), F32)
        ],
        copies=3, flops=2 * work, moved=4 << 20,
    )(pre_grad, message, w_self, counts)
    (payload,) = call(
        "pack", functools.partial(pack_kernel, dims), (VMEM,) * 4 + (HBM,),
        ((shape((peers, length, width), BF16), VMEM),), flops=work // 4, moved=4 << 20,
    )(received, keep, keep_rows, own_bias, base)
    arrived = lax.all_to_all(payload, cube, 0, 0, tiled=True)
    pairs = shape((share + half + 16, width), BF16)
    keep_sum, send_sum = call(
        "sum_shares", functools.partial(sum_kernel, cap, share), (SMEM, VMEM), ((pairs, VMEM), (pairs, VMEM)),
        flops=work // 8, moved=1 << 20,
    )(place, arrived)
    received_sum = lax.ppermute(send_sum, "wide", swap)
    copies_out, bias_sum = call(
        "total", functools.partial(total_kernel, factor), (VMEM, VMEM),
        ((shape((peers, share, width), BF16), VMEM), (shape((1, width), F32), VMEM)),
        flops=work // 8, moved=1 << 20,
    )(keep_sum, received_sum)
    mine = lax.all_to_all(copies_out, cube, 0, 0, tiled=True).reshape(own_rows, width)
    (grad_features,) = call(
        "owner_sum", functools.partial(owner_kernel, share), (HBM, VMEM, VMEM, HBM), ((square32, HBM),),
        scratch=[VMEM((1, slots), jnp.int32), VMEM((own_rows, width), F32)],
        copies=3, flops=work, moved=3 << 20,
    )(order, keep_sum, received_sum, base)
    other = lax.ppermute(mine, "core", swap)
    halves = ((square32, HBM), (square32, HBM))
    scratch = [VMEM((own_rows, width), F32)]
    parts = call(
        "finish_mine", functools.partial(finish_kernel, factor, 0), (SMEM, VMEM, HBM), halves,
        scratch=scratch, copies=1, flops=work // 2, moved=3 << 20,
    )(place, mine, grad_features)
    grad_self, grad_neigh = call(
        "finish_other", functools.partial(finish_kernel, factor, 1), (SMEM, VMEM, HBM, HBM), halves,
        scratch=scratch, copies=1, flops=work // 2, moved=3 << 20, aliases={2: 0, 3: 1},
    )(place, other, *parts)
    return grad_features, grad_self, grad_neigh, bias_sum.reshape(width)


def solution(mesh):
    groups, members = mesh.shape["group"], mesh.shape["member"]
    nodes = ("across", "core", "wide", "near")
    fine = Mesh(mesh.devices.reshape(groups // 2, 2, 2, members // 2), nodes)
    rows = P(nodes, None)
    return jax.shard_map(
        local,
        mesh=fine,
        in_specs=(rows, rows, P(), P(), P(), rows, P(nodes), rows),
        out_specs=(rows, P(), P(), P()),
        check_vma=False,
    )
```

time: 80.1 us -> 71.1 us (0.89)
  blocking collectives: 45.7 us -> 29.1 us
  Pallas kernels: 11.2 us -> 16.9 us
  waiting for transfers between devices: 3 us -> 6.92 us
  local copies, waits for them, and re-layouts: 10.5 us -> 6.64 us
  starting transfers between devices: 7.55 us -> 10.1 us
    all_gather x1 -> x0, blocking collectives: 9.78 us -> none  [local(): mine = lax.all_gather(column, ('across', 'inner'), axis=0, tiled=True)]
    all_to_all x2, blocking collectives: 36 us -> 29.1 us  [the longest x1 16.8 us: local(): arrived = lax.all_to_all(payload, cube, 0, 0, tiled=True)]
    ppermute x0 -> x1, waiting for transfers between devices: none -> 6.12 us  [local(): received_sum = lax.ppermute(send_sum, 'wide', swap)]
    pallas_call x8 -> x10, Pallas kernels: 11.2 us -> 16.9 us  [the longest x1 4.53 us: local(): call('own_aggregate', functools.partial(own_kernel, dims), (SMEM,) + (HBM...]
    unnamed x28, local copies, waits for them, and re-layouts: 10.3 us -> 6.64 us
    ppermute x0 -> x1, starting transfers between devices: none -> 2.53 us  [local(): received_sum = lax.ppermute(send_sum, 'wide', swap)]
    ppermute x1, waiting for transfers between devices: 1.91 us -> 0.8 us  [local(): received = lax.ppermute(send, 'core', swap)]
    all_to_all x1, waiting for transfers between devices: 1.09 us -> 0.01 us  [local(): incoming = lax.all_to_all(outgoing, everyone, 0, 0, tiled=True)]
  transfers between devices with their start and end apart: 3 -> 4, of which waited for: 2 -> 2; matrix products, arithmetic and copies ran while one was open for 3% -> 0% of each run, Pallas kernels for 6% -> 12%
where the time goes in v2:
time: 71.1 us; the launch traced here: 70.6 us
  blocking collectives  29.1 us (41%)
  Pallas kernels  16.9 us (24%)
  starting transfers between devices  10.1 us (14%)
  waiting for transfers between devices  6.92 us (10%)
  local copies, waits for them, and re-layouts  6.64 us (9%)
  between operations  0.79 us (1%)
    all_to_all x1, blocking collectives, local(): arrived = lax.all_to_all(payload, cube, 0, 0, tiled=True)  16.8 us
    all_to_all x1, blocking collectives, local(): lax.all_to_all(copies_out, cube, 0, 0, tiled=True).reshape(own_rows, width)  12.3 us
    all_to_all x1, starting transfers between devices, local(): incoming = lax.all_to_all(outgoing, everyone, 0, 0, tiled=True)  7.3 us
    unnamed x28, local copies, waits for them, and re-layouts  6.64 us
    ppermute x1, waiting for transfers between devices, local(): received_sum = lax.ppermute(send_sum, 'wide', swap)  6.12 us
    pallas_call x1, Pallas kernels, local(): call('own_aggregate', functools.partial(own_kernel, dims), (SMEM,) + (HBM...  4.53 us
    pallas_call x1, Pallas kernels, local(): call('layer_grad', main_kernel, (SMEM, VMEM) + (HBM,) * 7, ((shape((own_r...  4.38 us
    ppermute x1, starting transfers between devices, local(): received_sum = lax.ppermute(send_sum, 'wide', swap)  2.53 us
  transfers between devices with their start and end apart: 4, of which 2 were waited for; matrix products, arithmetic and copies ran while one was open for 0% of the time, Pallas kernels for 12%

profile of v2, /device:TPU:0, one launch (start us, length us, event | category | flops | bytes accessed | tf_op | source)
XLA Modules:
  0.0 70.6 jit_solution(7707049950103599568)
XLA Ops:
  0.7 1.1 %copy-done.2 = bf16[512,512]{1,0:T(8,128)(2,1)S(1)} copy-done((bf16[512,512]{1,0:T(8,128)(2,1)S(1)}, bf16[512,512]{1,0:T(8,128)(2,1)}, u32[]{:S(2)}) %copy-start.2) | copy-done | bytes 524312
  1.7 0.7 copy-done.5
  2.4 1.0 %serve.1 = bf16[32,4,512]{2,1,0:T(4,128)(2,1)} custom-call(s32[1,128]{1,0:T(1,128)S(1)} %copy-done.5, bf16[512,512]{1,0:T(8,128)(2,1)S(1)} %copy-done.2), custom_call_target="tpu_custom_call" | custom-call | flops 67108864 | bytes 1048576 | tf_op jit(solution)/shard_map/serve/pallas_call | solution.py:319
  3.4 7.3 %all-to-all-start = ((bf16[32,4,512]{2,1,0:T(4,128)(2,1)}), bf16[32,4,512]{2,1,0:T(4,128)(2,1)S(1)}, u32[]{:S(2)}, u32[]{:S(2)}) async-start(bf16[32,4,512]{2,1,0:T(4,128)(2,1)} %serve.1), calls=%async_computation | async-start | bytes 262144 | tf_op jit(solution)/shard_map/all_to_all | solution.py:324
  10.9 0.6 copy-done.11
  11.5 1.0 %copy-done.3 = bf16[512,512]{1,0:T(8,128)(2,1)S(1)} copy-done((bf16[512,512]{1,0:T(8,128)(2,1)S(1)}, bf16[512,512]{1,0:T(8,128)(2,1)}, u32[]{:S(2)}) %copy-start.3) | copy-done | bytes 524312
  12.6 4.5 %own_aggregate.1 = (bf16[640,512]{1,0:T(8,128)(2,1)S(1)}, f32[512,128]{1,0:T(8,128)S(1)}, f32[512,512]{1,0:T(8,128)S(1)}, f32[512,512]{1,0:T(8,128)S(1)}, s32[1,128]{1,0:T(1,128)S(1)}) custom-call(s32[2]{0:T(128)S(1)} %pad_add_fusion.place_ref, s32[16,512]{1,0:T(8,128)S(1)} %bitcast.9, s32[1,512]{1,0:T(1,128)S(1)} %bitcast.10, s32[1,128]{1,0:T(1,128)S(1)} %copy-done.6, ...), custom_call_target="tpu_custom_call" | custom-call | flops 5368709120 | bytes 4194304 | tf_op jit(solution)/shard_map/own_aggregate/pallas_call | solution.py:332
  17.1 1.0 %copy-done.12 = f32[512,512]{1,0:T(8,128)} copy-done((f32[512,512]{1,0:T(8,128)}, f32[512,512]{1,0:T(8,128)S(1)}, u32[]{:S(2)}) %copy-start.12) | copy-done | bytes 1048600
  18.1 1.0 %copy-done.13 = f32[512,512]{1,0:T(8,128)} copy-done((f32[512,512]{1,0:T(8,128)}, f32[512,512]{1,0:T(8,128)S(1)}, u32[]{:S(2)}) %copy-start.13) | copy-done | bytes 1048600
  19.1 4.4 %layer_grad.1 = (bf16[592,512]{1,0:T(8,128)(2,1)S(1)}, f32[512,512]{1,0:T(8,128)S(1)}, bf16[2,32,512]{2,1,0:T(8,128)(2,1)S(1)}, bf16[16,512]{1,0:T(8,128)(2,1)S(...) custom-call(s32[2]{0:T(128)S(1)} %pad_add_fusion.place_ref, ...), custom_call_target="tpu_custom_call" | custom-call | flops 1342177280 | bytes 8388608 | tf_op jit(solution)/shard_map/layer_grad/pallas_call | solution.py:350
  23.5 0.3 collective-permute-start
  23.8 1.0 %own_grad.1.after_hbm.base_hbm = f32[512,512]{1,0:T(8,128)S(1)} custom-call(bf16[512,512]{1,0:T(8,128)(2,1)S(1)} %get-tuple-element.32.pre_grad_ref, bf16[512,512]{1,0:T(8,128)(2,1)S(1)} %get-tuple-element.33.message_ref, bf16[512,512]{1,0:T(8,128)(2,1)S(1)} %copy-done.1, bf16[640,512]{1,0:T(8,128)(2,1)S(1)} %get-tuple-element.24.counts_hbm), custom_call_target="tpu_custom_call" | custom-call | flops 536870912 | bytes 4194304 | tf_op jit(solution)/shard_map/own_grad/pallas_call | solution.py:373
  24.8 0.8 %collective-permute-done.received_ref = bf16[592,512]{1,0:T(8,128)(2,1)S(1)} collective-permute-done((bf16[592,512]{1,0:T(8,128)(2,1)S(1)}, bf16[592,512]{1,0:T(8,128)(2,1)S(1)}, u32[]{:S(2)}, u32[]{:S(2)}) %collective-permute-start) | collective-permute-done | bytes 606240 | tf_op jit(solution)/shard_map/ppermute | solution.py:372
  25.6 0.1 pack.1
  25.7 16.8 %all_to_all.15.payload_ref = bf16[8,88,512]{2,1,0:T(8,128)(2,1)S(1)} all-to-all(bf16[8,88,512]{2,1,0:T(8,128)(2,1)S(1)} %pack.1), channel_id=1, replica_groups=mesh['across'=2,'core'=2,'wide'=2,'near'=4] {'across','near'}, dimensions={0} | all-to-all | bytes 1441792 | tf_op jit(solution)/shard_map/all_to_all | solution.py:384
  42.5 0.7 sum_shares.1
  43.2 2.5 %collective-permute-start.1 = (bf16[144,512]{1,0:T(8,128)(2,1)S(1)}, bf16[144,512]{1,0:T(8,128)(2,1)S(1)}, u32[]{:S(2)}, u32[]{:S(2)}) collective-permute-start(bf16[144,512]{1,0:T(8,128)(2,1)S(1)} %get-tuple-element.35), channel_id=1, source_target_pairs={{0,4},{4,0},{1,5},{5,1},{2,6},{6,2},{3,7},{7,3},{8,12},{12,8},{9,1... | collective-permute-start | bytes 442376 | tf_op jit(solution)/shard_map/ppermute | solution.py:390
  45.7 6.1 %collective-permute-done.1.received_ref = bf16[144,512]{1,0:T(8,128)(2,1)S(1)} collective-permute-done((bf16[144,512]{1,0:T(8,128)(2,1)S(1)}, bf16[144,512]{1,0:T(8,128)(2,1)S(1)}, u32[]{:S(2)}, u32[]{:S(2)}) %collective-permute-start.1) | collective-permute-done | bytes 147488 | tf_op jit(solution)/shard_map/ppermute | solution.py:390
  51.8 0.6 total.1
  52.4 12.3 %all_to_all.16 = bf16[8,64,512]{2,1,0:T(8,128)(2,1)S(1)} all-to-all(bf16[8,64,512]{2,1,0:T(8,128)(2,1)S(1)} %get-tuple-element.36), channel_id=1, replica_groups=mesh['across'=2,'core'=2,'wide'=2,'near'=4] {'across','near'}, dimensions={0} | all-to-all | bytes 1048576 | tf_op jit(solution)/shard_map/all_to_all | solution.py:396
  64.7 1.4 %owner_sum.1.refs_0_ = f32[512,512]{1,0:T(8,128)} custom-call(s32[1,128]{1,0:T(1,128)S(1)} %get-tuple-element.23.order_hbm, bf16[144,512]{1,0:T(8,128)(2,1)S(1)} %get-tuple-element.34.keep_ref, bf16[144,512]{1,0:T(8,128)(2,1)S(1)} %collective-permute-done.1.received_ref, f32[512,512]{1,0:T(8,128)S(1)} %own_grad.1.after_hbm.base_hbm), custom_call_target="tpu_custom_call" | custom-call | flops 268435456 | bytes 3145728 | tf_op jit(solution)/shard_map/owner_sum/pallas_call | solution.py:397
  66.2 1.2 %copy-done = f32[512,512]{1,0:T(8,128)S(1)} copy-done((f32[512,512]{1,0:T(8,128)S(1)}, f32[512,512]{1,0:T(8,128)}, u32[]{:S(2)}) %copy-start) | copy-done | bytes 1048600
  67.4 1.6 %finish_mine.1 = (f32[512,512]{1,0:T(8,128)}, f32[512,512]{1,0:T(8,128)}) custom-call(s32[2]{0:T(128)S(1)} %pad_add_fusion.place_ref, bf16[512,512]{1,0:T(8,128)(2,1)S(1)} %bitcast.8, f32[512,512]{1,0:T(8,128)S(1)} %copy-done), custom_call_target="tpu_custom_call" | custom-call | flops 134217728 | bytes 3145728 | tf_op jit(solution)/shard_map/finish_mine/pallas_call | solution.py:405
  69.0 1.6 %finish_other.1 = (f32[512,512]{1,0:T(8,128)}, f32[512,512]{1,0:T(8,128)}) custom-call(s32[2]{0:T(128)S(1)} %pad_add_fusion.place_ref, bf16[512,512]{1,0:T(8,128)(2,1)S(1)} %collective-permute-done.2.half_ref, f32[512,512]{1,0:T(8,128)} %get-tuple-element.37.refs_0_, f32[512,512]{1,0:T(8,128)} %get-tuple-element.38.refs_1_), custom_call_target="tpu_custom_call", output_to_operand_aliasing={{0}: (2, {}), {1}: (3, {})} | custom-call | flops 134217728 | bytes 3145728 | tf_op jit(solution)/shard_map/finish_other/pallas_call | solution.py:409
  (25 shorter events, 0.2 us)
Async XLA Ops:
  0.6 10.2 %copy-start.1 = (bf16[512,512]{1,0:T(8,128)(2,1)S(1)}, bf16[512,512]{1,0:T(8,128)(2,1)}, u32[]{:S(2)}) copy-start(bf16[512,512]{1,0:T(8,128)(2,1)} %w_self_hbm.3) | copy-start | bytes 1572868
  0.6 1.1 %copy-start.2 = (bf16[512,512]{1,0:T(8,128)(2,1)S(1)}, bf16[512,512]{1,0:T(8,128)(2,1)}, u32[]{:S(2)}) copy-start(bf16[512,512]{1,0:T(8,128)(2,1)} %features_hbm.5) | copy-start | bytes 1572868
  1.7 0.7 copy-start.5
  3.4 7.4 %copy-start.9 = (s32[512,16]{0,1:T(8,128)S(1)}, s32[512,16]{0,1:T(8,128)}, u32[]{:S(2)}) copy-start(s32[512,16]{0,1:T(8,128)} %param.13) | copy-start | bytes 98308
  3.4 15.6 %all-to-all-start = ((bf16[32,4,512]{2,1,0:T(4,128)(2,1)}), bf16[32,4,512]{2,1,0:T(4,128)(2,1)S(1)}, u32[]{:S(2)}, u32[]{:S(2)}) async-start(bf16[32,4,512]{2,1,0:T(4,128)(2,1)} %serve.1), calls=%async_computation | async-start | bytes 262144 | tf_op jit(solution)/shard_map/all_to_all | solution.py:324
  10.8 0.7 copy-start.11
  10.8 0.7 copy-start.10
  10.8 0.7 copy-start.6
  11.5 1.0 %copy-start.3 = (bf16[512,512]{1,0:T(8,128)(2,1)S(1)}, bf16[512,512]{1,0:T(8,128)(2,1)}, u32[]{:S(2)}) copy-start(bf16[512,512]{1,0:T(8,128)(2,1)} %features_hbm.5) | copy-start | bytes 1572868
  12.6 6.5 %copy-start.4 = (bf16[512,512]{1,0:T(8,128)(2,1)S(1)}, bf16[512,512]{1,0:T(8,128)(2,1)}, u32[]{:S(2)}) copy-start(bf16[512,512]{1,0:T(8,128)(2,1)} %features_hbm.5) | copy-start | bytes 1572868
  12.6 6.5 %copy-start.7 = (bf16[512,512]{1,0:T(8,128)(2,1)S(1)}, bf16[512,512]{1,0:T(8,128)(2,1)}, u32[]{:S(2)}) copy-start(bf16[512,512]{1,0:T(8,128)(2,1)} %cotangent_hbm.1) | copy-start | bytes 1572868
  12.6 6.5 %copy-start.8 = (bf16[512,512]{1,0:T(8,128)(2,1)S(1)}, bf16[512,512]{1,0:T(8,128)(2,1)}, u32[]{:S(2)}) copy-start(bf16[512,512]{1,0:T(8,128)(2,1)} %w_neigh_hbm.1) | copy-start | bytes 1572868
  17.1 1.0 %copy-start.12 = (f32[512,512]{1,0:T(8,128)}, f32[512,512]{1,0:T(8,128)S(1)}, u32[]{:S(2)}) copy-start(f32[512,512]{1,0:T(8,128)S(1)} %get-tuple-element.26.own_sum_hbm) | copy-start | bytes 3145732
  18.1 1.0 %copy-start.13 = (f32[512,512]{1,0:T(8,128)}, f32[512,512]{1,0:T(8,128)S(1)}, u32[]{:S(2)}) copy-start(f32[512,512]{1,0:T(8,128)S(1)} %get-tuple-element.27.pre_hbm) | copy-start | bytes 3145732
  23.5 2.1 %collective-permute-start = (bf16[592,512]{1,0:T(8,128)(2,1)S(1)}, bf16[592,512]{1,0:T(8,128)(2,1)S(1)}, u32[]{:S(2)}, u32[]{:S(2)}) collective-permute-start(bf16[592,512]{1,0:T(8,128)(2,1)S(1)} %get-tuple-element.28), channel_id=1, source_target_pairs={{0,8},{8,0},{1,9},{9,1},{2,10},{10,2},{3,11},{11,3},{4,12},{12,4},... | collective-permute-start | bytes 1818632 | tf_op jit(solution)/shard_map/ppermute | solution.py:372
  43.2 8.6 %collective-permute-start.1 = (bf16[144,512]{1,0:T(8,128)(2,1)S(1)}, bf16[144,512]{1,0:T(8,128)(2,1)S(1)}, u32[]{:S(2)}, u32[]{:S(2)}) collective-permute-start(bf16[144,512]{1,0:T(8,128)(2,1)S(1)} %get-tuple-element.35), channel_id=1, source_target_pairs={{0,4},{4,0},{1,5},{5,1},{2,6},{6,2},{3,7},{7,3},{8,12},{12,8},{9,1... | collective-permute-start | bytes 442376 | tf_op jit(solution)/shard_map/ppermute | solution.py:390
  64.7 4.3 %collective-permute-start.2 = (bf16[512,512]{1,0:T(8,128)(2,1)S(1)}, bf16[512,512]{1,0:T(8,128)(2,1)S(1)}, u32[]{:S(2)}, u32[]{:S(2)}) collective-permute-start(bf16[512,512]{1,0:T(8,128)(2,1)S(1)} %bitcast.7), channel_id=1, source_target_pairs={{0,8},{8,0},{1,9},{9,1},{2,10},{10,2},{3,11},{11,3},{4,12},{12,4},... | collective-permute-start | bytes 1572872 | tf_op jit(solution)/shard_map/ppermute | solution.py:402
  66.2 1.2 %copy-start = (f32[512,512]{1,0:T(8,128)S(1)}, f32[512,512]{1,0:T(8,128)}, u32[]{:S(2)}) copy-start(f32[512,512]{1,0:T(8,128)} %owner_sum.1.refs_0_) | copy-start | bytes 3145732

commit v3 on v2

v3 whole, which is shorter than its diff:
```python
import functools
import math

import jax
import jax.numpy as jnp
from jax import lax
from jax.experimental import pallas as pl
from jax.experimental.pallas import tpu as pltpu
from jax.sharding import Mesh
from jax.sharding import PartitionSpec as P

BF16 = jnp.bfloat16
F32 = jnp.float32
VMEM, HBM = pltpu.VMEM, pltpu.HBM
shape = jax.ShapeDtypeStruct


def product(left, right, left_dim, right_dim):
    return lax.dot_general(
        left, right, (((left_dim,), (right_dim,)), ((), ())), preferred_element_type=F32
    )


def call(name, body, ins, outs, scratch=(), copies=0, flops=0, moved=0, aliases=None):
    scratch = list(scratch)
    if copies:
        scratch.append(pltpu.SemaphoreType.DMA((copies,)))
    run = pl.pallas_call(
        body,
        out_shape=tuple(
            HBM(out.shape, out.dtype) if memory is HBM else out for out, memory in outs
        ),
        in_specs=[pl.BlockSpec(memory_space=memory) for memory in ins],
        out_specs=tuple(pl.BlockSpec(memory_space=memory) for _, memory in outs),
        scratch_shapes=scratch,
        input_output_aliases=aliases or {},
        compiler_params=pltpu.CompilerParams(vmem_limit_bytes=48 * 1024 * 1024),
        cost_estimate=pl.CostEstimate(flops=flops, bytes_accessed=moved, transcendentals=0),
        name=name,
    )

    def held(*operands):
        return run(*(
            pltpu.with_memory_space_constraint(operand, HBM) if memory is HBM else operand
            for operand, memory in zip(operands, ins, strict=True)
        ))

    return held


def start_all(sems, *pairs):
    copies = [pltpu.make_async_copy(a, b, sems.at[at]) for at, (a, b) in enumerate(pairs)]
    for copy in copies:
        copy.start()
    return copies


def serve_kernel(serve_hbm, features_hbm, out_ref, serve_ref, features_ref, sems):
    copies = start_all(sems, (serve_hbm, serve_ref), (features_hbm, features_ref))
    own_rows = features_ref.shape[0]
    slots = serve_ref.shape[1]
    copies[0].wait()
    row = lax.broadcasted_iota(jnp.int32, (own_rows, slots), 0)
    picks = (row == serve_ref[...]).astype(F32).astype(BF16)
    copies[1].wait()
    rows = product(picks, features_ref[...], 0, 0)
    out_ref[...] = rows.reshape(out_ref.shape).astype(BF16)


def own_kernel(
    dims, neighbours_ref, count_ref, serve_ref, features_ref, w_self_ref, bias_ref,
    counts_ref, slot_counts_ref, inverse_ref, order_ref, flipped_hbm, pre_hbm,
    flipped_ref, pre_ref, live_ref, table_ref, sems,
):
    fanout, own_rows = neighbours_ref.shape
    table_rows = table_ref.shape[0]
    features = features_ref[...]
    flipped_ref[...] = features.T
    pre_ref[...] = product(features, w_self_ref[...], 1, 0) + bias_ref[...]
    copies = start_all(sems, (flipped_ref, flipped_hbm), (pre_ref, pre_hbm))
    count = count_ref[...]
    position = lax.broadcasted_iota(jnp.int32, (fanout, own_rows), 0)
    live_ref[...] = jnp.where(position < count, neighbours_ref[...], -1)
    inverse_ref[...] = jnp.broadcast_to(1.0 / count.astype(F32), (128, own_rows)).T
    step = 32

    def fill(at, carry):
        start = pl.multiple_of(at * step, step)
        row = lax.broadcasted_iota(jnp.int32, (step, own_rows), 0) + start
        total = jnp.zeros((step, own_rows), F32)
        for k in range(fanout):
            total = total + jnp.where(row == live_ref[k : k + 1, :], 1.0, 0.0)
        table_ref[pl.ds(start, step), :] = total.astype(BF16)
        return carry

    lax.fori_loop(0, table_rows // step, fill, 0)
    counts_ref[...] = table_ref[...].T
    slot_counts_ref[...] = table_ref[own_rows:, :]
    across, near, cap = dims
    slots = serve_ref.shape[1]
    to = lax.broadcasted_iota(jnp.int32, (slots, slots), 1)
    slot = to % cap
    core = (to // cap % 2 + lax.axis_index("core")) % 2
    n = to // (2 * cap) % near
    a = to // (2 * cap * near) % across
    wide = (to // (2 * cap * near * across) + lax.axis_index("wide")) % 2
    source = (((a * 2 + core) * 2 + wide) * near + n) * cap + slot
    at = lax.broadcasted_iota(jnp.int32, (slots, slots), 0)
    moves = (at == source).astype(F32).astype(BF16)
    serve = serve_ref[...]
    high = (serve // 32).astype(F32).astype(BF16)
    low = (serve % 32).astype(F32).astype(BF16)
    order_ref[...] = (
        product(high, moves, 1, 0) * 32.0 + product(low, moves, 1, 0)
    ).astype(jnp.int32)
    for copy in copies:
        copy.wait()


def spread_wide(inverse, width):
    return jnp.concatenate([inverse] * (width // 128), axis=1)


def main_kernel(
    incoming_ref, counts_ref, slot_counts_ref, inverse_ref, features_ref, w_neigh_ref,
    pre_hbm, cotangent_hbm, flipped_hbm,
    send_ref, keep_ref, keep_rows_ref, bias_ref, pre_grad_ref, message_ref,
    pre_ref, cotangent_ref, flipped_ref, rows_ref, sems,
):
    own_rows, width = features_ref.shape
    slots = rows_ref.shape[0]
    copies = start_all(
        sems, (pre_hbm, pre_ref), (cotangent_hbm, cotangent_ref), (flipped_hbm, flipped_ref)
    )
    core = lax.axis_index("core")
    first = core == 0
    incoming = incoming_ref[...].astype(F32).reshape(slots, width).astype(BF16)
    summed = product(counts_ref[:, :own_rows], features_ref[...], 1, 0) + product(
        counts_ref[:, own_rows:], incoming, 1, 0
    )
    inverse = spread_wide(inverse_ref[...], width)
    aggregated = (summed * inverse).astype(BF16)
    mixed = product(aggregated, w_neigh_ref[...], 1, 0)
    copies[0].wait()
    pre = pre_ref[...] + mixed
    sigmoid_pre = jax.nn.sigmoid(pre)
    copies[1].wait()
    pre_grad = (
        cotangent_ref[...].astype(F32) * sigmoid_pre * (1.0 + pre * (1.0 - sigmoid_pre))
    ).astype(BF16)
    pre_grad_ref[...] = pre_grad
    copies[2].wait()
    grad_self = product(flipped_ref[...], pre_grad, 1, 0)
    grad_neigh = product(aggregated, pre_grad, 0, 0)
    keep_ref[...] = jnp.where(first, grad_self, grad_neigh)
    send_ref[:own_rows, :] = jnp.where(first, grad_neigh, grad_self).astype(BF16)
    message = (product(pre_grad, w_neigh_ref[...], 1, 1) * inverse).astype(BF16)
    message_ref[...] = message
    rows_ref[...] = product(slot_counts_ref[...], message, 1, 0)
    half = slots // 2
    blocks, length = keep_rows_ref.shape[0], keep_rows_ref.shape[1]
    for at in range(blocks):
        mine = pl.multiple_of((at * 2 + core) * length, length)
        other = pl.multiple_of((at * 2 + 1 - core) * length, length)
        keep_rows_ref[at] = rows_ref[pl.ds(mine, length), :].astype(BF16)
        send_ref[own_rows + at * length : own_rows + (at + 1) * length, :] = rows_ref[
            pl.ds(other, length), :
        ].astype(BF16)
    bias = jnp.sum(pre_grad.astype(F32), axis=0, keepdims=True).astype(BF16)
    bias_ref[...] = jnp.broadcast_to(bias, bias_ref.shape)
    send_ref[own_rows + half :, :] = jnp.broadcast_to(bias, bias_ref.shape)


def own_grad_kernel(pre_grad_ref, message_ref, w_self_ref, counts_ref, out_ref):
    own_rows = pre_grad_ref.shape[0]
    out_ref[...] = product(pre_grad_ref[...], w_self_ref[...], 1, 1) + product(
        counts_ref[:, :own_rows], message_ref[...], 0, 0
    )


def pack_kernel(dims, received_ref, keep_ref, keep_rows_ref, bias_ref, after_ref, out_ref):
    across, near, cap = dims
    own_rows, width = keep_ref.shape
    peers, length = out_ref.shape[0], out_ref.shape[1]
    half = 2 * peers * cap
    share = own_rows // peers
    keep_rows = keep_rows_ref[...].astype(F32).reshape(half, width)
    other_rows = received_ref[own_rows : own_rows + half, :].astype(F32)
    bias = bias_ref[...].astype(F32) + received_ref[own_rows + half :, :].astype(F32)
    summed = keep_ref[...] + received_ref[:own_rows, :].astype(F32)
    for peer in range(peers):
        parts = [summed[peer * share : (peer + 1) * share]]
        for wide in range(2):
            at = ((peer // near * 2 + wide) * near + peer % near) * cap
            parts += [keep_rows[at : at + cap], other_rows[at : at + cap]]
        parts.append(bias[: length - share - 4 * cap])
        out_ref[peer] = jnp.concatenate(parts, axis=0).astype(BF16)


def sum_kernel(cap, share, payload_ref, keep_ref, send_ref):
    peers, length, width = payload_ref.shape
    pair = 2 * cap
    count = peers * pair
    grads = jnp.zeros((share, width), F32)
    bias = jnp.zeros((8, width), F32)
    lower, upper = [], []
    for peer in range(peers):
        grads = grads + payload_ref[peer, :share, :].astype(F32)
        rest = payload_ref[peer, share:, :].astype(F32)
        lower.append(rest[:pair])
        upper.append(rest[pair : 2 * pair])
        bias = bias + jnp.broadcast_to(rest[2 * pair : 2 * pair + 1], bias.shape)
    grads = grads.astype(BF16)
    bias = jnp.concatenate([bias, bias], axis=0).astype(BF16)
    first = lax.axis_index("wide") == 0
    lower, upper = jnp.concatenate(lower, axis=0), jnp.concatenate(upper, axis=0)
    for ref, rows in (
        (keep_ref, jnp.where(first, lower, upper)),
        (send_ref, jnp.where(first, upper, lower)),
    ):
        ref[:share, :] = grads
        ref[share : share + count, :] = rows.astype(BF16)
        ref[share + count :, :] = bias


def total_kernel(keep_ref, received_ref, out_ref):
    peers, share, width = out_ref.shape
    total = (keep_ref[:share, :].astype(F32) + received_ref[:share, :].astype(F32)).astype(BF16)
    for peer in range(peers):
        out_ref[peer] = total


def send_half(matrix, source_ref, self_hbm, neigh_hbm, sem, rows, wait):
    source = source_ref.at[rows, :]
    for index, target in enumerate((self_hbm, neigh_hbm)):

        @pl.when(matrix == index)
        def _(target=target):
            copy = pltpu.make_async_copy(source, target.at[rows, :], sem)
            if wait:
                copy.wait()
            else:
                copy.start()


def tail_kernel(
    factor, share, order_ref, keep_ref, received_ref, base_ref, mine_ref,
    out_hbm, self_hbm, neigh_hbm, bias_hbm, wide_ref, out_ref, bias_ref, sems,
):
    own_rows, slots = base_ref.shape[0], order_ref.shape[1]
    half = slots // 2
    matrix = lax.axis_index("core")
    everything = pl.ds(0, own_rows)
    wide_ref[...] = mine_ref[...].astype(F32) * factor
    send_half(matrix, wide_ref, self_hbm, neigh_hbm, sems.at[0], everything, False)
    last = keep_ref.shape[0] - 16
    bias = keep_ref[last:, :].astype(F32) + received_ref[last:, :].astype(F32)
    bias_ref[...] = bias[:1] * factor
    copies = [pltpu.make_async_copy(bias_ref, bias_hbm, sems.at[1])]
    copies[0].start()
    rows = jnp.concatenate(
        [keep_ref[share : share + half, :], received_ref[share : share + half, :]], axis=0
    )
    row = lax.broadcasted_iota(jnp.int32, (own_rows, slots), 0)
    picks = (row == order_ref[...]).astype(F32).astype(BF16)
    out_ref[...] = base_ref[...] + product(picks, rows, 1, 0)
    copies.append(pltpu.make_async_copy(out_ref, out_hbm, sems.at[2]))
    copies[1].start()
    send_half(matrix, wide_ref, self_hbm, neigh_hbm, sems.at[0], everything, True)
    for copy in copies:
        copy.wait()


def other_kernel(factor, half_ref, self_in, neigh_in, self_hbm, neigh_hbm, wide_ref, sems):
    own_rows = half_ref.shape[0]
    pieces = 4
    length = own_rows // pieces
    matrix = 1 - lax.axis_index("core")
    spans = [pl.ds(at * length, length) for at in range(pieces)]
    for at, span in enumerate(spans):
        wide_ref[span, :] = half_ref[span, :].astype(F32) * factor
        send_half(matrix, wide_ref, self_hbm, neigh_hbm, sems.at[at], span, False)
    for at, span in enumerate(spans):
        send_half(matrix, wide_ref, self_hbm, neigh_hbm, sems.at[at], span, True)


def local(features, cotangent, w_self, w_neigh, bias, neighbours, neigh_count, serve_rows):
    own_rows, width = features.shape
    fanout = neighbours.shape[1]
    across, near = lax.axis_size("across"), lax.axis_size("near")
    peers = across * near
    devices = 4 * peers
    slots = serve_rows.shape[1]
    cap = slots // devices
    half = slots // 2
    table_rows = own_rows + slots
    share = own_rows // peers
    length = -(-(share + 4 * cap + 1) // 8) * 8
    everyone = ("across", "core", "wide", "near")
    cube = ("across", "near")
    dims = (across, near, cap)
    swap = [(0, 1), (1, 0)]
    factor = 1.0 / math.sqrt(own_rows * devices)
    work = 2 * own_rows * own_rows * width
    square16 = shape((own_rows, width), BF16)
    square32 = shape((own_rows, width), F32)

    (outgoing,) = call(
        "serve", serve_kernel, (HBM, HBM), ((shape((devices, cap, width), BF16), VMEM),),
        scratch=[VMEM((1, slots), jnp.int32), VMEM((own_rows, width), BF16)],
        copies=2, flops=work // 4, moved=1 << 20,
    )(serve_rows, features)
    incoming = lax.all_to_all(outgoing, everyone, 0, 0, tiled=True)
    counts, slot_counts, inverse, order, flipped, pre = call(
        "own_aggregate", functools.partial(own_kernel, dims), (VMEM,) * 6,
        (
            (shape((own_rows, table_rows), BF16), VMEM),
            (shape((slots, own_rows), BF16), VMEM),
            (shape((own_rows, 128), F32), VMEM),
            (shape((1, slots), jnp.int32), VMEM),
            (shape((width, own_rows), BF16), HBM),
            (square32, HBM),
        ),
        scratch=[
            VMEM((width, own_rows), BF16),
            VMEM((own_rows, width), F32),
            VMEM((fanout, own_rows), jnp.int32),
            VMEM((table_rows, own_rows), BF16),
        ],
        copies=2, flops=20 * work, moved=4 << 20,
    )(
        neighbours.T, neigh_count.reshape(1, own_rows), serve_rows, features, w_self,
        bias.reshape(1, width),
    )
    send, keep, keep_rows, own_bias, pre_grad, message = call(
        "layer_grad", main_kernel, (VMEM,) * 6 + (HBM,) * 3,
        (
            (shape((own_rows + half + 16, width), BF16), VMEM),
            (square32, VMEM),
            (shape((across, 2 * near * cap, width), BF16), VMEM),
            (shape((16, width), BF16), VMEM),
            (square16, VMEM),
            (square16, VMEM),
        ),
        scratch=[
            VMEM((own_rows, width), F32),
            VMEM((own_rows, width), BF16),
            VMEM((width, own_rows), BF16),
            VMEM((slots, width), F32),
        ],
        copies=3, flops=5 * work, moved=8 << 20,
    )(incoming, counts, slot_counts, inverse, features, w_neigh, pre, cotangent, flipped)
    received = lax.ppermute(send, "core", swap)
    (base,) = call(
        "own_grad", own_grad_kernel, (VMEM,) * 4, ((square32, VMEM),), flops=2 * work, moved=4 << 20,
    )(pre_grad, message, w_self, counts)
    (payload,) = call(
        "pack", functools.partial(pack_kernel, dims), (VMEM,) * 5,
        ((shape((peers, length, width), BF16), VMEM),), flops=work // 4, moved=4 << 20,
    )(received, keep, keep_rows, own_bias, base)
    arrived = lax.all_to_all(payload, cube, 0, 0, tiled=True)
    pairs = shape((share + half + 16, width), BF16)
    keep_sum, send_sum = call(
        "sum_shares", functools.partial(sum_kernel, cap, share), (VMEM,),
        ((pairs, VMEM), (pairs, VMEM)), flops=work // 8, moved=1 << 20,
    )(arrived)
    received_sum = lax.ppermute(send_sum, "wide", swap)
    (total,) = call(
        "total", total_kernel, (VMEM, VMEM), ((shape((peers, share, width), BF16), VMEM),),
        flops=work // 8, moved=1 << 20,
    )(keep_sum, received_sum)
    mine = lax.all_to_all(total, cube, 0, 0, tiled=True).reshape(own_rows, width)
    other = lax.ppermute(mine, "core", swap)
    wide = VMEM((own_rows, width), F32)
    grad_features, self_part, neigh_part, bias_sum = call(
        "tail", functools.partial(tail_kernel, factor, share), (VMEM,) * 5,
        ((square32, HBM), (square32, HBM), (square32, HBM), (shape((1, width), F32), HBM)),
        scratch=[wide, wide, VMEM((1, width), F32)], copies=3, flops=work, moved=4 << 20,
    )(order, keep_sum, received_sum, base, mine)
    grad_self, grad_neigh = call(
        "other_half", functools.partial(other_kernel, factor), (VMEM, HBM, HBM),
        ((square32, HBM), (square32, HBM)),
        scratch=[wide], copies=4, flops=work // 2, moved=3 << 20, aliases={1: 0, 2: 1},
    )(other, self_part, neigh_part)
    return grad_features, grad_self, grad_neigh, bias_sum.reshape(width)


def solution(mesh):
    groups, members = mesh.shape["group"], mesh.shape["member"]
    nodes = ("across", "core", "wide", "near")
    fine = Mesh(mesh.devices.reshape(groups // 2, 2, 2, members // 2), nodes)
    rows = P(nodes, None)
    return jax.shard_map(
        local,
        mesh=fine,
        in_specs=(rows, rows, P(), P(), P(), rows, P(nodes), rows),
        out_specs=(rows, P(), P(), P()),
        check_vma=False,
    )
```

time: 71.1 us -> 62.7 us (0.88)
  local copies, waits for them, and re-layouts: 6.64 us -> 1.71 us
  Pallas kernels: 16.9 us -> 12.1 us
  waiting for transfers between devices: 6.92 us -> 11.7 us
  blocking collectives: 29.1 us -> 27.1 us
  starting transfers between devices: 10.1 us -> 8.9 us
    unnamed x28 -> x16, local copies, waits for them, and re-layouts: 6.64 us -> 1.71 us
    pallas_call x10 -> x9, Pallas kernels: 16.9 us -> 12.1 us  [held(): run(*(pltpu.with_memory_space_constraint(operand, HBM) if memory is HBM e...]
    all_to_all x1, waiting for transfers between devices: 0.01 us -> 3.15 us  [local(): incoming = lax.all_to_all(outgoing, everyone, 0, 0, tiled=True)]
    all_to_all x1, blocking collectives: 16.8 us -> 14.9 us  [local(): arrived = lax.all_to_all(payload, cube, 0, 0, tiled=True)]
    ppermute x1, starting transfers between devices: 2.53 us -> 1.42 us  [local(): received_sum = lax.ppermute(send_sum, 'wide', swap)]
    ppermute x1, waiting for transfers between devices: 6.12 us -> 7.15 us  [local(): received_sum = lax.ppermute(send_sum, 'wide', swap)]
  transfers between devices with their start and end apart: 4 -> 4, of which waited for: 2 -> 4; matrix products, arithmetic and copies ran while one was open for 0% -> 0% of each run, Pallas kernels for 12% -> 8%
where the time goes in v3:
time: 62.7 us; the launch traced here: 62.3 us
  blocking collectives  27.1 us (43%)
  Pallas kernels  12.1 us (19%)
  waiting for transfers between devices  11.7 us (19%)
  starting transfers between devices  8.9 us (14%)
  local copies, waits for them, and re-layouts  1.71 us (3%)
  between operations  0.76 us (1%)
    all_to_all x1, blocking collectives, local(): arrived = lax.all_to_all(payload, cube, 0, 0, tiled=True)  14.9 us
    all_to_all x1, blocking collectives, local(): lax.all_to_all(total, cube, 0, 0, tiled=True).reshape(own_rows, width)  12.2 us
    pallas_call x9, Pallas kernels, held(): run(*(pltpu.with_memory_space_constraint(operand, HBM) if memory is HBM e...  12.1 us
    all_to_all x1, starting transfers between devices, local(): incoming = lax.all_to_all(outgoing, everyone, 0, 0, tiled=True)  7.3 us
    ppermute x1, waiting for transfers between devices, local(): received_sum = lax.ppermute(send_sum, 'wide', swap)  7.15 us
    all_to_all x1, waiting for transfers between devices, local(): incoming = lax.all_to_all(outgoing, everyone, 0, 0, tiled=True)  3.15 us
    unnamed x16, local copies, waits for them, and re-layouts  1.71 us
    ppermute x1, starting transfers between devices, local(): received_sum = lax.ppermute(send_sum, 'wide', swap)  1.42 us
  transfers between devices with their start and end apart: 4, of which 4 were waited for; matrix products, arithmetic and copies ran while one was open for 0% of the time, Pallas kernels for 8%

profile of v3, /device:TPU:0, one launch (start us, length us, event | category | flops | bytes accessed | tf_op | source)
XLA Modules:
  0.0 62.3 jit_solution(6749016318616018903)
XLA Ops:
  0.6 2.1 %serve.1 = bf16[32,4,512]{2,1,0:T(4,128)(2,1)} custom-call(s32[1,128]{1,0:T(1,128)} %serve_hbm.1, bf16[512,512]{1,0:T(8,128)(2,1)} %features_ref.3), custom_call_target="tpu_custom_call" | custom-call | flops 67108864 | bytes 1048576 | tf_op jit(solution)/shard_map/serve/pallas_call | solution.py:43
  2.7 0.0 copy-start.5
  2.7 0.0 copy-start.7
  2.7 7.3 %all-to-all-start = ((bf16[32,4,512]{2,1,0:T(4,128)(2,1)}), bf16[32,4,512]{2,1,0:T(4,128)(2,1)S(1)}, u32[]{:S(2)}, u32[]{:S(2)}) async-start(bf16[32,4,512]{2,1,0:T(4,128)(2,1)} %serve.1), calls=%async_computation | async-start | bytes 262144 | tf_op jit(solution)/shard_map/all_to_all | solution.py:313
  10.0 0.0 copy-start.6
  10.0 0.0 copy-start.3
  10.1 0.6 %copy-done.6 = s32[512]{0:T(512)S(1)} copy-done((s32[512]{0:T(512)S(1)}, s32[512]{0:T(512)}, u32[]{:S(2)}) %copy-start.6) | copy-done | bytes 2072
  10.7 1.0 %copy-done.1 = bf16[512,512]{1,0:T(8,128)(2,1)S(1)} copy-done((bf16[512,512]{1,0:T(8,128)(2,1)S(1)}, bf16[512,512]{1,0:T(8,128)(2,1)}, u32[]{:S(2)}) %copy-start.1) | copy-done | bytes 524312
  11.8 2.8 %own_aggregate.1 = (bf16[512,640]{1,0:T(8,128)(2,1)S(1)}, bf16[128,512]{1,0:T(8,128)(2,1)S(1)}, f32[512,128]{1,0:T(8,128)S(1)}, s32[1,128]{1,0:T(1,128)S(1)}, bf...) custom-call(s32[16,512]{1,0:T(8,128)S(1)} %bitcast.7, s32[1,512]{1,0:T(1,128)S(1)} %bitcast.8, s32[1,128]{1,0:T(1,128)S(1)} %copy-done.3, ...), custom_call_target="tpu_custom_call" | custom-call | flops 5368709120 | bytes 4194304 | tf_op jit(solution)/shard_map/own_aggregate/pallas_call | solution.py:43
  14.6 3.1 %all-to-all-done.incoming_ref = bf16[32,4,512]{2,1,0:T(4,128)(2,1)S(1)} async-done(((bf16[32,4,512]{2,1,0:T(4,128)(2,1)}), bf16[32,4,512]{2,1,0:T(4,128)(2,1)S(1)}, u32[]{:S(2)}, u32[]{:S(2)}) %all-to-all-start) | async-done | bytes 131104 | tf_op jit(solution)/shard_map/all_to_all | solution.py:313
  17.8 3.5 %layer_grad.1 = (bf16[592,512]{1,0:T(8,128)(2,1)S(1)}, f32[512,512]{1,0:T(8,128)S(1)}, bf16[2,32,512]{2,1,0:T(8,128)(2,1)S(1)}, bf16[16,512]{1,0:T(8,128)(2,1)S(...) custom-call(bf16[32,4,512]{2,1,0:T(4,128)(2,1)S(1)} %all-to-all-done.incoming_ref, ...), custom_call_target="tpu_custom_call" | custom-call | flops 1342177280 | bytes 8388608 | tf_op jit(solution)/shard_map/layer_grad/pallas_call | solution.py:43
  21.3 0.2 collective-permute-start
  21.5 0.7 %own_grad.1.after_ref.base_ref = f32[512,512]{1,0:T(8,128)S(1)} custom-call(bf16[512,512]{1,0:T(8,128)(2,1)S(1)} %get-tuple-element.34.pre_grad_ref, bf16[512,512]{1,0:T(8,128)(2,1)S(1)} %get-tuple-element.35.message_ref, bf16[512,512]{1,0:T(8,128)(2,1)S(1)} %copy-done, bf16[512,640]{1,0:T(8,128)(2,1)S(1)} %get-tuple-element.25.counts_ref), custom_call_target="tpu_custom_call" | custom-call | flops 536870912 | bytes 4194304 | tf_op jit(solution)/shard_map/own_grad/pallas_call | solution.py:43
  22.2 1.2 %collective-permute-done.received_ref = bf16[592,512]{1,0:T(8,128)(2,1)S(1)} collective-permute-done((bf16[592,512]{1,0:T(8,128)(2,1)S(1)}, bf16[592,512]{1,0:T(8,128)(2,1)S(1)}, u32[]{:S(2)}, u32[]{:S(2)}) %collective-permute-start) | collective-permute-done | bytes 606240 | tf_op jit(solution)/shard_map/ppermute | solution.py:353
  23.4 0.1 pack.1
  23.5 14.9 %all_to_all.15.payload_ref = bf16[8,88,512]{2,1,0:T(8,128)(2,1)S(1)} all-to-all(bf16[8,88,512]{2,1,0:T(8,128)(2,1)S(1)} %pack.1), channel_id=1, replica_groups=mesh['across'=2,'core'=2,'wide'=2,'near'=4] {'across','near'}, dimensions={0} | all-to-all | bytes 1441792 | tf_op jit(solution)/shard_map/all_to_all | solution.py:361
  38.4 0.1 sum_shares.1
  38.5 1.4 %collective-permute-start.1 = (bf16[144,512]{1,0:T(8,128)(2,1)S(1)}, bf16[144,512]{1,0:T(8,128)(2,1)S(1)}, u32[]{:S(2)}, u32[]{:S(2)}) collective-permute-start(bf16[144,512]{1,0:T(8,128)(2,1)S(1)} %get-tuple-element.37), channel_id=1, source_target_pairs={{0,4},{4,0},{1,5},{5,1},{2,6},{6,2},{3,7},{7,3},{8,12},{12,8},{9,1... | collective-permute-start | bytes 442376 | tf_op jit(solution)/shard_map/ppermute | solution.py:367
  39.9 7.2 %collective-permute-done.1.received_ref = bf16[144,512]{1,0:T(8,128)(2,1)S(1)} collective-permute-done((bf16[144,512]{1,0:T(8,128)(2,1)S(1)}, bf16[144,512]{1,0:T(8,128)(2,1)S(1)}, u32[]{:S(2)}, u32[]{:S(2)}) %collective-permute-start.1) | collective-permute-done | bytes 147488 | tf_op jit(solution)/shard_map/ppermute | solution.py:367
  47.1 12.2 %all_to_all.16 = bf16[8,64,512]{2,1,0:T(8,128)(2,1)S(1)} all-to-all(bf16[8,64,512]{2,1,0:T(8,128)(2,1)S(1)} %total.1), channel_id=1, replica_groups=mesh['across'=2,'core'=2,'wide'=2,'near'=4] {'across','near'}, dimensions={0} | all-to-all | bytes 1048576 | tf_op jit(solution)/shard_map/all_to_all | solution.py:372
  59.3 0.0 collective-permute-start.2
  59.3 1.7 %tail.1 = (f32[512,512]{1,0:T(8,128)}, f32[512,512]{1,0:T(8,128)}, f32[512,512]{1,0:T(8,128)}, f32[1,512]{1,0:T(1,128)}) custom-call(s32[1,128]{1,0:T(1,128)S(1)} %get-tuple-element.24.order_ref, bf16[144,512]{1,0:T(8,128)(2,1)S(1)} %get-tuple-element.36.keep_ref, bf16[144,512]{1,0:T(8,128)(2,1)S(1)} %collective-permute-done.1.received_ref, ...), custom_call_target="tpu_custom_call" | custom-call | flops 268435456 | bytes 4194304 | tf_op jit(solution)/shard_map/tail/pallas_call | solution.py:43
  61.0 0.2 collective-permute-done.2.half_ref
  61.3 1.0 %other_half.1 = (f32[512,512]{1,0:T(8,128)}, f32[512,512]{1,0:T(8,128)}) custom-call(bf16[512,512]{1,0:T(8,128)(2,1)S(1)} %collective-permute-done.2.half_ref, f32[512,512]{1,0:T(8,128)} %get-tuple-element.39.self_in, f32[512,512]{1,0:T(8,128)} %get-tuple-element.40.neigh_in), custom_call_target="tpu_custom_call", output_to_operand_aliasing={{0}: (1, {}), {1}: (2, {})} | custom-call | flops 134217728 | bytes 3145728 | tf_op jit(solution)/shard_map/other_half/pallas_call | solution.py:43
  (11 shorter events, 0.1 us)
Async XLA Ops:
  0.6 9.4 %copy-start = (bf16[512,512]{1,0:T(8,128)(2,1)S(1)}, bf16[512,512]{1,0:T(8,128)(2,1)}, u32[]{:S(2)}) copy-start(bf16[512,512]{1,0:T(8,128)(2,1)} %w_self_ref.3) | copy-start | bytes 1572868
  2.7 7.4 %copy-start.5 = (s32[512,16]{0,1:T(8,128)S(1)}, s32[512,16]{0,1:T(8,128)}, u32[]{:S(2)}) copy-start(s32[512,16]{0,1:T(8,128)} %param.13) | copy-start | bytes 98308
  2.7 7.4 %copy-start.7 = (f32[512]{0:T(512)S(1)}, f32[512]{0:T(512)}, u32[]{:S(2)}) copy-start(f32[512]{0:T(512)} %param.12) | copy-start | bytes 6148
  2.7 15.1 %all-to-all-start = ((bf16[32,4,512]{2,1,0:T(4,128)(2,1)}), bf16[32,4,512]{2,1,0:T(4,128)(2,1)S(1)}, u32[]{:S(2)}, u32[]{:S(2)}) async-start(bf16[32,4,512]{2,1,0:T(4,128)(2,1)} %serve.1), calls=%async_computation | async-start | bytes 262144 | tf_op jit(solution)/shard_map/all_to_all | solution.py:313
  10.0 0.7 %copy-start.6 = (s32[512]{0:T(512)S(1)}, s32[512]{0:T(512)}, u32[]{:S(2)}) copy-start(s32[512]{0:T(512)} %param.14) | copy-start | bytes 6148
  10.0 0.7 %copy-start.3 = (s32[1,128]{1,0:T(1,128)S(1)}, s32[1,128]{1,0:T(1,128)}, u32[]{:S(2)}) copy-start(s32[1,128]{1,0:T(1,128)} %serve_hbm.1) | copy-start | bytes 1540
  10.7 1.0 %copy-start.1 = (bf16[512,512]{1,0:T(8,128)(2,1)S(1)}, bf16[512,512]{1,0:T(8,128)(2,1)}, u32[]{:S(2)}) copy-start(bf16[512,512]{1,0:T(8,128)(2,1)} %features_ref.3) | copy-start | bytes 1572868
  11.8 6.0 %copy-start.2 = (bf16[512,512]{1,0:T(8,128)(2,1)S(1)}, bf16[512,512]{1,0:T(8,128)(2,1)}, u32[]{:S(2)}) copy-start(bf16[512,512]{1,0:T(8,128)(2,1)} %features_ref.3) | copy-start | bytes 1572868
  11.8 6.0 %copy-start.4 = (bf16[512,512]{1,0:T(8,128)(2,1)S(1)}, bf16[512,512]{1,0:T(8,128)(2,1)}, u32[]{:S(2)}) copy-start(bf16[512,512]{1,0:T(8,128)(2,1)} %w_neigh_ref.1) | copy-start | bytes 1572868
  21.3 2.1 %collective-permute-start = (bf16[592,512]{1,0:T(8,128)(2,1)S(1)}, bf16[592,512]{1,0:T(8,128)(2,1)S(1)}, u32[]{:S(2)}, u32[]{:S(2)}) collective-permute-start(bf16[592,512]{1,0:T(8,128)(2,1)S(1)} %get-tuple-element.30), channel_id=1, source_target_pairs={{0,8},{8,0},{1,9},{9,1},{2,10},{10,2},{3,11},{11,3},{4,12},{12,4},... | collective-permute-start | bytes 1818632 | tf_op jit(solution)/shard_map/ppermute | solution.py:353
  38.5 8.6 %collective-permute-start.1 = (bf16[144,512]{1,0:T(8,128)(2,1)S(1)}, bf16[144,512]{1,0:T(8,128)(2,1)S(1)}, u32[]{:S(2)}, u32[]{:S(2)}) collective-permute-start(bf16[144,512]{1,0:T(8,128)(2,1)S(1)} %get-tuple-element.37), channel_id=1, source_target_pairs={{0,4},{4,0},{1,5},{5,1},{2,6},{6,2},{3,7},{7,3},{8,12},{12,8},{9,1... | collective-permute-start | bytes 442376 | tf_op jit(solution)/shard_map/ppermute | solution.py:367
  59.3 1.9 %collective-permute-start.2 = (bf16[512,512]{1,0:T(8,128)(2,1)S(1)}, bf16[512,512]{1,0:T(8,128)(2,1)S(1)}, u32[]{:S(2)}, u32[]{:S(2)}) collective-permute-start(bf16[512,512]{1,0:T(8,128)(2,1)S(1)} %bitcast.5), channel_id=1, source_target_pairs={{0,8},{8,0},{1,9},{9,1},{2,10},{10,2},{3,11},{11,3},{4,12},{12,4},... | collective-permute-start | bytes 1572872 | tf_op jit(solution)/shard_map/ppermute | solution.py:373

commit v4 on v3

--- a/solution.py
+++ b/solution.py
@@ -60,24 +60,44 @@
     own_rows = features_ref.shape[0]
     slots = serve_ref.shape[1]
     copies[0].wait()
-    row = lax.broadcasted_iota(jnp.int32, (own_rows, slots), 0)
-    picks = (row == serve_ref[...]).astype(F32).astype(BF16)
+    wanted = jnp.broadcast_to(serve_ref[...], (128, slots)).astype(F32).T
+    row = lax.broadcasted_iota(jnp.int32, (slots, 128), 1).astype(F32)
+    picks = jnp.concatenate(
+        [
+            jnp.where(row + float(at) == wanted, 1.0, 0.0).astype(BF16)
+            for at in range(0, own_rows, 128)
+        ],
+        axis=1,
+    )
     copies[1].wait()
-    rows = product(picks, features_ref[...], 0, 0)
+    rows = product(picks, features_ref[...], 1, 0)
     out_ref[...] = rows.reshape(out_ref.shape).astype(BF16)
 
 
 def own_kernel(
-    dims, neighbours_ref, count_ref, serve_ref, features_ref, w_self_ref, bias_ref,
-    counts_ref, slot_counts_ref, inverse_ref, order_ref, flipped_hbm, pre_hbm,
-    flipped_ref, pre_ref, live_ref, table_ref, sems,
+    dims, neighbours_hbm, count_hbm, serve_hbm, features_hbm, w_self_hbm, bias_hbm,
+    own_sum_ref, fetch_counts_ref, slot_counts_ref, inverse_ref, order_ref, top_ref, low_hbm, own_counts_hbm,
+    neighbours_ref, count_ref, serve_ref, features_ref, w_self_ref, bias_ref, low_ref, live_ref, table_ref, sems,
 ):
+    ins = start_all(
+        sems,
+        (neighbours_hbm, neighbours_ref),
+        (count_hbm, count_ref),
+        (serve_hbm, serve_ref),
+        (features_hbm, features_ref),
+        (w_self_hbm, w_self_ref),
+        (bias_hbm, bias_ref),
+    )
     fanout, own_rows = neighbours_ref.shape
     table_rows = table_ref.shape[0]
+    for copy in ins:
+        copy.wait()
     features = features_ref[...]
-    flipped_ref[...] = features.T
-    pre_ref[...] = product(features, w_self_ref[...], 1, 0) + bias_ref[...]
-    copies = start_all(sems, (flipped_ref, flipped_hbm), (pre_ref, pre_hbm))
+    upper = own_rows // 2
+    low_ref[...] = product(features[upper:], w_self_ref[...], 1, 0) + bias_ref[...]
+    copies = [pltpu.make_async_copy(low_ref, low_hbm, sems.at[len(ins)])]
+    copies[0].start()
+    top_ref[...] = product(features[:upper], w_self_ref[...], 1, 0) + bias_ref[...]
     count = count_ref[...]
     position = lax.broadcasted_iota(jnp.int32, (fanout, own_rows), 0)
     live_ref[...] = jnp.where(position < count, neighbours_ref[...], -1)
@@ -94,7 +114,11 @@
         return carry
 
     lax.fori_loop(0, table_rows // step, fill, 0)
-    counts_ref[...] = table_ref[...].T
+    own_counts = table_ref.at[pl.ds(0, own_rows), :]
+    copies.append(pltpu.make_async_copy(own_counts, own_counts_hbm, sems.at[len(ins) + 1]))
+    copies[-1].start()
+    own_sum_ref[...] = product(table_ref[:own_rows, :], features, 0, 0)
+    fetch_counts_ref[...] = table_ref[own_rows:, :].T
     slot_counts_ref[...] = table_ref[own_rows:, :]
     across, near, cap = dims
     slots = serve_ref.shape[1]
@@ -122,41 +146,38 @@
 
 
 def main_kernel(
-    incoming_ref, counts_ref, slot_counts_ref, inverse_ref, features_ref, w_neigh_ref,
-    pre_hbm, cotangent_hbm, flipped_hbm,
+    incoming_ref, own_sum_ref, fetch_counts_ref, slot_counts_ref, inverse_ref, w_neigh_ref, cotangent_ref, top_ref,
+    low_hbm, features_hbm,
     send_ref, keep_ref, keep_rows_ref, bias_ref, pre_grad_ref, message_ref,
-    pre_ref, cotangent_ref, flipped_ref, rows_ref, sems,
+    low_ref, left_ref, rows_ref, sems,
 ):
-    own_rows, width = features_ref.shape
+    own_rows, width = own_sum_ref.shape
     slots = rows_ref.shape[0]
-    copies = start_all(
-        sems, (pre_hbm, pre_ref), (cotangent_hbm, cotangent_ref), (flipped_hbm, flipped_ref)
-    )
     core = lax.axis_index("core")
-    first = core == 0
+    copies = start_all(sems, (low_hbm, low_ref), (features_hbm, left_ref.at[0]))
     incoming = incoming_ref[...].astype(F32).reshape(slots, width).astype(BF16)
-    summed = product(counts_ref[:, :own_rows], features_ref[...], 1, 0) + product(
-        counts_ref[:, own_rows:], incoming, 1, 0
-    )
     inverse = spread_wide(inverse_ref[...], width)
+    summed = own_sum_ref[...] + product(fetch_counts_ref[...], incoming, 1, 0)
     aggregated = (summed * inverse).astype(BF16)
-    mixed = product(aggregated, w_neigh_ref[...], 1, 0)
-    copies[0].wait()
-    pre = pre_ref[...] + mixed
-    sigmoid_pre = jax.nn.sigmoid(pre)
-    copies[1].wait()
-    pre_grad = (
-        cotangent_ref[...].astype(F32) * sigmoid_pre * (1.0 + pre * (1.0 - sigmoid_pre))
-    ).astype(BF16)
-    pre_grad_ref[...] = pre_grad
-    copies[2].wait()
-    grad_self = product(flipped_ref[...], pre_grad, 1, 0)
-    grad_neigh = product(aggregated, pre_grad, 0, 0)
-    keep_ref[...] = jnp.where(first, grad_self, grad_neigh)
-    send_ref[:own_rows, :] = jnp.where(first, grad_neigh, grad_self).astype(BF16)
+    left_ref[1] = aggregated
+    upper = own_rows // 2
+    for at, part_ref in enumerate((top_ref, low_ref)):
+        rows = slice(at * upper, (at + 1) * upper)
+        mixed = product(aggregated[rows], w_neigh_ref[...], 1, 0)
+        if at:
+            copies[0].wait()
+        pre = part_ref[...] + mixed
+        sigmoid_pre = jax.nn.sigmoid(pre)
+        pre_grad_ref[rows] = (
+            cotangent_ref[rows].astype(F32) * sigmoid_pre * (1.0 + pre * (1.0 - sigmoid_pre))
+        ).astype(BF16)
+    pre_grad = pre_grad_ref[...]
     message = (product(pre_grad, w_neigh_ref[...], 1, 1) * inverse).astype(BF16)
     message_ref[...] = message
     rows_ref[...] = product(slot_counts_ref[...], message, 1, 0)
+    copies[1].wait()
+    keep_ref[...] = product(left_ref[core], pre_grad, 0, 0)
+    send_ref[:own_rows, :] = product(left_ref[1 - core], pre_grad, 0, 0).astype(BF16)
     half = slots // 2
     blocks, length = keep_rows_ref.shape[0], keep_rows_ref.shape[1]
     for at in range(blocks):
@@ -171,14 +192,17 @@
     send_ref[own_rows + half :, :] = jnp.broadcast_to(bias, bias_ref.shape)
 
 
-def own_grad_kernel(pre_grad_ref, message_ref, w_self_ref, counts_ref, out_ref):
-    own_rows = pre_grad_ref.shape[0]
-    out_ref[...] = product(pre_grad_ref[...], w_self_ref[...], 1, 1) + product(
-        counts_ref[:, :own_rows], message_ref[...], 0, 0
-    )
-
-
-def pack_kernel(dims, received_ref, keep_ref, keep_rows_ref, bias_ref, after_ref, out_ref):
+def own_grad_kernel(
+    pre_grad_ref, message_ref, w_self_hbm, counts_hbm, out_ref, w_self_ref, counts_ref, sems
+):
+    copies = start_all(sems, (counts_hbm, counts_ref), (w_self_hbm, w_self_ref))
+    copies[0].wait()
+    spread = product(counts_ref[...], message_ref[...], 1, 0)
+    copies[1].wait()
+    out_ref[...] = spread + product(pre_grad_ref[...], w_self_ref[...], 1, 1)
+
+
+def pack_kernel(dims, received_ref, keep_ref, keep_rows_ref, bias_ref, out_ref):
     across, near, cap = dims
     own_rows, width = keep_ref.shape
     peers, length = out_ref.shape[0], out_ref.shape[1]
@@ -211,7 +235,7 @@
         upper.append(rest[pair : 2 * pair])
         bias = bias + jnp.broadcast_to(rest[2 * pair : 2 * pair + 1], bias.shape)
     grads = grads.astype(BF16)
-    bias = jnp.concatenate([bias, bias], axis=0).astype(BF16)
+    bias = bias.astype(BF16)
     first = lax.axis_index("wide") == 0
     lower, upper = jnp.concatenate(lower, axis=0), jnp.concatenate(upper, axis=0)
     for ref, rows in (
@@ -223,7 +247,7 @@
         ref[share + count :, :] = bias
 
 
-def total_kernel(keep_ref, received_ref, out_ref):
+def total_kernel(keep_ref, received_ref, after_ref, out_ref):
     peers, share, width = out_ref.shape
     total = (keep_ref[:share, :].astype(F32) + received_ref[:share, :].astype(F32)).astype(BF16)
     for peer in range(peers):
@@ -253,7 +277,7 @@
     everything = pl.ds(0, own_rows)
     wide_ref[...] = mine_ref[...].astype(F32) * factor
     send_half(matrix, wide_ref, self_hbm, neigh_hbm, sems.at[0], everything, False)
-    last = keep_ref.shape[0] - 16
+    last = keep_ref.shape[0] - 8
     bias = keep_ref[last:, :].astype(F32) + received_ref[last:, :].astype(F32)
     bias_ref[...] = bias[:1] * factor
     copies = [pltpu.make_async_copy(bias_ref, bias_hbm, sems.at[1])]
@@ -311,64 +335,73 @@
         copies=2, flops=work // 4, moved=1 << 20,
     )(serve_rows, features)
     incoming = lax.all_to_all(outgoing, everyone, 0, 0, tiled=True)
-    counts, slot_counts, inverse, order, flipped, pre = call(
-        "own_aggregate", functools.partial(own_kernel, dims), (VMEM,) * 6,
+    upper = shape((own_rows // 2, width), F32)
+    own_sum, fetch_counts, slot_counts, inverse, order, top, low, own_counts = call(
+        "own_aggregate", functools.partial(own_kernel, dims), (HBM,) * 6,
         (
-            (shape((own_rows, table_rows), BF16), VMEM),
+            (square32, VMEM),
+            (shape((own_rows, slots), BF16), VMEM),
             (shape((slots, own_rows), BF16), VMEM),
             (shape((own_rows, 128), F32), VMEM),
             (shape((1, slots), jnp.int32), VMEM),
-            (shape((width, own_rows), BF16), HBM),
-            (square32, HBM),
+            (upper, VMEM),
+            (upper, HBM),
+            (shape((own_rows, own_rows), BF16), HBM),
         ),
         scratch=[
-            VMEM((width, own_rows), BF16),
-            VMEM((own_rows, width), F32),
+            VMEM((fanout, own_rows), jnp.int32),
+            VMEM((1, own_rows), jnp.int32),
+            VMEM((1, slots), jnp.int32),
+            VMEM((own_rows, width), BF16),
+            VMEM((width, width), BF16),
+            VMEM((1, width), F32),
+            VMEM(upper.shape, F32),
             VMEM((fanout, own_rows), jnp.int32),
             VMEM((table_rows, own_rows), BF16),
         ],
-        copies=2, flops=20 * work, moved=4 << 20,
+        copies=8, flops=20 * work, moved=4 << 20,
     )(
         neighbours.T, neigh_count.reshape(1, own_rows), serve_rows, features, w_self,
         bias.reshape(1, width),
     )
     send, keep, keep_rows, own_bias, pre_grad, message = call(
-        "layer_grad", main_kernel, (VMEM,) * 6 + (HBM,) * 3,
+        "layer_grad", main_kernel, (VMEM,) * 8 + (HBM,) * 2,
         (
-            (shape((own_rows + half + 16, width), BF16), VMEM),
+            (shape((own_rows + half + 8, width), BF16), VMEM),
             (square32, VMEM),
             (shape((across, 2 * near * cap, width), BF16), VMEM),
-            (shape((16, width), BF16), VMEM),
+            (shape((8, width), BF16), VMEM),
             (square16, VMEM),
             (square16, VMEM),
         ),
         scratch=[
-            VMEM((own_rows, width), F32),
-            VMEM((own_rows, width), BF16),
-            VMEM((width, own_rows), BF16),
+            VMEM(upper.shape, F32),
+            VMEM((2, own_rows, width), BF16),
             VMEM((slots, width), F32),
         ],
-        copies=3, flops=5 * work, moved=8 << 20,
-    )(incoming, counts, slot_counts, inverse, features, w_neigh, pre, cotangent, flipped)
+        copies=2, flops=5 * work, moved=8 << 20,
+    )(incoming, own_sum, fetch_counts, slot_counts, inverse, w_neigh, cotangent, top, low, features)
     received = lax.ppermute(send, "core", swap)
     (base,) = call(
-        "own_grad", own_grad_kernel, (VMEM,) * 4, ((square32, VMEM),), flops=2 * work, moved=4 << 20,
-    )(pre_grad, message, w_self, counts)
+        "own_grad", own_grad_kernel, (VMEM, VMEM, HBM, HBM), ((square32, VMEM),),
+        scratch=[VMEM((width, width), BF16), VMEM((own_rows, own_rows), BF16)],
+        copies=2, flops=2 * work, moved=4 << 20,
+    )(pre_grad, message, w_self, own_counts)
     (payload,) = call(
-        "pack", functools.partial(pack_kernel, dims), (VMEM,) * 5,
+        "pack", functools.partial(pack_kernel, dims), (VMEM,) * 4,
         ((shape((peers, length, width), BF16), VMEM),), flops=work // 4, moved=4 << 20,
-    )(received, keep, keep_rows, own_bias, base)
+    )(received, keep, keep_rows, own_bias)
     arrived = lax.all_to_all(payload, cube, 0, 0, tiled=True)
-    pairs = shape((share + half + 16, width), BF16)
+    pairs = shape((share + half + 8, width), BF16)
     keep_sum, send_sum = call(
         "sum_shares", functools.partial(sum_kernel, cap, share), (VMEM,),
         ((pairs, VMEM), (pairs, VMEM)), flops=work // 8, moved=1 << 20,
     )(arrived)
     received_sum = lax.ppermute(send_sum, "wide", swap)
     (total,) = call(
-        "total", total_kernel, (VMEM, VMEM), ((shape((peers, share, width), BF16), VMEM),),
+        "total", total_kernel, (VMEM, VMEM, VMEM), ((shape((peers, share, width), BF16), VMEM),),
         flops=work // 8, moved=1 << 20,
-    )(keep_sum, received_sum)
+    )(keep_sum, received_sum, base)
     mine = lax.all_to_all(total, cube, 0, 0, tiled=True).reshape(own_rows, width)
     other = lax.ppermute(mine, "core", swap)
     wide = VMEM((own_rows, width), F32)

time: 62.7 us -> 61.1 us (0.974)
  waiting for transfers between devices: 11.7 us -> 9.4 us
  Pallas kernels: 12.1 us -> 14.3 us
  local copies, waits for them, and re-layouts: 1.71 us -> 0.01 us
    ppermute x1, waiting for transfers between devices: 7.15 us -> 4.52 us  [local(): received_sum = lax.ppermute(send_sum, 'wide', swap)]
    pallas_call x9, Pallas kernels: 12.1 us -> 14.3 us  [held(): run(*(pltpu.with_memory_space_constraint(operand, HBM) if memory is HBM e...]
    unnamed x16 -> x4, local copies, waits for them, and re-layouts: 1.71 us -> 0.01 us
    ppermute x1, waiting for transfers between devices: 1.19 us -> 1.9 us  [local(): received = lax.ppermute(send, 'core', swap)]
  transfers between devices with their start and end apart: 4 -> 4, of which waited for: 4 -> 4; matrix products, arithmetic and copies ran while one was open for 0% -> 0% of each run, Pallas kernels for 8% -> 14%
where the time goes in v4:
time: 61.1 us; the launch traced here: 60.7 us
  blocking collectives  27 us (44%)
  Pallas kernels  14.3 us (23%)
  waiting for transfers between devices  9.4 us (15%)
  starting transfers between devices  9.23 us (15%)
  between operations  0.71 us (1%)
    all_to_all x1, blocking collectives, local(): arrived = lax.all_to_all(payload, cube, 0, 0, tiled=True)  14.9 us
    pallas_call x9, Pallas kernels, held(): run(*(pltpu.with_memory_space_constraint(operand, HBM) if memory is HBM e...  14.3 us
    all_to_all x1, blocking collectives, local(): lax.all_to_all(total, cube, 0, 0, tiled=True).reshape(own_rows, width)  12.1 us
    all_to_all x1, starting transfers between devices, local(): incoming = lax.all_to_all(outgoing, everyone, 0, 0, tiled=True)  7.3 us
    ppermute x1, waiting for transfers between devices, local(): received_sum = lax.ppermute(send_sum, 'wide', swap)  4.52 us
    all_to_all x1, waiting for transfers between devices, local(): incoming = lax.all_to_all(outgoing, everyone, 0, 0, tiled=True)  2.78 us
    ppermute x1, waiting for transfers between devices, local(): received = lax.ppermute(send, 'core', swap)  1.9 us
    ppermute x1, starting transfers between devices, local(): received_sum = lax.ppermute(send_sum, 'wide', swap)  1.75 us
  transfers between devices with their start and end apart: 4, of which 4 were waited for; matrix products, arithmetic and copies ran while one was open for 0% of the time, Pallas kernels for 14%

profile of v4, /device:TPU:0, one launch (start us, length us, event | category | flops | bytes accessed | tf_op | source)
XLA Modules:
  0.0 60.7 jit_solution(14859626421416752723)
XLA Ops:
  0.6 2.0 %serve.1 = bf16[32,4,512]{2,1,0:T(4,128)(2,1)} custom-call(s32[1,128]{1,0:T(1,128)} %serve_hbm.3, bf16[512,512]{1,0:T(8,128)(2,1)} %features_hbm.5), custom_call_target="tpu_custom_call" | custom-call | flops 67108864 | bytes 1048576 | tf_op jit(solution)/shard_map/serve/pallas_call | solution.py:43
  2.6 7.3 %all-to-all-start = ((bf16[32,4,512]{2,1,0:T(4,128)(2,1)}), bf16[32,4,512]{2,1,0:T(4,128)(2,1)S(1)}, u32[]{:S(2)}, u32[]{:S(2)}) async-start(bf16[32,4,512]{2,1,0:T(4,128)(2,1)} %serve.1), calls=%async_computation | async-start | bytes 262144 | tf_op jit(solution)/shard_map/all_to_all | solution.py:337
  9.9 0.0 copy-start
  9.9 0.0 copy-start.1
  9.9 4.9 %own_aggregate.1 = (f32[512,512]{1,0:T(8,128)S(1)}, bf16[512,128]{1,0:T(8,128)(2,1)S(1)}, bf16[128,512]{1,0:T(8,128)(2,1)S(1)}, f32[512,128]{1,0:T(8,128)S(1)}, ...) custom-call(s32[16,512]{1,0:T(8,128)} %bitcast.7, ...), custom_call_target="tpu_custom_call" | custom-call | flops 5368709120 | bytes 4194304 | tf_op jit(solution)/shard_map/own_aggregate/pallas_call | solution.py:43
  14.9 2.8 %all-to-all-done.incoming_ref = bf16[32,4,512]{2,1,0:T(4,128)(2,1)S(1)} async-done(((bf16[32,4,512]{2,1,0:T(4,128)(2,1)}), bf16[32,4,512]{2,1,0:T(4,128)(2,1)S(1)}, u32[]{:S(2)}, u32[]{:S(2)}) %all-to-all-start) | async-done | bytes 131104 | tf_op jit(solution)/shard_map/all_to_all | solution.py:337
  17.7 0.0 copy-done
  17.7 0.0 copy-done.1
  17.7 2.5 %layer_grad.1 = (bf16[584,512]{1,0:T(8,128)(2,1)S(1)}, f32[512,512]{1,0:T(8,128)S(1)}, bf16[2,32,512]{2,1,0:T(8,128)(2,1)S(1)}, bf16[8,512]{1,0:T(8,128)(2,1)S(1...) custom-call(bf16[32,4,512]{2,1,0:T(4,128)(2,1)S(1)} %all-to-all-done.incoming_ref, ...), custom_call_target="tpu_custom_call" | custom-call | flops 1342177280 | bytes 8388608 | tf_op jit(solution)/shard_map/layer_grad/pallas_call | solution.py:43
  20.2 0.2 collective-permute-start
  20.3 1.9 %collective-permute-done.received_ref = bf16[584,512]{1,0:T(8,128)(2,1)S(1)} collective-permute-done((bf16[584,512]{1,0:T(8,128)(2,1)S(1)}, bf16[584,512]{1,0:T(8,128)(2,1)S(1)}, u32[]{:S(2)}, u32[]{:S(2)}) %collective-permute-start) | collective-permute-done | bytes 598048 | tf_op jit(solution)/shard_map/ppermute | solution.py:384
  22.2 0.1 pack.1
  22.4 14.9 %all_to_all.15.payload_ref = bf16[8,88,512]{2,1,0:T(8,128)(2,1)S(1)} all-to-all(bf16[8,88,512]{2,1,0:T(8,128)(2,1)S(1)} %pack.1), channel_id=1, replica_groups=mesh['across'=2,'core'=2,'wide'=2,'near'=4] {'across','near'}, dimensions={0} | all-to-all | bytes 1441792 | tf_op jit(solution)/shard_map/all_to_all | solution.py:394
  37.3 0.1 sum_shares.1
  37.4 1.7 %collective-permute-start.1 = (bf16[136,512]{1,0:T(8,128)(2,1)S(1)}, bf16[136,512]{1,0:T(8,128)(2,1)S(1)}, u32[]{:S(2)}, u32[]{:S(2)}) collective-permute-start(bf16[136,512]{1,0:T(8,128)(2,1)S(1)} %get-tuple-element.38), channel_id=1, source_target_pairs={{0,4},{4,0},{1,5},{5,1},{2,6},{6,2},{3,7},{7,3},{8,12},{12,8},{9,1... | collective-permute-start | bytes 417800 | tf_op jit(solution)/shard_map/ppermute | solution.py:400
  39.1 2.0 %own_grad.1.after_ref.base_ref = f32[512,512]{1,0:T(8,128)S(1)} custom-call(bf16[512,512]{1,0:T(8,128)(2,1)S(1)} %get-tuple-element.39.pre_grad_ref, bf16[512,512]{1,0:T(8,128)(2,1)S(1)} %get-tuple-element.40.message_ref, bf16[512,512]{1,0:T(8,128)(2,1)} %w_self_hbm.3, bf16[512,512]{1,0:T(8,128)(2,1)} %get-tuple-element.41.counts_hbm), custom_call_target="tpu_custom_call" | custom-call | flops 536870912 | bytes 4194304 | tf_op jit(solution)/shard_map/own_grad/pallas_call | solution.py:43
  41.1 4.5 %collective-permute-done.1.received_ref = bf16[136,512]{1,0:T(8,128)(2,1)S(1)} collective-permute-done((bf16[136,512]{1,0:T(8,128)(2,1)S(1)}, bf16[136,512]{1,0:T(8,128)(2,1)S(1)}, u32[]{:S(2)}, u32[]{:S(2)}) %collective-permute-start.1) | collective-permute-done | bytes 139296 | tf_op jit(solution)/shard_map/ppermute | solution.py:400
  45.6 12.1 %all_to_all.16 = bf16[8,64,512]{2,1,0:T(8,128)(2,1)S(1)} all-to-all(bf16[8,64,512]{2,1,0:T(8,128)(2,1)S(1)} %total.1), channel_id=1, replica_groups=mesh['across'=2,'core'=2,'wide'=2,'near'=4] {'across','near'}, dimensions={0} | all-to-all | bytes 1048576 | tf_op jit(solution)/shard_map/all_to_all | solution.py:405
  57.8 0.0 collective-permute-start.2
  57.8 1.7 %tail.1 = (f32[512,512]{1,0:T(8,128)}, f32[512,512]{1,0:T(8,128)}, f32[512,512]{1,0:T(8,128)}, f32[1,512]{1,0:T(1,128)}) custom-call(s32[1,128]{1,0:T(1,128)S(1)} %get-tuple-element.26.order_ref, bf16[136,512]{1,0:T(8,128)(2,1)S(1)} %get-tuple-element.37.keep_ref, bf16[136,512]{1,0:T(8,128)(2,1)S(1)} %collective-permute-done.1.received_ref, ...), custom_call_target="tpu_custom_call" | custom-call | flops 268435456 | bytes 4194304 | tf_op jit(solution)/shard_map/tail/pallas_call | solution.py:43
  59.5 0.2 collective-permute-done.2.half_ref
  59.7 1.0 %other_half.1 = (f32[512,512]{1,0:T(8,128)}, f32[512,512]{1,0:T(8,128)}) custom-call(bf16[512,512]{1,0:T(8,128)(2,1)S(1)} %collective-permute-done.2.half_ref, f32[512,512]{1,0:T(8,128)} %get-tuple-element.43.self_in, f32[512,512]{1,0:T(8,128)} %get-tuple-element.44.neigh_in), custom_call_target="tpu_custom_call", output_to_operand_aliasing={{0}: (1, {}), {1}: (2, {})} | custom-call | flops 134217728 | bytes 3145728 | tf_op jit(solution)/shard_map/other_half/pallas_call | solution.py:43
  (1 shorter events, 0.0 us)
Async XLA Ops:
  2.6 15.1 %all-to-all-start = ((bf16[32,4,512]{2,1,0:T(4,128)(2,1)}), bf16[32,4,512]{2,1,0:T(4,128)(2,1)S(1)}, u32[]{:S(2)}, u32[]{:S(2)}) async-start(bf16[32,4,512]{2,1,0:T(4,128)(2,1)} %serve.1), calls=%async_computation | async-start | bytes 262144 | tf_op jit(solution)/shard_map/all_to_all | solution.py:337
  9.9 7.7 %copy-start = (bf16[512,512]{1,0:T(8,128)(2,1)S(1)}, bf16[512,512]{1,0:T(8,128)(2,1)}, u32[]{:S(2)}) copy-start(bf16[512,512]{1,0:T(8,128)(2,1)} %w_neigh_ref.1) | copy-start | bytes 1572868
  9.9 7.7 %copy-start.1 = (bf16[512,512]{1,0:T(8,128)(2,1)S(1)}, bf16[512,512]{1,0:T(8,128)(2,1)}, u32[]{:S(2)}) copy-start(bf16[512,512]{1,0:T(8,128)(2,1)} %cotangent_ref.1) | copy-start | bytes 1572868
  20.2 2.1 %collective-permute-start = (bf16[584,512]{1,0:T(8,128)(2,1)S(1)}, bf16[584,512]{1,0:T(8,128)(2,1)S(1)}, u32[]{:S(2)}, u32[]{:S(2)}) collective-permute-start(bf16[584,512]{1,0:T(8,128)(2,1)S(1)} %get-tuple-element.33), channel_id=1, source_target_pairs={{0,8},{8,0},{1,9},{9,1},{2,10},{10,2},{3,11},{11,3},{4,12},{12,4},... | collective-permute-start | bytes 1794056 | tf_op jit(solution)/shard_map/ppermute | solution.py:384
  37.4 8.2 %collective-permute-start.1 = (bf16[136,512]{1,0:T(8,128)(2,1)S(1)}, bf16[136,512]{1,0:T(8,128)(2,1)S(1)}, u32[]{:S(2)}, u32[]{:S(2)}) collective-permute-start(bf16[136,512]{1,0:T(8,128)(2,1)S(1)} %get-tuple-element.38), channel_id=1, source_target_pairs={{0,4},{4,0},{1,5},{5,1},{2,6},{6,2},{3,7},{7,3},{8,12},{12,8},{9,1... | collective-permute-start | bytes 417800 | tf_op jit(solution)/shard_map/ppermute | solution.py:400
  57.8 1.9 %collective-permute-start.2 = (bf16[512,512]{1,0:T(8,128)(2,1)S(1)}, bf16[512,512]{1,0:T(8,128)(2,1)S(1)}, u32[]{:S(2)}, u32[]{:S(2)}) collective-permute-start(bf16[512,512]{1,0:T(8,128)(2,1)S(1)} %bitcast.5), channel_id=1, source_target_pairs={{0,8},{8,0},{1,9},{9,1},{2,10},{10,2},{3,11},{11,3},{4,12},{12,4},... | collective-permute-start | bytes 1572872 | tf_op jit(solution)/shard_map/ppermute | solution.py:406

commit v5 on v4

v5 whole, which is shorter than its diff:
```python
import functools
import math

import jax
import jax.numpy as jnp
from jax import lax
from jax.experimental import pallas as pl
from jax.experimental.pallas import tpu as pltpu
from jax.sharding import Mesh
from jax.sharding import PartitionSpec as P

BF16 = jnp.bfloat16
F32 = jnp.float32
VMEM, HBM = pltpu.VMEM, pltpu.HBM
shape = jax.ShapeDtypeStruct


def product(left, right, left_dim, right_dim):
    return lax.dot_general(
        left, right, (((left_dim,), (right_dim,)), ((), ())), preferred_element_type=F32
    )


def call(name, body, ins, outs, scratch=(), copies=0, flops=0, moved=0, aliases=None):
    scratch = list(scratch)
    if copies:
        scratch.append(pltpu.SemaphoreType.DMA((copies,)))
    run = pl.pallas_call(
        body,
        out_shape=tuple(
            HBM(out.shape, out.dtype) if memory is HBM else out for out, memory in outs
        ),
        in_specs=[pl.BlockSpec(memory_space=memory) for memory in ins],
        out_specs=tuple(pl.BlockSpec(memory_space=memory) for _, memory in outs),
        scratch_shapes=scratch,
        input_output_aliases=aliases or {},
        compiler_params=pltpu.CompilerParams(vmem_limit_bytes=48 * 1024 * 1024),
        cost_estimate=pl.CostEstimate(flops=flops, bytes_accessed=moved, transcendentals=0),
        name=name,
    )

    def held(*operands):
        return run(*(
            pltpu.with_memory_space_constraint(operand, HBM) if memory is HBM else operand
            for operand, memory in zip(operands, ins, strict=True)
        ))

    return held


def core_of(near):
    return lax.axis_index("node") // (2 * near) % 2


def wide_of(near):
    return lax.axis_index("node") // near % 2


def start_all(sems, *pairs):
    copies = [pltpu.make_async_copy(a, b, sems.at[at]) for at, (a, b) in enumerate(pairs)]
    for copy in copies:
        copy.start()
    return copies


def serve_kernel(serve_hbm, features_hbm, out_ref, serve_ref, features_ref, sems):
    copies = start_all(sems, (serve_hbm, serve_ref), (features_hbm, features_ref))
    own_rows = features_ref.shape[0]
    slots = serve_ref.shape[1]
    copies[0].wait()
    wanted = jnp.broadcast_to(serve_ref[...], (128, slots)).astype(F32).T
    row = lax.broadcasted_iota(jnp.int32, (slots, 128), 1).astype(F32)
    picks = jnp.concatenate(
        [
            jnp.where(row + float(at) == wanted, 1.0, 0.0).astype(BF16)
            for at in range(0, own_rows, 128)
        ],
        axis=1,
    )
    copies[1].wait()
    rows = product(picks, features_ref[...], 1, 0)
    out_ref[...] = rows.reshape(out_ref.shape).astype(BF16)


def find_live(neighbours_ref, count_ref):
    fanout, own_rows = neighbours_ref.shape
    position = lax.broadcasted_iota(jnp.int32, (fanout, own_rows), 0)
    return jnp.where(position < count_ref[...], neighbours_ref[...], -1)


def fill_counts(live, live_ref, table_ref, base):
    fanout, own_rows = live.shape
    for block in range(0, table_ref.shape[0], 256):
        table_rows = min(256, table_ref.shape[0] - block)
        step = min(64, table_rows)
        live_ref[...] = (live - (base + block)).astype(F32).astype(BF16)

        def fill(at, carry):
            start = pl.multiple_of(at * step, step)
            row = (lax.broadcasted_iota(jnp.int32, (step, own_rows), 0) + start).astype(F32).astype(BF16)
            total = jnp.zeros((step, own_rows), BF16)
            for k in range(fanout):
                named = jnp.broadcast_to(live_ref[k : k + 1, :], (step, own_rows))
                total = total + jnp.where(row == named, jnp.bfloat16(1), jnp.bfloat16(0))
            table_ref[pl.ds(pl.multiple_of(block + start, step), step), :] = total
            return carry

        lax.fori_loop(0, table_rows // step, fill, 0)


def own_kernel(
    neighbours_hbm, count_hbm, features_hbm, w_self_hbm, bias_hbm,
    own_sum_ref, fetch_counts_ref, slot_counts_ref, inverse_ref, pre_ref,
    neighbours_ref, count_ref, features_ref, w_self_ref, bias_ref, live_ref, table_ref, sems,
):
    copies = start_all(
        sems,
        (neighbours_hbm, neighbours_ref),
        (count_hbm, count_ref),
        (features_hbm, features_ref),
        (w_self_hbm, w_self_ref),
        (bias_hbm, bias_ref),
    )
    own_rows = features_ref.shape[0]
    for copy in copies[:2]:
        copy.wait()
    inverse_ref[...] = jnp.broadcast_to(1.0 / count_ref[...].astype(F32), (128, own_rows)).T
    live = find_live(neighbours_ref, count_ref)
    fill_counts(live, live_ref, slot_counts_ref, own_rows)
    fetch_counts_ref[...] = slot_counts_ref[...].T
    fill_counts(live, live_ref, table_ref, 0)
    for copy in copies[2:]:
        copy.wait()
    features = features_ref[...]
    own_sum_ref[...] = product(table_ref[...], features, 0, 0)
    pre_ref[...] = product(features, w_self_ref[...], 1, 0) + bias_ref[...]


def spread_wide(inverse, width):
    return jnp.concatenate([inverse] * (width // 128), axis=1)


def main_kernel(
    near, incoming_ref, own_sum_ref, fetch_counts_ref, slot_counts_ref, inverse_ref, pre_ref, w_neigh_ref,
    cotangent_hbm, features_hbm,
    send_ref, keep_ref, keep_rows_ref, bias_ref, pre_grad_ref, message_ref,
    cotangent_ref, left_ref, rows_ref, sems,
):
    own_rows, width = own_sum_ref.shape
    slots = rows_ref.shape[0]
    core = core_of(near)
    copies = start_all(sems, (cotangent_hbm, cotangent_ref), (features_hbm, left_ref.at[0]))
    incoming = incoming_ref[...].astype(F32).reshape(slots, width).astype(BF16)
    inverse = spread_wide(inverse_ref[...], width)
    summed = own_sum_ref[...] + product(fetch_counts_ref[...], incoming, 1, 0)
    aggregated = (summed * inverse).astype(BF16)
    left_ref[1] = aggregated
    pre = pre_ref[...] + product(aggregated, w_neigh_ref[...], 1, 0)
    sigmoid_pre = jax.nn.sigmoid(pre)
    slope = sigmoid_pre * (1.0 + pre * (1.0 - sigmoid_pre))
    slope_ref = keep_ref
    slope_ref[...] = slope
    copies[0].wait()
    pre_grad_ref[...] = (cotangent_ref[...].astype(F32) * slope_ref[...]).astype(BF16)
    pre_grad = pre_grad_ref[...]
    message = (product(pre_grad, w_neigh_ref[...], 1, 1) * inverse).astype(BF16)
    message_ref[...] = message
    rows_ref[...] = product(slot_counts_ref[...], message, 1, 0)
    copies[1].wait()
    keep_ref[...] = product(left_ref[core], pre_grad, 0, 0)
    send_ref[:own_rows, :] = product(left_ref[1 - core], pre_grad, 0, 0).astype(BF16)
    half = slots // 2
    blocks, length = keep_rows_ref.shape[0], keep_rows_ref.shape[1]
    for at in range(blocks):
        mine = pl.multiple_of((at * 2 + core) * length, length)
        other = pl.multiple_of((at * 2 + 1 - core) * length, length)
        keep_rows_ref[at] = rows_ref[pl.ds(mine, length), :].astype(BF16)
        send_ref[own_rows + at * length : own_rows + (at + 1) * length, :] = rows_ref[
            pl.ds(other, length), :
        ].astype(BF16)
    bias = jnp.sum(pre_grad.astype(F32), axis=0, keepdims=True).astype(BF16)
    bias_ref[...] = jnp.broadcast_to(bias, bias_ref.shape)
    send_ref[own_rows + half :, :] = jnp.broadcast_to(bias, bias_ref.shape)


def own_grad_kernel(
    dims, pre_grad_ref, message_ref, neighbours_hbm, count_hbm, serve_hbm, w_self_hbm, out_ref, order_ref,
    neighbours_ref, count_ref, serve_ref, w_self_ref, live_ref, table_ref, sems,
):
    copies = start_all(
        sems,
        (neighbours_hbm, neighbours_ref),
        (count_hbm, count_ref),
        (serve_hbm, serve_ref),
        (w_self_hbm, w_self_ref),
    )
    for copy in copies:
        copy.wait()
    fill_counts(find_live(neighbours_ref, count_ref), live_ref, table_ref, 0)
    out_ref[...] = product(pre_grad_ref[...], w_self_ref[...], 1, 1) + product(
        table_ref[...], message_ref[...], 1, 0
    )
    across, near, cap = dims
    slots = serve_ref.shape[1]
    to = lax.broadcasted_iota(jnp.int32, (slots, slots), 1)
    slot = to % cap
    core = (to // cap % 2 + core_of(near)) % 2
    n = to // (2 * cap) % near
    a = to // (2 * cap * near) % across
    wide = (to // (2 * cap * near * across) + wide_of(near)) % 2
    source = (((a * 2 + core) * 2 + wide) * near + n) * cap + slot
    at = lax.broadcasted_iota(jnp.int32, (slots, slots), 0)
    moves = (at == source).astype(F32).astype(BF16)
    serve = serve_ref[...]
    high = (serve // 32).astype(F32).astype(BF16)
    low = (serve % 32).astype(F32).astype(BF16)
    order_ref[...] = (
        product(high, moves, 1, 0) * 32.0 + product(low, moves, 1, 0)
    ).astype(jnp.int32)


def pack_kernel(dims, order, received_ref, keep_ref, keep_rows_ref, bias_ref, out_ref):
    across, near, cap = dims
    own_rows, width = keep_ref.shape
    peers, length = out_ref.shape[0], out_ref.shape[1]
    half = 2 * peers * cap
    share = own_rows // peers
    keep_rows = keep_rows_ref[...].astype(F32).reshape(half, width)
    other_rows = received_ref[own_rows : own_rows + half, :].astype(F32)
    bias = bias_ref[...].astype(F32) + received_ref[own_rows + half :, :].astype(F32)
    summed = keep_ref[...] + received_ref[:own_rows, :].astype(F32)
    for peer in range(peers):
        parts = [summed[peer * share : (peer + 1) * share]]
        for wide in range(2):
            place = order[peer]
            at = ((place // near * 2 + wide) * near + place % near) * cap
            parts += [keep_rows[at : at + cap], other_rows[at : at + cap]]
        parts.append(bias[: length - share - 4 * cap])
        out_ref[peer] = jnp.concatenate(parts, axis=0).astype(BF16)


def sum_kernel(dims, order, payload_ref, keep_ref, send_ref):
    cap = dims[2]
    peers, length, width = payload_ref.shape
    pair = 2 * cap
    count = peers * pair
    share = keep_ref.shape[0] - count - 8
    grads = jnp.zeros((share, width), F32)
    bias = jnp.zeros((8, width), F32)
    lower, upper = [None] * peers, [None] * peers
    for peer in range(peers):
        grads = grads + payload_ref[peer, :share, :].astype(F32)
        rest = payload_ref[peer, share:, :].astype(F32)
        lower[order[peer]] = rest[:pair]
        upper[order[peer]] = rest[pair : 2 * pair]
        bias = bias + jnp.broadcast_to(rest[2 * pair : 2 * pair + 1], bias.shape)
    grads = grads.astype(BF16)
    bias = bias.astype(BF16)
    first = wide_of(dims[1]) == 0
    lower, upper = jnp.concatenate(lower, axis=0), jnp.concatenate(upper, axis=0)
    for ref, rows in (
        (keep_ref, jnp.where(first, lower, upper)),
        (send_ref, jnp.where(first, upper, lower)),
    ):
        ref[:share, :] = grads
        ref[share : share + count, :] = rows.astype(BF16)
        ref[share + count :, :] = bias


def total_kernel(keep_ref, received_ref, after_ref, out_ref):
    peers, share, width = out_ref.shape
    total = (keep_ref[:share, :].astype(F32) + received_ref[:share, :].astype(F32)).astype(BF16)
    for peer in range(peers):
        out_ref[peer] = total


def send_half(matrix, source_ref, self_hbm, neigh_hbm, sem, rows, wait):
    source = source_ref.at[rows, :]
    for index, target in enumerate((self_hbm, neigh_hbm)):

        @pl.when(matrix == index)
        def _(target=target):
            copy = pltpu.make_async_copy(source, target.at[rows, :], sem)
            if wait:
                copy.wait()
            else:
                copy.start()


def tail_kernel(
    factor, share, near, order_ref, keep_ref, received_ref, base_ref, mine_ref,
    out_hbm, self_hbm, neigh_hbm, bias_hbm, wide_ref, out_ref, bias_ref, sems,
):
    own_rows, slots = base_ref.shape[0], order_ref.shape[1]
    half = slots // 2
    matrix = core_of(near)
    everything = pl.ds(0, own_rows)
    wide_ref[...] = mine_ref[...].astype(F32) * factor
    send_half(matrix, wide_ref, self_hbm, neigh_hbm, sems.at[0], everything, False)
    last = keep_ref.shape[0] - 8
    bias = keep_ref[last:, :].astype(F32) + received_ref[last:, :].astype(F32)
    bias_ref[...] = bias[:1] * factor
    copies = [pltpu.make_async_copy(bias_ref, bias_hbm, sems.at[1])]
    copies[0].start()
    rows = jnp.concatenate(
        [keep_ref[share : share + half, :], received_ref[share : share + half, :]], axis=0
    )
    row = lax.broadcasted_iota(jnp.int32, (own_rows, slots), 0)
    picks = (row == order_ref[...]).astype(F32).astype(BF16)
    out_ref[...] = base_ref[...] + product(picks, rows, 1, 0)
    copies.append(pltpu.make_async_copy(out_ref, out_hbm, sems.at[2]))
    copies[1].start()
    send_half(matrix, wide_ref, self_hbm, neigh_hbm, sems.at[0], everything, True)
    for copy in copies:
        copy.wait()


def other_kernel(factor, near, half_ref, self_in, neigh_in, self_hbm, neigh_hbm, wide_ref, sems):
    own_rows = half_ref.shape[0]
    pieces = 4
    length = own_rows // pieces
    matrix = 1 - core_of(near)
    spans = [pl.ds(at * length, length) for at in range(pieces)]
    for at, span in enumerate(spans):
        wide_ref[span, :] = half_ref[span, :].astype(F32) * factor
        send_half(matrix, wide_ref, self_hbm, neigh_hbm, sems.at[at], span, False)
    for at, span in enumerate(spans):
        send_half(matrix, wide_ref, self_hbm, neigh_hbm, sems.at[at], span, True)


def local(across, near, features, cotangent, w_self, w_neigh, bias, neighbours, neigh_count, serve_rows):
    own_rows, width = features.shape
    fanout = neighbours.shape[1]
    peers = across * near
    devices = 4 * peers
    slots = serve_rows.shape[1]
    cap = slots // devices
    half = slots // 2
    share = own_rows // peers
    length = -(-(share + 4 * cap + 1) // 8) * 8
    dims = (across, near, cap)
    chips = [place ^ (place >> 1) for place in reversed(range(peers))]
    cubes = [
        [(place // near * 4 + plane) * near + place % near for place in chips]
        for plane in range(4)
    ]
    swap_core = [(at, at ^ (2 * near)) for at in range(devices)]
    swap_wide = [(at, at ^ near) for at in range(devices)]
    factor = 1.0 / math.sqrt(own_rows * devices)
    work = 2 * own_rows * own_rows * width
    square16 = shape((own_rows, width), BF16)
    square32 = shape((own_rows, width), F32)

    (outgoing,) = call(
        "serve", serve_kernel, (HBM, HBM), ((shape((devices, cap, width), BF16), VMEM),),
        scratch=[VMEM((1, slots), jnp.int32), VMEM((own_rows, width), BF16)],
        copies=2, flops=work // 4, moved=1 << 20,
    )(serve_rows, features)
    incoming = lax.all_to_all(outgoing, "node", 0, 0, tiled=True)
    neighbours = neighbours.T
    neigh_count = neigh_count.reshape(1, own_rows)
    held = [VMEM((fanout, own_rows), jnp.int32), VMEM((1, own_rows), jnp.int32)]
    counted = [VMEM((fanout, own_rows), BF16), VMEM((own_rows, own_rows), BF16)]
    own_sum, fetch_counts, slot_counts, inverse, pre = call(
        "own_aggregate", own_kernel, (HBM,) * 5,
        (
            (square32, VMEM),
            (shape((own_rows, slots), BF16), VMEM),
            (shape((slots, own_rows), BF16), VMEM),
            (shape((own_rows, 128), F32), VMEM),
            (square32, VMEM),
        ),
        scratch=[
            *held,
            VMEM((own_rows, width), BF16),
            VMEM((width, width), BF16),
            VMEM((1, width), F32),
            *counted,
        ],
        copies=5, flops=20 * work, moved=4 << 20,
    )(neighbours, neigh_count, features, w_self, bias.reshape(1, width))
    send, keep, keep_rows, own_bias, pre_grad, message = call(
        "layer_grad", functools.partial(main_kernel, near), (VMEM,) * 7 + (HBM,) * 2,
        (
            (shape((own_rows + half + 8, width), BF16), VMEM),
            (square32, VMEM),
            (shape((across, 2 * near * cap, width), BF16), VMEM),
            (shape((8, width), BF16), VMEM),
            (square16, VMEM),
            (square16, VMEM),
        ),
        scratch=[
            VMEM((own_rows, width), BF16),
            VMEM((2, own_rows, width), BF16),
            VMEM((slots, width), F32),
        ],
        copies=2, flops=5 * work, moved=8 << 20,
    )(incoming, own_sum, fetch_counts, slot_counts, inverse, pre, w_neigh, cotangent, features)
    received = lax.ppermute(send, "node", swap_core)
    base, order = call(
        "own_grad", functools.partial(own_grad_kernel, dims), (VMEM,) * 2 + (HBM,) * 4,
        ((square32, VMEM), (shape((1, slots), jnp.int32), VMEM)),
        scratch=[*held, VMEM((1, slots), jnp.int32), VMEM((width, width), BF16), *counted],
        copies=4, flops=2 * work, moved=4 << 20,
    )(pre_grad, message, neighbours, neigh_count, serve_rows, w_self)
    (payload,) = call(
        "pack", functools.partial(pack_kernel, dims, chips), (VMEM,) * 4,
        ((shape((peers, length, width), BF16), VMEM),), flops=work // 4, moved=4 << 20,
    )(received, keep, keep_rows, own_bias)
    arrived = lax.all_to_all(payload, "node", 0, 0, axis_index_groups=cubes, tiled=True)
    pairs = shape((share + half + 8, width), BF16)
    keep_sum, send_sum = call(
        "sum_shares", functools.partial(sum_kernel, dims, chips), (VMEM,),
        ((pairs, VMEM), (pairs, VMEM)), flops=work // 8, moved=1 << 20,
    )(arrived)
    received_sum = lax.ppermute(send_sum, "node", swap_wide)
    (total,) = call(
        "total", total_kernel, (VMEM, VMEM, VMEM), ((shape((peers, share, width), BF16), VMEM),),
        flops=work // 8, moved=1 << 20,
    )(keep_sum, received_sum, base)
    mine = lax.all_to_all(total, "node", 0, 0, axis_index_groups=cubes, tiled=True).reshape(own_rows, width)
    other = lax.ppermute(mine, "node", swap_core)
    wide = VMEM((own_rows, width), F32)
    grad_features, self_part, neigh_part, bias_sum = call(
        "tail", functools.partial(tail_kernel, factor, share, near), (VMEM,) * 5,
        ((square32, HBM), (square32, HBM), (square32, HBM), (shape((1, width), F32), HBM)),
        scratch=[wide, wide, VMEM((1, width), F32)], copies=3, flops=work, moved=4 << 20,
    )(order, keep_sum, received_sum, base, mine)
    grad_self, grad_neigh = call(
        "other_half", functools.partial(other_kernel, factor, near), (VMEM, HBM, HBM),
        ((square32, HBM), (square32, HBM)),
        scratch=[wide], copies=4, flops=work // 2, moved=3 << 20, aliases={1: 0, 2: 1},
    )(other, self_part, neigh_part)
    return grad_features, grad_self, grad_neigh, bias_sum.reshape(width)


def solution(mesh):
    across, near = mesh.shape["group"] // 2, mesh.shape["member"] // 2
    line = Mesh(mesh.devices.reshape(-1), ("node",))
    rows = P("node", None)
    return jax.shard_map(
        functools.partial(local, across, near),
        mesh=line,
        in_specs=(rows, rows, P(), P(), P(), rows, P("node"), rows),
        out_specs=(rows, P(), P(), P()),
        check_vma=False,
    )
```

time: 61.1 us -> 59.7 us (0.977)
  blocking collectives: 27 us -> 25.7 us
  waiting for transfers between devices: 9.4 us -> 10.5 us
    all_to_all x1, waiting for transfers between devices: 2.78 us -> 4.49 us  [local(): incoming = lax.all_to_all(outgoing, 'node', 0, 0, tiled=True)]
    all_to_all x2, blocking collectives: 27 us -> 25.7 us  [the longest x1 14.3 us: local(): lax.all_to_all(payload, 'node', 0, 0, axis_index_groups=cubes, tiled=True)]
    pallas_call x9, Pallas kernels: 14.3 us -> 13.7 us  [held(): run(*(pltpu.with_memory_space_constraint(operand, HBM) if memory is HBM e...]
    ppermute x3, waiting for transfers between devices: 6.62 us -> 6.01 us  [the longest x1 3.9 us: local(): received_sum = lax.ppermute(send_sum, 'node', swap_wide)]
  transfers between devices with their start and end apart: 4 -> 4, of which waited for: 4 -> 4; matrix products, arithmetic and copies ran while one was open for 0% -> 0% of each run, Pallas kernels for 14% -> 13%
where the time goes in v5:
time: 59.7 us; the launch traced here: 59.4 us
  blocking collectives  25.7 us (43%)
  Pallas kernels  13.7 us (23%)
  waiting for transfers between devices  10.5 us (18%)
  starting transfers between devices  8.84 us (15%)
  between operations  0.7 us (1%)
    all_to_all x1, blocking collectives, local(): lax.all_to_all(payload, 'node', 0, 0, axis_index_groups=cubes, tiled=True)  14.3 us
    pallas_call x9, Pallas kernels, held(): run(*(pltpu.with_memory_space_constraint(operand, HBM) if memory is HBM e...  13.7 us
    all_to_all x1, blocking collectives, local(): lax.all_to_all(total, 'node', 0, 0, axis_index_groups=cubes, tiled=True)  11.4 us
    all_to_all x1, starting transfers between devices, local(): incoming = lax.all_to_all(outgoing, 'node', 0, 0, tiled=True)  7.3 us
    all_to_all x1, waiting for transfers between devices, local(): incoming = lax.all_to_all(outgoing, 'node', 0, 0, tiled=True)  4.49 us
    ppermute x1, waiting for transfers between devices, local(): received_sum = lax.ppermute(send_sum, 'node', swap_wide)  3.9 us
    ppermute x1, waiting for transfers between devices, local(): received = lax.ppermute(send, 'node', swap_core)  1.9 us
    ppermute x1, starting transfers between devices, local(): received_sum = lax.ppermute(send_sum, 'node', swap_wide)  1.35 us
  transfers between devices with their start and end apart: 4, of which 4 were waited for; matrix products, arithmetic and copies ran while one was open for 0% of the time, Pallas kernels for 13%

profile of v5, /device:TPU:0, one launch (start us, length us, event | category | flops | bytes accessed | tf_op | source)
XLA Modules:
  0.0 59.4 jit_solution(5264817821712402374)
XLA Ops:
  0.6 2.0 %serve.1 = bf16[32,4,512]{2,1,0:T(4,128)(2,1)} custom-call(s32[1,128]{1,0:T(1,128)} %serve_hbm.3, bf16[512,512]{1,0:T(8,128)(2,1)} %features_hbm.5), custom_call_target="tpu_custom_call" | custom-call | flops 67108864 | bytes 1048576 | tf_op jit(solution)/shard_map/serve/pallas_call | solution.py:43
  2.6 7.3 %all-to-all-start = ((bf16[32,4,512]{2,1,0:T(4,128)(2,1)}), bf16[32,4,512]{2,1,0:T(4,128)(2,1)S(1)}, u32[]{:S(2)}, u32[]{:S(2)}) async-start(bf16[32,4,512]{2,1,0:T(4,128)(2,1)} %serve.1), calls=%async_computation | async-start | bytes 262144 | tf_op jit(solution)/shard_map/all_to_all | solution.py:359
  9.9 0.0 copy-start
  9.9 3.2 %own_aggregate.1 = (f32[512,512]{1,0:T(8,128)S(1)}, bf16[512,128]{1,0:T(8,128)(2,1)S(1)}, bf16[128,512]{1,0:T(8,128)(2,1)S(1)}, f32[512,128]{1,0:T(8,128)S(1)}, f32[512,512]{1,0:T(8,128)S(1)}) custom-call(s32[16,512]{1,0:T(8,128)} %bitcast.7, s32[1,512]{1,0:T(1,128)} %bitcast.10, bf16[512,512]{1,0:T(8,128)(2,1)} %features_hbm.5, ...), custom_call_target="tpu_custom_call" | custom-call | flops 5368709120 | bytes 4194304 | tf_op jit(solution)/shard_map/own_aggregate/pallas_call | solution.py:43
  13.2 4.5 %all-to-all-done.incoming_ref = bf16[32,4,512]{2,1,0:T(4,128)(2,1)S(1)} async-done(((bf16[32,4,512]{2,1,0:T(4,128)(2,1)}), bf16[32,4,512]{2,1,0:T(4,128)(2,1)S(1)}, u32[]{:S(2)}, u32[]{:S(2)}) %all-to-all-start) | async-done | bytes 131104 | tf_op jit(solution)/shard_map/all_to_all | solution.py:359
  17.7 0.0 copy-done
  17.7 2.5 %layer_grad.1 = (bf16[584,512]{1,0:T(8,128)(2,1)S(1)}, f32[512,512]{1,0:T(8,128)S(1)}, bf16[2,32,512]{2,1,0:T(8,128)(2,1)S(1)}, bf16[8,512]{1,0:T(8,128)(2,1)S(1...) custom-call(bf16[32,4,512]{2,1,0:T(4,128)(2,1)S(1)} %all-to-all-done.incoming_ref, ...), custom_call_target="tpu_custom_call" | custom-call | flops 1342177280 | bytes 8388608 | tf_op jit(solution)/shard_map/layer_grad/pallas_call | solution.py:43
  20.2 0.2 collective-permute-start
  20.4 1.9 %collective-permute-done.received_ref = bf16[584,512]{1,0:T(8,128)(2,1)S(1)} collective-permute-done((bf16[584,512]{1,0:T(8,128)(2,1)S(1)}, bf16[584,512]{1,0:T(8,128)(2,1)S(1)}, u32[]{:S(2)}, u32[]{:S(2)}) %collective-permute-start) | collective-permute-done | bytes 598048 | tf_op jit(solution)/shard_map/ppermute | solution.py:399
  22.3 0.1 pack.1
  22.4 14.3 %all_to_all.15.payload_ref = bf16[8,88,512]{2,1,0:T(8,128)(2,1)S(1)} all-to-all(bf16[8,88,512]{2,1,0:T(8,128)(2,1)S(1)} %pack.1), channel_id=1, replica_groups={{16,17,19,18,2,3,1,0},{20,21,23,22,6,7,5,4},{24,25,27,26,10,11,9,8},{28..., dimensions={0} | all-to-all | bytes 1441792 | tf_op jit(solution)/shard_map/all_to_all | solution.py:410
  36.7 0.1 sum_shares.1
  36.8 1.4 %collective-permute-start.1 = (bf16[136,512]{1,0:T(8,128)(2,1)S(1)}, bf16[136,512]{1,0:T(8,128)(2,1)S(1)}, u32[]{:S(2)}, u32[]{:S(2)}) collective-permute-start(bf16[136,512]{1,0:T(8,128)(2,1)S(1)} %get-tuple-element.38), channel_id=1, source_target_pairs={{0,4},{1,5},{2,6},{3,7},{4,0},{5,1},{6,2},{7,3},{8,12},{9,13},{10,... | collective-permute-start | bytes 417800 | tf_op jit(solution)/shard_map/ppermute | solution.py:416
  38.2 3.0 %own_grad.1 = (f32[512,512]{1,0:T(8,128)S(1)}, s32[1,128]{1,0:T(1,128)S(1)}) custom-call(bf16[512,512]{1,0:T(8,128)(2,1)S(1)} %get-tuple-element.30.pre_grad_ref, bf16[512,512]{1,0:T(8,128)(2,1)S(1)} %get-tuple-element.31.message_ref, s32[16,512]{1,0:T(8,128)} %bitcast.8, s32[1,512]{1,0:T(1,128)} %bitcast.11, s32[1,128]{1,0:T(1,128)} %serve_hbm.3, ...), custom_call_target="tpu_custom_call" | custom-call | flops 536870912 | bytes 4194304 | tf_op jit(solution)/shard_map/own_grad/pallas_call | solution.py:43
  41.2 3.9 %collective-permute-done.1.received_ref = bf16[136,512]{1,0:T(8,128)(2,1)S(1)} collective-permute-done((bf16[136,512]{1,0:T(8,128)(2,1)S(1)}, bf16[136,512]{1,0:T(8,128)(2,1)S(1)}, u32[]{:S(2)}, u32[]{:S(2)}) %collective-permute-start.1) | collective-permute-done | bytes 139296 | tf_op jit(solution)/shard_map/ppermute | solution.py:416
  45.1 11.4 %all_to_all.16 = bf16[8,64,512]{2,1,0:T(8,128)(2,1)S(1)} all-to-all(bf16[8,64,512]{2,1,0:T(8,128)(2,1)S(1)} %total.1), channel_id=1, replica_groups={{16,17,19,18,2,3,1,0},{20,21,23,22,6,7,5,4},{24,25,27,26,10,11,9,8},{28..., dimensions={0} | all-to-all | bytes 1048576 | tf_op jit(solution)/shard_map/all_to_all | solution.py:421
  56.5 0.0 collective-permute-start.2
  56.5 1.7 %tail.1 = (f32[512,512]{1,0:T(8,128)}, f32[512,512]{1,0:T(8,128)}, f32[512,512]{1,0:T(8,128)}, f32[1,512]{1,0:T(1,128)}) custom-call(s32[1,128]{1,0:T(1,128)S(1)} %get-tuple-element.32.order_ref, bf16[136,512]{1,0:T(8,128)(2,1)S(1)} %get-tuple-element.37.keep_ref, bf16[136,512]{1,0:T(8,128)(2,1)S(1)} %collective-permute-done.1.received_ref, ...), custom_call_target="tpu_custom_call" | custom-call | flops 268435456 | bytes 4194304 | tf_op jit(solution)/shard_map/tail/pallas_call | solution.py:43
  58.2 0.2 collective-permute-done.2.half_ref
  58.4 1.0 %other_half.1 = (f32[512,512]{1,0:T(8,128)}, f32[512,512]{1,0:T(8,128)}) custom-call(bf16[512,512]{1,0:T(8,128)(2,1)S(1)} %collective-permute-done.2.half_ref, f32[512,512]{1,0:T(8,128)} %get-tuple-element.41.self_in, f32[512,512]{1,0:T(8,128)} %get-tuple-element.42.neigh_in), custom_call_target="tpu_custom_call", output_to_operand_aliasing={{0}: (1, {}), {1}: (2, {})} | custom-call | flops 134217728 | bytes 3145728 | tf_op jit(solution)/shard_map/other_half/pallas_call | solution.py:43
  (1 shorter events, 0.0 us)
Async XLA Ops:
  2.6 15.1 %all-to-all-start = ((bf16[32,4,512]{2,1,0:T(4,128)(2,1)}), bf16[32,4,512]{2,1,0:T(4,128)(2,1)S(1)}, u32[]{:S(2)}, u32[]{:S(2)}) async-start(bf16[32,4,512]{2,1,0:T(4,128)(2,1)} %serve.1), calls=%async_computation | async-start | bytes 262144 | tf_op jit(solution)/shard_map/all_to_all | solution.py:359
  9.9 7.7 %copy-start = (bf16[512,512]{1,0:T(8,128)(2,1)S(1)}, bf16[512,512]{1,0:T(8,128)(2,1)}, u32[]{:S(2)}) copy-start(bf16[512,512]{1,0:T(8,128)(2,1)} %w_neigh_ref.1) | copy-start | bytes 1572868
  20.2 2.1 %collective-permute-start = (bf16[584,512]{1,0:T(8,128)(2,1)S(1)}, bf16[584,512]{1,0:T(8,128)(2,1)S(1)}, u32[]{:S(2)}, u32[]{:S(2)}) collective-permute-start(bf16[584,512]{1,0:T(8,128)(2,1)S(1)} %get-tuple-element.33), channel_id=1, source_target_pairs={{0,8},{1,9},{2,10},{3,11},{4,12},{5,13},{6,14},{7,15},{8,0},{9,1},... | collective-permute-start | bytes 1794056 | tf_op jit(solution)/shard_map/ppermute | solution.py:399
  36.8 8.2 %collective-permute-start.1 = (bf16[136,512]{1,0:T(8,128)(2,1)S(1)}, bf16[136,512]{1,0:T(8,128)(2,1)S(1)}, u32[]{:S(2)}, u32[]{:S(2)}) collective-permute-start(bf16[136,512]{1,0:T(8,128)(2,1)S(1)} %get-tuple-element.38), channel_id=1, source_target_pairs={{0,4},{1,5},{2,6},{3,7},{4,0},{5,1},{6,2},{7,3},{8,12},{9,13},{10,... | collective-permute-start | bytes 417800 | tf_op jit(solution)/shard_map/ppermute | solution.py:416
  56.5 1.9 %collective-permute-start.2 = (bf16[512,512]{1,0:T(8,128)(2,1)S(1)}, bf16[512,512]{1,0:T(8,128)(2,1)S(1)}, u32[]{:S(2)}, u32[]{:S(2)}) collective-permute-start(bf16[512,512]{1,0:T(8,128)(2,1)S(1)} %bitcast.5), channel_id=1, source_target_pairs={{0,8},{1,9},{2,10},{3,11},{4,12},{5,13},{6,14},{7,15},{8,0},{9,1},... | collective-permute-start | bytes 1572872 | tf_op jit(solution)/shard_map/ppermute | solution.py:422

commit v6 on v5

--- a/solution.py
+++ b/solution.py
@@ -141,13 +141,13 @@
 
 
 def main_kernel(
-    near, incoming_ref, own_sum_ref, fetch_counts_ref, slot_counts_ref, inverse_ref, pre_ref, w_neigh_ref,
+    near, incoming_ref, own_sum_ref, fetch_counts_ref, inverse_ref, pre_ref, w_neigh_ref,
     cotangent_hbm, features_hbm,
-    send_ref, keep_ref, keep_rows_ref, bias_ref, pre_grad_ref, message_ref,
-    cotangent_ref, left_ref, rows_ref, sems,
+    send_ref, left_ref, pre_grad_ref,
+    cotangent_ref, slope_ref, sems,
 ):
     own_rows, width = own_sum_ref.shape
-    slots = rows_ref.shape[0]
+    slots = fetch_counts_ref.shape[1]
     core = core_of(near)
     copies = start_all(sems, (cotangent_hbm, cotangent_ref), (features_hbm, left_ref.at[0]))
     incoming = incoming_ref[...].astype(F32).reshape(slots, width).astype(BF16)
@@ -158,29 +158,38 @@
     pre = pre_ref[...] + product(aggregated, w_neigh_ref[...], 1, 0)
     sigmoid_pre = jax.nn.sigmoid(pre)
     slope = sigmoid_pre * (1.0 + pre * (1.0 - sigmoid_pre))
-    slope_ref = keep_ref
     slope_ref[...] = slope
     copies[0].wait()
     pre_grad_ref[...] = (cotangent_ref[...].astype(F32) * slope_ref[...]).astype(BF16)
     pre_grad = pre_grad_ref[...]
+    copies[1].wait()
+    send_ref[...] = product(left_ref[1 - core], pre_grad, 0, 0).astype(BF16)
+
+
+def keep_kernel(near, left_ref, pre_grad_ref, keep_ref):
+    keep_ref[...] = product(left_ref[core_of(near)], pre_grad_ref[...], 0, 0)
+
+
+def message_kernel(
+    dims, pre_grad_ref, w_neigh_ref, inverse_ref, slot_counts_ref, message_ref, send_ref, keep_ref, rows_ref
+):
+    own_rows, width = pre_grad_ref.shape
+    slots = rows_ref.shape[0]
+    _, near, cap = dims
+    core = core_of(near)
+    pre_grad = pre_grad_ref[...]
+    inverse = spread_wide(inverse_ref[...], width)
     message = (product(pre_grad, w_neigh_ref[...], 1, 1) * inverse).astype(BF16)
     message_ref[...] = message
     rows_ref[...] = product(slot_counts_ref[...], message, 1, 0)
-    copies[1].wait()
-    keep_ref[...] = product(left_ref[core], pre_grad, 0, 0)
-    send_ref[:own_rows, :] = product(left_ref[1 - core], pre_grad, 0, 0).astype(BF16)
     half = slots // 2
-    blocks, length = keep_rows_ref.shape[0], keep_rows_ref.shape[1]
-    for at in range(blocks):
-        mine = pl.multiple_of((at * 2 + core) * length, length)
-        other = pl.multiple_of((at * 2 + 1 - core) * length, length)
-        keep_rows_ref[at] = rows_ref[pl.ds(mine, length), :].astype(BF16)
-        send_ref[own_rows + at * length : own_rows + (at + 1) * length, :] = rows_ref[
-            pl.ds(other, length), :
-        ].astype(BF16)
+    length = 2 * near * cap
     bias = jnp.sum(pre_grad.astype(F32), axis=0, keepdims=True).astype(BF16)
-    bias_ref[...] = jnp.broadcast_to(bias, bias_ref.shape)
-    send_ref[own_rows + half :, :] = jnp.broadcast_to(bias, bias_ref.shape)
+    for index, ref in ((core, keep_ref), (1 - core, send_ref)):
+        for at in range(half // length):
+            start = pl.multiple_of((at * 2 + index) * length, length)
+            ref[at * length : (at + 1) * length, :] = rows_ref[pl.ds(start, length), :].astype(BF16)
+        ref[half:, :] = jnp.broadcast_to(bias, (8, width))
 
 
 def own_grad_kernel(
@@ -219,16 +228,16 @@
     ).astype(jnp.int32)
 
 
-def pack_kernel(dims, order, received_ref, keep_ref, keep_rows_ref, bias_ref, out_ref):
+def pack_kernel(dims, order, received_ref, keep_ref, received_rows_ref, keep_rows_ref, out_ref):
     across, near, cap = dims
     own_rows, width = keep_ref.shape
     peers, length = out_ref.shape[0], out_ref.shape[1]
     half = 2 * peers * cap
     share = own_rows // peers
-    keep_rows = keep_rows_ref[...].astype(F32).reshape(half, width)
-    other_rows = received_ref[own_rows : own_rows + half, :].astype(F32)
-    bias = bias_ref[...].astype(F32) + received_ref[own_rows + half :, :].astype(F32)
-    summed = keep_ref[...] + received_ref[:own_rows, :].astype(F32)
+    keep_rows = keep_rows_ref[...].astype(F32)
+    other_rows = received_rows_ref[...].astype(F32)
+    bias = keep_rows[half:] + other_rows[half:]
+    summed = keep_ref[...] + received_ref[...].astype(F32)
     for peer in range(peers):
         parts = [summed[peer * share : (peer + 1) * share]]
         for wide in range(2):
@@ -339,7 +348,7 @@
     share = own_rows // peers
     length = -(-(share + 4 * cap + 1) // 8) * 8
     dims = (across, near, cap)
-    chips = [place ^ (place >> 1) for place in reversed(range(peers))]
+    chips = list(reversed(range(peers)))
     cubes = [
         [(place // near * 4 + plane) * near + place % near for place in chips]
         for plane in range(4)
@@ -379,24 +388,24 @@
         ],
         copies=5, flops=20 * work, moved=4 << 20,
     )(neighbours, neigh_count, features, w_self, bias.reshape(1, width))
-    send, keep, keep_rows, own_bias, pre_grad, message = call(
-        "layer_grad", functools.partial(main_kernel, near), (VMEM,) * 7 + (HBM,) * 2,
-        (
-            (shape((own_rows + half + 8, width), BF16), VMEM),
-            (square32, VMEM),
-            (shape((across, 2 * near * cap, width), BF16), VMEM),
-            (shape((8, width), BF16), VMEM),
-            (square16, VMEM),
-            (square16, VMEM),
-        ),
-        scratch=[
-            VMEM((own_rows, width), BF16),
-            VMEM((2, own_rows, width), BF16),
-            VMEM((slots, width), F32),
-        ],
+    send, left, pre_grad = call(
+        "layer_grad", functools.partial(main_kernel, near), (VMEM,) * 6 + (HBM,) * 2,
+        ((square16, VMEM), (shape((2, own_rows, width), BF16), VMEM), (square16, VMEM)),
+        scratch=[VMEM((own_rows, width), BF16), VMEM((own_rows, width), F32)],
         copies=2, flops=5 * work, moved=8 << 20,
-    )(incoming, own_sum, fetch_counts, slot_counts, inverse, pre, w_neigh, cotangent, features)
+    )(incoming, own_sum, fetch_counts, inverse, pre, w_neigh, cotangent, features)
     received = lax.ppermute(send, "node", swap_core)
+    returns = shape((half + 8, width), BF16)
+    message, send_rows, keep_rows = call(
+        "messages", functools.partial(message_kernel, dims), (VMEM,) * 4,
+        ((square16, VMEM), (returns, VMEM), (returns, VMEM)),
+        scratch=[VMEM((slots, width), F32)], flops=2 * work, moved=4 << 20,
+    )(pre_grad, w_neigh, inverse, slot_counts)
+    received_rows = lax.ppermute(send_rows, "node", swap_core)
+    (keep,) = call(
+        "keep_grad", functools.partial(keep_kernel, near), (VMEM, VMEM), ((square32, VMEM),),
+        flops=work, moved=2 << 20,
+    )(left, pre_grad)
     base, order = call(
         "own_grad", functools.partial(own_grad_kernel, dims), (VMEM,) * 2 + (HBM,) * 4,
         ((square32, VMEM), (shape((1, slots), jnp.int32), VMEM)),
@@ -406,7 +415,7 @@
     (payload,) = call(
         "pack", functools.partial(pack_kernel, dims, chips), (VMEM,) * 4,
         ((shape((peers, length, width), BF16), VMEM),), flops=work // 4, moved=4 << 20,
-    )(received, keep, keep_rows, own_bias)
+    )(received, keep, received_rows, keep_rows)
     arrived = lax.all_to_all(payload, "node", 0, 0, axis_index_groups=cubes, tiled=True)
     pairs = shape((share + half + 8, width), BF16)
     keep_sum, send_sum = call(

time: 59.7 us -> 59 us (0.988)
  waiting for transfers between devices: 10.5 us -> 9.07 us
    ppermute x1, waiting for transfers between devices: 1.9 us -> 0.01 us  [local(): received = lax.ppermute(send, 'node', swap_core)]
    pallas_call x9 -> x11, Pallas kernels: 13.7 us -> 14 us  [held(): run(*(pltpu.with_memory_space_constraint(operand, HBM) if memory is HBM e...]
  transfers between devices with their start and end apart: 4 -> 5, of which waited for: 4 -> 4; matrix products, arithmetic and copies ran while one was open for 0% -> 0% of each run, Pallas kernels for 13% -> 15%
where the time goes in v6:
time: 59 us; the launch traced here: 58.7 us
  blocking collectives  25.5 us (43%)
  Pallas kernels  14 us (24%)
  starting transfers between devices  9.37 us (16%)
  waiting for transfers between devices  9.07 us (15%)
  between operations  0.71 us (1%)
    all_to_all x1, blocking collectives, local(): lax.all_to_all(payload, 'node', 0, 0, axis_index_groups=cubes, tiled=True)  14 us
    pallas_call x11, Pallas kernels, held(): run(*(pltpu.with_memory_space_constraint(operand, HBM) if memory is HBM e...  14 us
    all_to_all x1, blocking collectives, local(): lax.all_to_all(total, 'node', 0, 0, axis_index_groups=cubes, tiled=True)  11.5 us
    all_to_all x1, starting transfers between devices, local(): incoming = lax.all_to_all(outgoing, 'node', 0, 0, tiled=True)  7.3 us
    all_to_all x1, waiting for transfers between devices, local(): incoming = lax.all_to_all(outgoing, 'node', 0, 0, tiled=True)  4.49 us
    ppermute x1, waiting for transfers between devices, local(): received_sum = lax.ppermute(send_sum, 'node', swap_wide)  3.94 us
    ppermute x1, starting transfers between devices, local(): received_sum = lax.ppermute(send_sum, 'node', swap_wide)  1.42 us
  transfers between devices with their start and end apart: 5, of which 4 were waited for; matrix products, arithmetic and copies ran while one was open for 0% of the time, Pallas kernels for 15%

profile of v6, /device:TPU:0, one launch (start us, length us, event | category | flops | bytes accessed | tf_op | source)
XLA Modules:
  0.0 58.7 jit_solution(16631934759917236546)
XLA Ops:
  0.6 2.0 %serve.1 = bf16[32,4,512]{2,1,0:T(4,128)(2,1)} custom-call(s32[1,128]{1,0:T(1,128)} %serve_hbm.3, bf16[512,512]{1,0:T(8,128)(2,1)} %features_hbm.5), custom_call_target="tpu_custom_call" | custom-call | flops 67108864 | bytes 1048576 | tf_op jit(solution)/shard_map/serve/pallas_call | solution.py:43
  2.6 7.3 %all-to-all-start = ((bf16[32,4,512]{2,1,0:T(4,128)(2,1)}), bf16[32,4,512]{2,1,0:T(4,128)(2,1)S(1)}, u32[]{:S(2)}, u32[]{:S(2)}) async-start(bf16[32,4,512]{2,1,0:T(4,128)(2,1)} %serve.1), calls=%async_computation | async-start | bytes 262144 | tf_op jit(solution)/shard_map/all_to_all | solution.py:368
  9.9 0.0 copy-start
  9.9 3.2 %own_aggregate.1 = (f32[512,512]{1,0:T(8,128)S(1)}, bf16[512,128]{1,0:T(8,128)(2,1)S(1)}, bf16[128,512]{1,0:T(8,128)(2,1)S(1)}, f32[512,128]{1,0:T(8,128)S(1)}, f32[512,512]{1,0:T(8,128)S(1)}) custom-call(s32[16,512]{1,0:T(8,128)} %bitcast.7, s32[1,512]{1,0:T(1,128)} %bitcast.10, bf16[512,512]{1,0:T(8,128)(2,1)} %features_hbm.5, ...), custom_call_target="tpu_custom_call" | custom-call | flops 5368709120 | bytes 4194304 | tf_op jit(solution)/shard_map/own_aggregate/pallas_call | solution.py:43
  13.2 4.5 %all-to-all-done.incoming_ref = bf16[32,4,512]{2,1,0:T(4,128)(2,1)S(1)} async-done(((bf16[32,4,512]{2,1,0:T(4,128)(2,1)}), bf16[32,4,512]{2,1,0:T(4,128)(2,1)S(1)}, u32[]{:S(2)}, u32[]{:S(2)}) %all-to-all-start) | async-done | bytes 131104 | tf_op jit(solution)/shard_map/all_to_all | solution.py:368
  17.7 0.0 copy-done
  17.7 1.7 %layer_grad.1 = (bf16[512,512]{1,0:T(8,128)(2,1)S(1)}, bf16[2,512,512]{2,1,0:T(8,128)(2,1)S(1)}, bf16[512,512]{1,0:T(8,128)(2,1)S(1)}) custom-call(bf16[32,4,512]{2,1,0:T(4,128)(2,1)S(1)} %all-to-all-done.incoming_ref, f32[512,512]{1,0:T(8,128)S(1)} %get-tuple-element.25.own_sum_ref, bf16[512,128]{1,0:T(8,128)(2,1)S(1)} %get-tuple-element.26.fetch_counts_ref, ...), custom_call_target="tpu_custom_call" | custom-call | flops 1342177280 | bytes 8388608 | tf_op jit(solution)/shard_map/layer_grad/pallas_call | solution.py:43
  19.4 0.2 collective-permute-start
  19.6 0.7 %messages.1 = (bf16[512,512]{1,0:T(8,128)(2,1)S(1)}, bf16[72,512]{1,0:T(8,128)(2,1)S(1)}, bf16[72,512]{1,0:T(8,128)(2,1)S(1)}) custom-call(bf16[512,512]{1,0:T(8,128)(2,1)S(1)} %get-tuple-element.29.pre_grad_ref, bf16[512,512]{1,0:T(8,128)(2,1)S(1)} %copy-done, f32[512,128]{1,0:T(8,128)S(1)} %get-tuple-element.27.inverse_ref, ...), custom_call_target="tpu_custom_call" | custom-call | flops 536870912 | bytes 4194304 | tf_op jit(solution)/shard_map/messages/pallas_call | solution.py:43
  20.3 0.5 collective-permute-start.1
  20.7 0.5 keep_grad.1.keep_ref
  21.2 0.4 collective-permute-done.1.received_rows_ref
  21.6 0.0 collective-permute-done.received_ref
  21.6 0.1 pack.1
  21.8 14.0 %all_to_all.15.payload_ref = bf16[8,88,512]{2,1,0:T(8,128)(2,1)S(1)} all-to-all(bf16[8,88,512]{2,1,0:T(8,128)(2,1)S(1)} %pack.1), channel_id=1, replica_groups={{19,18,17,16,3,2,1,0},{23,22,21,20,7,6,5,4},{27,26,25,24,11,10,9,8},{31..., dimensions={0} | all-to-all | bytes 1441792 | tf_op jit(solution)/shard_map/all_to_all | solution.py:419
  35.8 0.1 sum_shares.1
  35.9 1.4 %collective-permute-start.2 = (bf16[136,512]{1,0:T(8,128)(2,1)S(1)}, bf16[136,512]{1,0:T(8,128)(2,1)S(1)}, u32[]{:S(2)}, u32[]{:S(2)}) collective-permute-start(bf16[136,512]{1,0:T(8,128)(2,1)S(1)} %get-tuple-element.38), channel_id=1, source_target_pairs={{0,4},{1,5},{2,6},{3,7},{4,0},{5,1},{6,2},{7,3},{8,12},{9,13},{10,... | collective-permute-start | bytes 417800 | tf_op jit(solution)/shard_map/ppermute | solution.py:425
  37.3 3.0 %own_grad.1 = (f32[512,512]{1,0:T(8,128)S(1)}, s32[1,128]{1,0:T(1,128)S(1)}) custom-call(bf16[512,512]{1,0:T(8,128)(2,1)S(1)} %get-tuple-element.29.pre_grad_ref, bf16[512,512]{1,0:T(8,128)(2,1)S(1)} %get-tuple-element.31.message_ref, s32[16,512]{1,0:T(8,128)} %bitcast.8, s32[1,512]{1,0:T(1,128)} %bitcast.11, s32[1,128]{1,0:T(1,128)} %serve_hbm.3, ...), custom_call_target="tpu_custom_call" | custom-call | flops 536870912 | bytes 4194304 | tf_op jit(solution)/shard_map/own_grad/pallas_call | solution.py:43
  40.3 3.9 %collective-permute-done.2.received_ref = bf16[136,512]{1,0:T(8,128)(2,1)S(1)} collective-permute-done((bf16[136,512]{1,0:T(8,128)(2,1)S(1)}, bf16[136,512]{1,0:T(8,128)(2,1)S(1)}, u32[]{:S(2)}, u32[]{:S(2)}) %collective-permute-start.2) | collective-permute-done | bytes 139296 | tf_op jit(solution)/shard_map/ppermute | solution.py:425
  44.3 11.5 %all_to_all.16 = bf16[8,64,512]{2,1,0:T(8,128)(2,1)S(1)} all-to-all(bf16[8,64,512]{2,1,0:T(8,128)(2,1)S(1)} %total.1), channel_id=1, replica_groups={{19,18,17,16,3,2,1,0},{23,22,21,20,7,6,5,4},{27,26,25,24,11,10,9,8},{31..., dimensions={0} | all-to-all | bytes 1048576 | tf_op jit(solution)/shard_map/all_to_all | solution.py:430
  55.8 0.0 collective-permute-start.3
  55.8 1.7 %tail.1 = (f32[512,512]{1,0:T(8,128)}, f32[512,512]{1,0:T(8,128)}, f32[512,512]{1,0:T(8,128)}, f32[1,512]{1,0:T(1,128)}) custom-call(s32[1,128]{1,0:T(1,128)S(1)} %get-tuple-element.32.order_ref, bf16[136,512]{1,0:T(8,128)(2,1)S(1)} %get-tuple-element.37.keep_ref, bf16[136,512]{1,0:T(8,128)(2,1)S(1)} %collective-permute-done.2.received_ref, ...), custom_call_target="tpu_custom_call" | custom-call | flops 268435456 | bytes 4194304 | tf_op jit(solution)/shard_map/tail/pallas_call | solution.py:43
  57.5 0.2 collective-permute-done.3.half_ref
  57.7 1.0 %other_half.1 = (f32[512,512]{1,0:T(8,128)}, f32[512,512]{1,0:T(8,128)}) custom-call(bf16[512,512]{1,0:T(8,128)(2,1)S(1)} %collective-permute-done.3.half_ref, f32[512,512]{1,0:T(8,128)} %get-tuple-element.41.self_in, f32[512,512]{1,0:T(8,128)} %get-tuple-element.42.neigh_in), custom_call_target="tpu_custom_call", output_to_operand_aliasing={{0}: (1, {}), {1}: (2, {})} | custom-call | flops 134217728 | bytes 3145728 | tf_op jit(solution)/shard_map/other_half/pallas_call | solution.py:43
  (1 shorter events, 0.0 us)
Async XLA Ops:
  2.6 15.1 %all-to-all-start = ((bf16[32,4,512]{2,1,0:T(4,128)(2,1)}), bf16[32,4,512]{2,1,0:T(4,128)(2,1)S(1)}, u32[]{:S(2)}, u32[]{:S(2)}) async-start(bf16[32,4,512]{2,1,0:T(4,128)(2,1)} %serve.1), calls=%async_computation | async-start | bytes 262144 | tf_op jit(solution)/shard_map/all_to_all | solution.py:368
  9.9 7.7 %copy-start = (bf16[512,512]{1,0:T(8,128)(2,1)S(1)}, bf16[512,512]{1,0:T(8,128)(2,1)}, u32[]{:S(2)}) copy-start(bf16[512,512]{1,0:T(8,128)(2,1)} %w_neigh_ref.3) | copy-start | bytes 1572868
  19.4 2.2 %collective-permute-start = (bf16[512,512]{1,0:T(8,128)(2,1)S(1)}, bf16[512,512]{1,0:T(8,128)(2,1)S(1)}, u32[]{:S(2)}, u32[]{:S(2)}) collective-permute-start(bf16[512,512]{1,0:T(8,128)(2,1)S(1)} %get-tuple-element.33), channel_id=1, source_target_pairs={{0,8},{1,9},{2,10},{3,11},{4,12},{5,13},{6,14},{7,15},{8,0},{9,1},... | collective-permute-start | bytes 1572872 | tf_op jit(solution)/shard_map/ppermute | solution.py:397
  20.3 1.4 %collective-permute-start.1 = (bf16[72,512]{1,0:T(8,128)(2,1)S(1)}, bf16[72,512]{1,0:T(8,128)(2,1)S(1)}, u32[]{:S(2)}, u32[]{:S(2)}) collective-permute-start(bf16[72,512]{1,0:T(8,128)(2,1)S(1)} %get-tuple-element.35), channel_id=1, source_target_pairs={{0,8},{1,9},{2,10},{3,11},{4,12},{5,13},{6,14},{7,15},{8,0},{9,1},... | collective-permute-start | bytes 221192 | tf_op jit(solution)/shard_map/ppermute | solution.py:404
  35.9 8.3 %collective-permute-start.2 = (bf16[136,512]{1,0:T(8,128)(2,1)S(1)}, bf16[136,512]{1,0:T(8,128)(2,1)S(1)}, u32[]{:S(2)}, u32[]{:S(2)}) collective-permute-start(bf16[136,512]{1,0:T(8,128)(2,1)S(1)} %get-tuple-element.38), channel_id=1, source_target_pairs={{0,4},{1,5},{2,6},{3,7},{4,0},{5,1},{6,2},{7,3},{8,12},{9,13},{10,... | collective-permute-start | bytes 417800 | tf_op jit(solution)/shard_map/ppermute | solution.py:425
  55.8 1.9 %collective-permute-start.3 = (bf16[512,512]{1,0:T(8,128)(2,1)S(1)}, bf16[512,512]{1,0:T(8,128)(2,1)S(1)}, u32[]{:S(2)}, u32[]{:S(2)}) collective-permute-start(bf16[512,512]{1,0:T(8,128)(2,1)S(1)} %bitcast.5), channel_id=1, source_target_pairs={{0,8},{1,9},{2,10},{3,11},{4,12},{5,13},{6,14},{7,15},{8,0},{9,1},... | collective-permute-start | bytes 1572872 | tf_op jit(solution)/shard_map/ppermute | solution.py:431

commit v7 on v6

--- a/solution.py
+++ b/solution.py
@@ -136,6 +136,17 @@
     pre_ref[...] = product(features, w_self_ref[...], 1, 0) + bias_ref[...]
 
 
+def split_in_two(bias):
+    high = bias.astype(BF16).astype(F32)
+    row = lax.broadcasted_iota(jnp.int32, (8, bias.shape[1]), 0)
+    return jnp.where(row == 0, high, jnp.where(row == 1, bias - high, 0.0)).astype(BF16)
+
+
+def join_two(rows):
+    rows = rows.astype(F32)
+    return rows[0:1] + rows[1:2]
+
+
 def spread_wide(inverse, width):
     return jnp.concatenate([inverse] * (width // 128), axis=1)
 
@@ -149,7 +160,13 @@
     own_rows, width = own_sum_ref.shape
     slots = fetch_counts_ref.shape[1]
     core = core_of(near)
-    copies = start_all(sems, (cotangent_hbm, cotangent_ref), (features_hbm, left_ref.at[0]))
+    parts = 2
+    spans = [pl.ds(at * own_rows // parts, own_rows // parts) for at in range(parts)]
+    copies = start_all(
+        sems,
+        *((cotangent_hbm.at[span, :], cotangent_ref.at[span, :]) for span in spans),
+        (features_hbm, left_ref.at[0]),
+    )
     incoming = incoming_ref[...].astype(F32).reshape(slots, width).astype(BF16)
     inverse = spread_wide(inverse_ref[...], width)
     summed = own_sum_ref[...] + product(fetch_counts_ref[...], incoming, 1, 0)
@@ -159,10 +176,13 @@
     sigmoid_pre = jax.nn.sigmoid(pre)
     slope = sigmoid_pre * (1.0 + pre * (1.0 - sigmoid_pre))
     slope_ref[...] = slope
-    copies[0].wait()
-    pre_grad_ref[...] = (cotangent_ref[...].astype(F32) * slope_ref[...]).astype(BF16)
+    for span, copy in zip(spans, copies[:parts], strict=True):
+        copy.wait()
+        pre_grad_ref[span, :] = (
+            cotangent_ref[span, :].astype(F32) * slope_ref[span, :]
+        ).astype(BF16)
     pre_grad = pre_grad_ref[...]
-    copies[1].wait()
+    copies[parts].wait()
     send_ref[...] = product(left_ref[1 - core], pre_grad, 0, 0).astype(BF16)
 
 
@@ -184,12 +204,12 @@
     rows_ref[...] = product(slot_counts_ref[...], message, 1, 0)
     half = slots // 2
     length = 2 * near * cap
-    bias = jnp.sum(pre_grad.astype(F32), axis=0, keepdims=True).astype(BF16)
+    bias = split_in_two(jnp.sum(pre_grad.astype(F32), axis=0, keepdims=True))
     for index, ref in ((core, keep_ref), (1 - core, send_ref)):
         for at in range(half // length):
             start = pl.multiple_of((at * 2 + index) * length, length)
             ref[at * length : (at + 1) * length, :] = rows_ref[pl.ds(start, length), :].astype(BF16)
-        ref[half:, :] = jnp.broadcast_to(bias, (8, width))
+        ref[half:, :] = bias
 
 
 def own_grad_kernel(
@@ -228,7 +248,7 @@
     ).astype(jnp.int32)
 
 
-def pack_kernel(dims, order, received_ref, keep_ref, received_rows_ref, keep_rows_ref, out_ref):
+def pack_kernel(dims, order, gather_order, received_ref, keep_ref, received_rows_ref, keep_rows_ref, out_ref):
     across, near, cap = dims
     own_rows, width = keep_ref.shape
     peers, length = out_ref.shape[0], out_ref.shape[1]
@@ -236,10 +256,11 @@
     share = own_rows // peers
     keep_rows = keep_rows_ref[...].astype(F32)
     other_rows = received_rows_ref[...].astype(F32)
-    bias = keep_rows[half:] + other_rows[half:]
+    bias = split_in_two(join_two(keep_rows[half:]) + join_two(other_rows[half:])).astype(F32)
     summed = keep_ref[...] + received_ref[...].astype(F32)
     for peer in range(peers):
-        parts = [summed[peer * share : (peer + 1) * share]]
+        start = gather_order.index(order[peer]) * share
+        parts = [summed[start : start + share]]
         for wide in range(2):
             place = order[peer]
             at = ((place // near * 2 + wide) * near + place % near) * cap
@@ -255,16 +276,16 @@
     count = peers * pair
     share = keep_ref.shape[0] - count - 8
     grads = jnp.zeros((share, width), F32)
-    bias = jnp.zeros((8, width), F32)
+    bias = jnp.zeros((1, width), F32)
     lower, upper = [None] * peers, [None] * peers
     for peer in range(peers):
         grads = grads + payload_ref[peer, :share, :].astype(F32)
         rest = payload_ref[peer, share:, :].astype(F32)
         lower[order[peer]] = rest[:pair]
         upper[order[peer]] = rest[pair : 2 * pair]
-        bias = bias + jnp.broadcast_to(rest[2 * pair : 2 * pair + 1], bias.shape)
+        bias = bias + join_two(rest[2 * pair :])
     grads = grads.astype(BF16)
-    bias = bias.astype(BF16)
+    bias = split_in_two(bias)
     first = wide_of(dims[1]) == 0
     lower, upper = jnp.concatenate(lower, axis=0), jnp.concatenate(upper, axis=0)
     for ref, rows in (
@@ -307,8 +328,7 @@
     wide_ref[...] = mine_ref[...].astype(F32) * factor
     send_half(matrix, wide_ref, self_hbm, neigh_hbm, sems.at[0], everything, False)
     last = keep_ref.shape[0] - 8
-    bias = keep_ref[last:, :].astype(F32) + received_ref[last:, :].astype(F32)
-    bias_ref[...] = bias[:1] * factor
+    bias_ref[...] = (join_two(keep_ref[last:, :]) + join_two(received_ref[last:, :])) * factor
     copies = [pltpu.make_async_copy(bias_ref, bias_hbm, sems.at[1])]
     copies[0].start()
     rows = jnp.concatenate(
@@ -348,11 +368,12 @@
     share = own_rows // peers
     length = -(-(share + 4 * cap + 1) // 8) * 8
     dims = (across, near, cap)
-    chips = list(reversed(range(peers)))
-    cubes = [
-        [(place // near * 4 + plane) * near + place % near for place in chips]
-        for plane in range(4)
-    ]
+    chips = [place ^ (place >> 1) for place in reversed(range(peers))]
+    gather_chips = list(reversed(range(peers)))
+    cubes, gather_cubes = (
+        [[(place // near * 4 + plane) * near + place % near for place in listed] for plane in range(4)]
+        for listed in (chips, gather_chips)
+    )
     swap_core = [(at, at ^ (2 * near)) for at in range(devices)]
     swap_wide = [(at, at ^ near) for at in range(devices)]
     factor = 1.0 / math.sqrt(own_rows * devices)
@@ -392,7 +413,7 @@
         "layer_grad", functools.partial(main_kernel, near), (VMEM,) * 6 + (HBM,) * 2,
         ((square16, VMEM), (shape((2, own_rows, width), BF16), VMEM), (square16, VMEM)),
         scratch=[VMEM((own_rows, width), BF16), VMEM((own_rows, width), F32)],
-        copies=2, flops=5 * work, moved=8 << 20,
+        copies=3, flops=5 * work, moved=8 << 20,
     )(incoming, own_sum, fetch_counts, inverse, pre, w_neigh, cotangent, features)
     received = lax.ppermute(send, "node", swap_core)
     returns = shape((half + 8, width), BF16)
@@ -413,7 +434,7 @@
         copies=4, flops=2 * work, moved=4 << 20,
     )(pre_grad, message, neighbours, neigh_count, serve_rows, w_self)
     (payload,) = call(
-        "pack", functools.partial(pack_kernel, dims, chips), (VMEM,) * 4,
+        "pack", functools.partial(pack_kernel, dims, chips, gather_chips), (VMEM,) * 4,
         ((shape((peers, length, width), BF16), VMEM),), flops=work // 4, moved=4 << 20,
     )(received, keep, received_rows, keep_rows)
     arrived = lax.all_to_all(payload, "node", 0, 0, axis_index_groups=cubes, tiled=True)
@@ -427,7 +448,7 @@
         "total", total_kernel, (VMEM, VMEM, VMEM), ((shape((peers, share, width), BF16), VMEM),),
         flops=work // 8, moved=1 << 20,
     )(keep_sum, received_sum, base)
-    mine = lax.all_to_all(total, "node", 0, 0, axis_index_groups=cubes, tiled=True).reshape(own_rows, width)
+    mine = lax.all_to_all(total, "node", 0, 0, axis_index_groups=gather_cubes, tiled=True).reshape(own_rows, width)
     other = lax.ppermute(mine, "node", swap_core)
     wide = VMEM((own_rows, width), F32)
     grad_features, self_part, neigh_part, bias_sum = call(

time: 59 us -> 58.6 us (level)
    all_to_all x1, blocking collectives: 11.5 us -> 10.6 us  [local(): lax.all_to_all(total, 'node', 0, 0, axis_index_groups=gather_cubes, tiled...]
where the time goes in v7:
time: 58.6 us; the launch traced here: 58.3 us
  blocking collectives  25.1 us (43%)
  Pallas kernels  14 us (24%)
  starting transfers between devices  9.3 us (16%)
  waiting for transfers between devices  9.14 us (16%)
  between operations  0.71 us (1%)
    all_to_all x1, blocking collectives, local(): lax.all_to_all(payload, 'node', 0, 0, axis_index_groups=cubes, tiled=True)  14.5 us
    pallas_call x11, Pallas kernels, held(): run(*(pltpu.with_memory_space_constraint(operand, HBM) if memory is HBM e...  14 us
    all_to_all x1, blocking collectives, local(): lax.all_to_all(total, 'node', 0, 0, axis_index_groups=gather_cubes, tiled...  10.6 us
    all_to_all x1, starting transfers between devices, local(): incoming = lax.all_to_all(outgoing, 'node', 0, 0, tiled=True)  7.3 us
    all_to_all x1, waiting for transfers between devices, local(): incoming = lax.all_to_all(outgoing, 'node', 0, 0, tiled=True)  4.49 us
    ppermute x1, waiting for transfers between devices, local(): received_sum = lax.ppermute(send_sum, 'node', swap_wide)  4.01 us
    ppermute x1, starting transfers between devices, local(): received_sum = lax.ppermute(send_sum, 'node', swap_wide)  1.35 us
  transfers between devices with their start and end apart: 5, of which 4 were waited for; matrix products, arithmetic and copies ran while one was open for 0% of the time, Pallas kernels for 15%

profile of v7, /device:TPU:0, one launch (start us, length us, event | category | flops | bytes accessed | tf_op | source)
XLA Modules:
  0.0 58.3 jit_solution(1266948165484328957)
XLA Ops:
  0.6 2.0 %serve.1 = bf16[32,4,512]{2,1,0:T(4,128)(2,1)} custom-call(s32[1,128]{1,0:T(1,128)} %serve_hbm.3, bf16[512,512]{1,0:T(8,128)(2,1)} %features_hbm.5), custom_call_target="tpu_custom_call" | custom-call | flops 67108864 | bytes 1048576 | tf_op jit(solution)/shard_map/serve/pallas_call | solution.py:43
  2.6 7.3 %all-to-all-start = ((bf16[32,4,512]{2,1,0:T(4,128)(2,1)}), bf16[32,4,512]{2,1,0:T(4,128)(2,1)S(1)}, u32[]{:S(2)}, u32[]{:S(2)}) async-start(bf16[32,4,512]{2,1,0:T(4,128)(2,1)} %serve.1), calls=%async_computation | async-start | bytes 262144 | tf_op jit(solution)/shard_map/all_to_all | solution.py:389
  9.9 0.0 copy-start
  9.9 3.2 %own_aggregate.1 = (f32[512,512]{1,0:T(8,128)S(1)}, bf16[512,128]{1,0:T(8,128)(2,1)S(1)}, bf16[128,512]{1,0:T(8,128)(2,1)S(1)}, f32[512,128]{1,0:T(8,128)S(1)}, f32[512,512]{1,0:T(8,128)S(1)}) custom-call(s32[16,512]{1,0:T(8,128)} %bitcast.7, s32[1,512]{1,0:T(1,128)} %bitcast.10, bf16[512,512]{1,0:T(8,128)(2,1)} %features_hbm.5, ...), custom_call_target="tpu_custom_call" | custom-call | flops 5368709120 | bytes 4194304 | tf_op jit(solution)/shard_map/own_aggregate/pallas_call | solution.py:43
  13.2 4.5 %all-to-all-done.incoming_ref = bf16[32,4,512]{2,1,0:T(4,128)(2,1)S(1)} async-done(((bf16[32,4,512]{2,1,0:T(4,128)(2,1)}), bf16[32,4,512]{2,1,0:T(4,128)(2,1)S(1)}, u32[]{:S(2)}, u32[]{:S(2)}) %all-to-all-start) | async-done | bytes 131104 | tf_op jit(solution)/shard_map/all_to_all | solution.py:389
  17.7 0.0 copy-done
  17.7 1.7 %layer_grad.1 = (bf16[512,512]{1,0:T(8,128)(2,1)S(1)}, bf16[2,512,512]{2,1,0:T(8,128)(2,1)S(1)}, bf16[512,512]{1,0:T(8,128)(2,1)S(1)}) custom-call(bf16[32,4,512]{2,1,0:T(4,128)(2,1)S(1)} %all-to-all-done.incoming_ref, f32[512,512]{1,0:T(8,128)S(1)} %get-tuple-element.25.own_sum_ref, bf16[512,128]{1,0:T(8,128)(2,1)S(1)} %get-tuple-element.26.fetch_counts_ref, ...), custom_call_target="tpu_custom_call" | custom-call | flops 1342177280 | bytes 8388608 | tf_op jit(solution)/shard_map/layer_grad/pallas_call | solution.py:43
  19.4 0.2 collective-permute-start
  19.6 0.7 %messages.1 = (bf16[512,512]{1,0:T(8,128)(2,1)S(1)}, bf16[72,512]{1,0:T(8,128)(2,1)S(1)}, bf16[72,512]{1,0:T(8,128)(2,1)S(1)}) custom-call(bf16[512,512]{1,0:T(8,128)(2,1)S(1)} %get-tuple-element.29.pre_grad_ref, bf16[512,512]{1,0:T(8,128)(2,1)S(1)} %copy-done, f32[512,128]{1,0:T(8,128)S(1)} %get-tuple-element.27.inverse_ref, ...), custom_call_target="tpu_custom_call" | custom-call | flops 536870912 | bytes 4194304 | tf_op jit(solution)/shard_map/messages/pallas_call | solution.py:43
  20.2 0.5 collective-permute-start.1
  20.7 0.5 keep_grad.1.keep_ref
  21.2 0.4 collective-permute-done.1.received_rows_ref
  21.6 0.0 collective-permute-done.received_ref
  21.6 0.1 pack.1
  21.8 14.5 %all_to_all.15.payload_ref = bf16[8,88,512]{2,1,0:T(8,128)(2,1)S(1)} all-to-all(bf16[8,88,512]{2,1,0:T(8,128)(2,1)S(1)} %pack.1), channel_id=1, replica_groups={{16,17,19,18,2,3,1,0},{20,21,23,22,6,7,5,4},{24,25,27,26,10,11,9,8},{28..., dimensions={0} | all-to-all | bytes 1441792 | tf_op jit(solution)/shard_map/all_to_all | solution.py:440
  36.3 0.1 sum_shares.1
  36.4 1.4 %collective-permute-start.2 = (bf16[136,512]{1,0:T(8,128)(2,1)S(1)}, bf16[136,512]{1,0:T(8,128)(2,1)S(1)}, u32[]{:S(2)}, u32[]{:S(2)}) collective-permute-start(bf16[136,512]{1,0:T(8,128)(2,1)S(1)} %get-tuple-element.38), channel_id=1, source_target_pairs={{0,4},{1,5},{2,6},{3,7},{4,0},{5,1},{6,2},{7,3},{8,12},{9,13},{10,... | collective-permute-start | bytes 417800 | tf_op jit(solution)/shard_map/ppermute | solution.py:446
  37.8 3.0 %own_grad.1 = (f32[512,512]{1,0:T(8,128)S(1)}, s32[1,128]{1,0:T(1,128)S(1)}) custom-call(bf16[512,512]{1,0:T(8,128)(2,1)S(1)} %get-tuple-element.29.pre_grad_ref, bf16[512,512]{1,0:T(8,128)(2,1)S(1)} %get-tuple-element.31.message_ref, s32[16,512]{1,0:T(8,128)} %bitcast.8, s32[1,512]{1,0:T(1,128)} %bitcast.11, s32[1,128]{1,0:T(1,128)} %serve_hbm.3, ...), custom_call_target="tpu_custom_call" | custom-call | flops 536870912 | bytes 4194304 | tf_op jit(solution)/shard_map/own_grad/pallas_call | solution.py:43
  40.7 4.0 %collective-permute-done.2.received_ref = bf16[136,512]{1,0:T(8,128)(2,1)S(1)} collective-permute-done((bf16[136,512]{1,0:T(8,128)(2,1)S(1)}, bf16[136,512]{1,0:T(8,128)(2,1)S(1)}, u32[]{:S(2)}, u32[]{:S(2)}) %collective-permute-start.2) | collective-permute-done | bytes 139296 | tf_op jit(solution)/shard_map/ppermute | solution.py:446
  44.8 10.6 %all_to_all.16 = bf16[8,64,512]{2,1,0:T(8,128)(2,1)S(1)} all-to-all(bf16[8,64,512]{2,1,0:T(8,128)(2,1)S(1)} %total.1), channel_id=1, replica_groups={{19,18,17,16,3,2,1,0},{23,22,21,20,7,6,5,4},{27,26,25,24,11,10,9,8},{31..., dimensions={0} | all-to-all | bytes 1048576 | tf_op jit(solution)/shard_map/all_to_all | solution.py:451
  55.3 0.0 collective-permute-start.3
  55.4 1.7 %tail.1 = (f32[512,512]{1,0:T(8,128)}, f32[512,512]{1,0:T(8,128)}, f32[512,512]{1,0:T(8,128)}, f32[1,512]{1,0:T(1,128)}) custom-call(s32[1,128]{1,0:T(1,128)S(1)} %get-tuple-element.32.order_ref, bf16[136,512]{1,0:T(8,128)(2,1)S(1)} %get-tuple-element.37.keep_ref, bf16[136,512]{1,0:T(8,128)(2,1)S(1)} %collective-permute-done.2.received_ref, ...), custom_call_target="tpu_custom_call" | custom-call | flops 268435456 | bytes 4194304 | tf_op jit(solution)/shard_map/tail/pallas_call | solution.py:43
  57.0 0.2 collective-permute-done.3.half_ref
  57.3 1.0 %other_half.1 = (f32[512,512]{1,0:T(8,128)}, f32[512,512]{1,0:T(8,128)}) custom-call(bf16[512,512]{1,0:T(8,128)(2,1)S(1)} %collective-permute-done.3.half_ref, f32[512,512]{1,0:T(8,128)} %get-tuple-element.41.self_in, f32[512,512]{1,0:T(8,128)} %get-tuple-element.42.neigh_in), custom_call_target="tpu_custom_call", output_to_operand_aliasing={{0}: (1, {}), {1}: (2, {})} | custom-call | flops 134217728 | bytes 3145728 | tf_op jit(solution)/shard_map/other_half/pallas_call | solution.py:43
  (1 shorter events, 0.0 us)
Async XLA Ops:
  2.6 15.1 %all-to-all-start = ((bf16[32,4,512]{2,1,0:T(4,128)(2,1)}), bf16[32,4,512]{2,1,0:T(4,128)(2,1)S(1)}, u32[]{:S(2)}, u32[]{:S(2)}) async-start(bf16[32,4,512]{2,1,0:T(4,128)(2,1)} %serve.1), calls=%async_computation | async-start | bytes 262144 | tf_op jit(solution)/shard_map/all_to_all | solution.py:389
  9.9 7.7 %copy-start = (bf16[512,512]{1,0:T(8,128)(2,1)S(1)}, bf16[512,512]{1,0:T(8,128)(2,1)}, u32[]{:S(2)}) copy-start(bf16[512,512]{1,0:T(8,128)(2,1)} %w_neigh_ref.3) | copy-start | bytes 1572868
  19.4 2.2 %collective-permute-start = (bf16[512,512]{1,0:T(8,128)(2,1)S(1)}, bf16[512,512]{1,0:T(8,128)(2,1)S(1)}, u32[]{:S(2)}, u32[]{:S(2)}) collective-permute-start(bf16[512,512]{1,0:T(8,128)(2,1)S(1)} %get-tuple-element.33), channel_id=1, source_target_pairs={{0,8},{1,9},{2,10},{3,11},{4,12},{5,13},{6,14},{7,15},{8,0},{9,1},... | collective-permute-start | bytes 1572872 | tf_op jit(solution)/shard_map/ppermute | solution.py:418
  20.2 1.4 %collective-permute-start.1 = (bf16[72,512]{1,0:T(8,128)(2,1)S(1)}, bf16[72,512]{1,0:T(8,128)(2,1)S(1)}, u32[]{:S(2)}, u32[]{:S(2)}) collective-permute-start(bf16[72,512]{1,0:T(8,128)(2,1)S(1)} %get-tuple-element.35), channel_id=1, source_target_pairs={{0,8},{1,9},{2,10},{3,11},{4,12},{5,13},{6,14},{7,15},{8,0},{9,1},... | collective-permute-start | bytes 221192 | tf_op jit(solution)/shard_map/ppermute | solution.py:425
  36.4 8.3 %collective-permute-start.2 = (bf16[136,512]{1,0:T(8,128)(2,1)S(1)}, bf16[136,512]{1,0:T(8,128)(2,1)S(1)}, u32[]{:S(2)}, u32[]{:S(2)}) collective-permute-start(bf16[136,512]{1,0:T(8,128)(2,1)S(1)} %get-tuple-element.38), channel_id=1, source_target_pairs={{0,4},{1,5},{2,6},{3,7},{4,0},{5,1},{6,2},{7,3},{8,12},{9,13},{10,... | collective-permute-start | bytes 417800 | tf_op jit(solution)/shard_map/ppermute | solution.py:446
  55.3 1.9 %collective-permute-start.3 = (bf16[512,512]{1,0:T(8,128)(2,1)S(1)}, bf16[512,512]{1,0:T(8,128)(2,1)S(1)}, u32[]{:S(2)}, u32[]{:S(2)}) collective-permute-start(bf16[512,512]{1,0:T(8,128)(2,1)S(1)} %bitcast.5), channel_id=1, source_target_pairs={{0,8},{1,9},{2,10},{3,11},{4,12},{5,13},{6,14},{7,15},{8,0},{9,1},... | collective-permute-start | bytes 1572872 | tf_op jit(solution)/shard_map/ppermute | solution.py:452

commit v8 on v7

--- a/solution.py
+++ b/solution.py
@@ -269,12 +269,12 @@
         out_ref[peer] = jnp.concatenate(parts, axis=0).astype(BF16)
 
 
-def sum_kernel(dims, order, payload_ref, keep_ref, send_ref):
+def sum_kernel(dims, order, payload_ref, grads_ref, keep_ref, send_ref):
     cap = dims[2]
     peers, length, width = payload_ref.shape
     pair = 2 * cap
     count = peers * pair
-    share = keep_ref.shape[0] - count - 8
+    share = grads_ref.shape[0]
     grads = jnp.zeros((share, width), F32)
     bias = jnp.zeros((1, width), F32)
     lower, upper = [None] * peers, [None] * peers
@@ -284,7 +284,7 @@
         lower[order[peer]] = rest[:pair]
         upper[order[peer]] = rest[pair : 2 * pair]
         bias = bias + join_two(rest[2 * pair :])
-    grads = grads.astype(BF16)
+    grads_ref[...] = grads.astype(BF16)
     bias = split_in_two(bias)
     first = wide_of(dims[1]) == 0
     lower, upper = jnp.concatenate(lower, axis=0), jnp.concatenate(upper, axis=0)
@@ -292,16 +292,19 @@
         (keep_ref, jnp.where(first, lower, upper)),
         (send_ref, jnp.where(first, upper, lower)),
     ):
-        ref[:share, :] = grads
-        ref[share : share + count, :] = rows.astype(BF16)
-        ref[share + count :, :] = bias
+        ref[:count, :] = rows.astype(BF16)
+        ref[count:, :] = bias
 
 
 def total_kernel(keep_ref, received_ref, after_ref, out_ref):
     peers, share, width = out_ref.shape
-    total = (keep_ref[:share, :].astype(F32) + received_ref[:share, :].astype(F32)).astype(BF16)
+    total = (keep_ref[...].astype(F32) + received_ref[...].astype(F32)).astype(BF16)
     for peer in range(peers):
         out_ref[peer] = total
+
+
+def pass_kernel(source_ref, after_ref, out_ref):
+    out_ref[...] = source_ref[...]
 
 
 def send_half(matrix, source_ref, self_hbm, neigh_hbm, sem, rows, wait):
@@ -318,7 +321,7 @@
 
 
 def tail_kernel(
-    factor, share, near, order_ref, keep_ref, received_ref, base_ref, mine_ref,
+    factor, near, order_ref, keep_ref, received_ref, base_ref, mine_ref,
     out_hbm, self_hbm, neigh_hbm, bias_hbm, wide_ref, out_ref, bias_ref, sems,
 ):
     own_rows, slots = base_ref.shape[0], order_ref.shape[1]
@@ -327,13 +330,10 @@
     everything = pl.ds(0, own_rows)
     wide_ref[...] = mine_ref[...].astype(F32) * factor
     send_half(matrix, wide_ref, self_hbm, neigh_hbm, sems.at[0], everything, False)
-    last = keep_ref.shape[0] - 8
-    bias_ref[...] = (join_two(keep_ref[last:, :]) + join_two(received_ref[last:, :])) * factor
+    bias_ref[...] = (join_two(keep_ref[half:, :]) + join_two(received_ref[half:, :])) * factor
     copies = [pltpu.make_async_copy(bias_ref, bias_hbm, sems.at[1])]
     copies[0].start()
-    rows = jnp.concatenate(
-        [keep_ref[share : share + half, :], received_ref[share : share + half, :]], axis=0
-    )
+    rows = jnp.concatenate([keep_ref[:half, :], received_ref[:half, :]], axis=0)
     row = lax.broadcasted_iota(jnp.int32, (own_rows, slots), 0)
     picks = (row == order_ref[...]).astype(F32).astype(BF16)
     out_ref[...] = base_ref[...] + product(picks, rows, 1, 0)
@@ -438,21 +438,26 @@
         ((shape((peers, length, width), BF16), VMEM),), flops=work // 4, moved=4 << 20,
     )(received, keep, received_rows, keep_rows)
     arrived = lax.all_to_all(payload, "node", 0, 0, axis_index_groups=cubes, tiled=True)
-    pairs = shape((share + half + 8, width), BF16)
-    keep_sum, send_sum = call(
+    grads = shape((share, width), BF16)
+    pairs = shape((half + 8, width), BF16)
+    keep_grads, keep_sum, send_sum = call(
         "sum_shares", functools.partial(sum_kernel, dims, chips), (VMEM,),
-        ((pairs, VMEM), (pairs, VMEM)), flops=work // 8, moved=1 << 20,
+        ((grads, VMEM), (pairs, VMEM), (pairs, VMEM)), flops=work // 8, moved=1 << 20,
     )(arrived)
+    received_grads = lax.ppermute(keep_grads, "node", swap_wide)
     received_sum = lax.ppermute(send_sum, "node", swap_wide)
     (total,) = call(
-        "total", total_kernel, (VMEM, VMEM, VMEM), ((shape((peers, share, width), BF16), VMEM),),
+        "total", total_kernel, (VMEM,) * 3, ((shape((peers, share, width), BF16), VMEM),),
         flops=work // 8, moved=1 << 20,
-    )(keep_sum, received_sum, base)
-    mine = lax.all_to_all(total, "node", 0, 0, axis_index_groups=gather_cubes, tiled=True).reshape(own_rows, width)
+    )(keep_grads, received_grads, base)
+    gathered = lax.all_to_all(total, "node", 0, 0, axis_index_groups=gather_cubes, tiled=True)
+    (mine,) = call(
+        "after_rows", pass_kernel, (VMEM, VMEM), ((square16, VMEM),), flops=work // 8, moved=1 << 20,
+    )(gathered.reshape(own_rows, width), received_sum)
     other = lax.ppermute(mine, "node", swap_core)
     wide = VMEM((own_rows, width), F32)
     grad_features, self_part, neigh_part, bias_sum = call(
-        "tail", functools.partial(tail_kernel, factor, share, near), (VMEM,) * 5,
+        "tail", functools.partial(tail_kernel, factor, near), (VMEM,) * 5,
         ((square32, HBM), (square32, HBM), (square32, HBM), (shape((1, width), F32), HBM)),
         scratch=[wide, wide, VMEM((1, width), F32)], copies=3, flops=work, moved=4 << 20,
     )(order, keep_sum, received_sum, base, mine)

time: 58.6 us -> 57.1 us (0.974)
  blocking collectives: 25.1 us -> 14.5 us
  starting transfers between devices: 9.3 us -> 15.1 us
  waiting for transfers between devices: 9.14 us -> 11.5 us
  Pallas kernels: 14 us -> 14.8 us
    all_to_all x1 -> x0, blocking collectives: 10.6 us -> none  [local(): lax.all_to_all(total, 'node', 0, 0, axis_index_groups=gather_cubes, tiled...]
    all_to_all x0 -> x1, starting transfers between devices: none -> 5.1 us  [local(): lax.all_to_all(total, 'node', 0, 0, axis_index_groups=gather_cubes, tiled...]
    ppermute x0 -> x1, waiting for transfers between devices: none -> 1.64 us  [local(): received_grads = lax.ppermute(keep_grads, 'node', swap_wide)]
    ppermute x0 -> x1, starting transfers between devices: none -> 1.35 us  [local(): received_grads = lax.ppermute(keep_grads, 'node', swap_wide)]
    pallas_call x11 -> x12, Pallas kernels: 14 us -> 14.8 us  [held(): run(*(pltpu.with_memory_space_constraint(operand, HBM) if memory is HBM e...]
    ppermute x1, waiting for transfers between devices: 4.01 us -> 4.74 us  [local(): received_sum = lax.ppermute(send_sum, 'node', swap_wide)]
    ppermute x1, starting transfers between devices: 1.35 us -> 0.63 us  [local(): received_sum = lax.ppermute(send_sum, 'node', swap_wide)]
  transfers between devices with their start and end apart: 5 -> 7, of which waited for: 4 -> 5; matrix products, arithmetic and copies ran while one was open for 0% -> 0% of each run, Pallas kernels for 15% -> 16%
where the time goes in v8:
time: 57.1 us; the launch traced here: 56.7 us
  starting transfers between devices  15.1 us (26%)
  Pallas kernels  14.8 us (26%)
  blocking collectives  14.5 us (25%)
  waiting for transfers between devices  11.5 us (20%)
  between operations  0.72 us (1%)
    pallas_call x12, Pallas kernels, held(): run(*(pltpu.with_memory_space_constraint(operand, HBM) if memory is HBM e...  14.8 us
    all_to_all x1, blocking collectives, local(): lax.all_to_all(payload, 'node', 0, 0, axis_index_groups=cubes, tiled=True)  14.5 us
    all_to_all x1, starting transfers between devices, local(): incoming = lax.all_to_all(outgoing, 'node', 0, 0, tiled=True)  7.3 us
    all_to_all x1, starting transfers between devices, local(): lax.all_to_all(total, 'node', 0, 0, axis_index_groups=gather_cubes, tiled...  5.1 us
    ppermute x1, waiting for transfers between devices, local(): received_sum = lax.ppermute(send_sum, 'node', swap_wide)  4.74 us
    all_to_all x1, waiting for transfers between devices, local(): incoming = lax.all_to_all(outgoing, 'node', 0, 0, tiled=True)  4.49 us
    ppermute x1, waiting for transfers between devices, local(): received_grads = lax.ppermute(keep_grads, 'node', swap_wide)  1.64 us
    ppermute x1, starting transfers between devices, local(): received_grads = lax.ppermute(keep_grads, 'node', swap_wide)  1.35 us
  transfers between devices with their start and end apart: 7, of which 5 were waited for; matrix products, arithmetic and copies ran while one was open for 0% of the time, Pallas kernels for 16%

profile of v8, /device:TPU:0, one launch (start us, length us, event | category | flops | bytes accessed | tf_op | source)
XLA Modules:
  0.0 56.7 jit_solution(14499064522266104063)
XLA Ops:
  0.6 2.0 %serve.1 = bf16[32,4,512]{2,1,0:T(4,128)(2,1)} custom-call(s32[1,128]{1,0:T(1,128)} %serve_hbm.3, bf16[512,512]{1,0:T(8,128)(2,1)} %features_hbm.5), custom_call_target="tpu_custom_call" | custom-call | flops 67108864 | bytes 1048576 | tf_op jit(solution)/shard_map/serve/pallas_call | solution.py:43
  2.6 7.3 %all-to-all-start = ((bf16[32,4,512]{2,1,0:T(4,128)(2,1)}), bf16[32,4,512]{2,1,0:T(4,128)(2,1)S(1)}, u32[]{:S(2)}, u32[]{:S(2)}) async-start(bf16[32,4,512]{2,1,0:T(4,128)(2,1)} %serve.1), calls=%async_computation | async-start | bytes 262144 | tf_op jit(solution)/shard_map/all_to_all | solution.py:389
  9.9 3.2 %own_aggregate.1 = (f32[512,512]{1,0:T(8,128)S(1)}, bf16[512,128]{1,0:T(8,128)(2,1)S(1)}, bf16[128,512]{1,0:T(8,128)(2,1)S(1)}, f32[512,128]{1,0:T(8,128)S(1)}, f32[512,512]{1,0:T(8,128)S(1)}) custom-call(s32[16,512]{1,0:T(8,128)} %bitcast.6, s32[1,512]{1,0:T(1,128)} %bitcast.9, bf16[512,512]{1,0:T(8,128)(2,1)} %features_hbm.5, bf16[512,512]{1,0:T(8,128)(2,1)} %w_self_hbm.3, ...), custom_call_target="tpu_custom_call" | custom-call | flops 5368709120 | bytes 4194304 | tf_op jit(solution)/shard_map/own_aggregate/pallas_call | solution.py:43
  13.2 4.5 %all-to-all-done.incoming_ref = bf16[32,4,512]{2,1,0:T(4,128)(2,1)S(1)} async-done(((bf16[32,4,512]{2,1,0:T(4,128)(2,1)}), bf16[32,4,512]{2,1,0:T(4,128)(2,1)S(1)}, u32[]{:S(2)}, u32[]{:S(2)}) %all-to-all-start) | async-done | bytes 131104 | tf_op jit(solution)/shard_map/all_to_all | solution.py:389
  17.7 1.7 %layer_grad.1 = (bf16[512,512]{1,0:T(8,128)(2,1)S(1)}, bf16[2,512,512]{2,1,0:T(8,128)(2,1)S(1)}, bf16[512,512]{1,0:T(8,128)(2,1)S(1)}) custom-call(bf16[32,4,512]{2,1,0:T(4,128)(2,1)S(1)} %all-to-all-done.incoming_ref, f32[512,512]{1,0:T(8,128)S(1)} %get-tuple-element.26.own_sum_ref, bf16[512,128]{1,0:T(8,128)(2,1)S(1)} %get-tuple-element.27.fetch_counts_ref, ...), custom_call_target="tpu_custom_call" | custom-call | flops 1342177280 | bytes 8388608 | tf_op jit(solution)/shard_map/layer_grad/pallas_call | solution.py:43
  19.4 0.2 collective-permute-start
  19.6 0.7 %messages.1 = (bf16[512,512]{1,0:T(8,128)(2,1)S(1)}, bf16[72,512]{1,0:T(8,128)(2,1)S(1)}, bf16[72,512]{1,0:T(8,128)(2,1)S(1)}) custom-call(bf16[512,512]{1,0:T(8,128)(2,1)S(1)} %get-tuple-element.30.pre_grad_ref, bf16[512,512]{1,0:T(8,128)(2,1)S(1)} %copy-done, f32[512,128]{1,0:T(8,128)S(1)} %get-tuple-element.28.inverse_ref, ...), custom_call_target="tpu_custom_call" | custom-call | flops 536870912 | bytes 4194304 | tf_op jit(solution)/shard_map/messages/pallas_call | solution.py:43
  20.2 0.5 collective-permute-start.1
  20.7 0.5 keep_grad.1.keep_ref
  21.2 0.4 collective-permute-done.1.received_rows_ref
  21.6 0.1 pack.1
  21.8 14.5 %all_to_all.15.payload_ref = bf16[8,88,512]{2,1,0:T(8,128)(2,1)S(1)} all-to-all(bf16[8,88,512]{2,1,0:T(8,128)(2,1)S(1)} %pack.1), channel_id=1, replica_groups={{16,17,19,18,2,3,1,0},{20,21,23,22,6,7,5,4},{24,25,27,26,10,11,9,8},{28..., dimensions={0} | all-to-all | bytes 1441792 | tf_op jit(solution)/shard_map/all_to_all | solution.py:440
  36.3 0.1 sum_shares.1
  36.4 1.4 %collective-permute-start.3 = (bf16[64,512]{1,0:T(8,128)(2,1)S(1)}, bf16[64,512]{1,0:T(8,128)(2,1)S(1)}, u32[]{:S(2)}, u32[]{:S(2)}) collective-permute-start(bf16[64,512]{1,0:T(8,128)(2,1)S(1)} %get-tuple-element.41.keep_ref), channel_id=1, source_target_pairs={{0,4},{1,5},{2,6},{3,7},{4,0},{5,1},{6,2},{7,3},{8,12},{9,13},{10,... | collective-permute-start | bytes 196616 | tf_op jit(solution)/shard_map/ppermute | solution.py:447
  37.8 3.0 %own_grad.1 = (f32[512,512]{1,0:T(8,128)S(1)}, s32[1,128]{1,0:T(1,128)S(1)}) custom-call(bf16[512,512]{1,0:T(8,128)(2,1)S(1)} %get-tuple-element.30.pre_grad_ref, bf16[512,512]{1,0:T(8,128)(2,1)S(1)} %get-tuple-element.32.message_ref, s32[16,512]{1,0:T(8,128)} %bitcast.7, s32[1,512]{1,0:T(1,128)} %bitcast.10, s32[1,128]{1,0:T(1,128)} %serve_hbm.3, ...), custom_call_target="tpu_custom_call" | custom-call | flops 536870912 | bytes 4194304 | tf_op jit(solution)/shard_map/own_grad/pallas_call | solution.py:43
  40.7 1.6 %collective-permute-done.3.received_ref = bf16[64,512]{1,0:T(8,128)(2,1)S(1)} collective-permute-done((bf16[64,512]{1,0:T(8,128)(2,1)S(1)}, bf16[64,512]{1,0:T(8,128)(2,1)S(1)}, u32[]{:S(2)}, u32[]{:S(2)}) %collective-permute-start.3) | collective-permute-done | bytes 65568 | tf_op jit(solution)/shard_map/ppermute | solution.py:447
  42.4 0.8 %total.1 = bf16[8,64,512]{2,1,0:T(8,128)(2,1)} custom-call(bf16[64,512]{1,0:T(8,128)(2,1)S(1)} %get-tuple-element.41.keep_ref, bf16[64,512]{1,0:T(8,128)(2,1)S(1)} %collective-permute-done.3.received_ref, f32[512,512]{1,0:T(8,128)S(1)} %get-tuple-element.40.after_ref.base_ref), custom_call_target="tpu_custom_call" | custom-call | flops 33554432 | bytes 1048576 | tf_op jit(solution)/shard_map/total/pallas_call | solution.py:43
  43.2 5.1 %all-to-all-start.2 = ((bf16[8,64,512]{2,1,0:T(8,128)(2,1)}), bf16[8,64,512]{2,1,0:T(8,128)(2,1)S(1)}, u32[]{:S(2)}, u32[]{:S(2)}) async-start(bf16[8,64,512]{2,1,0:T(8,128)(2,1)} %total.1), calls=%async_computation.2 | async-start | bytes 1048576 | tf_op jit(solution)/shard_map/all_to_all | solution.py:453
  48.3 0.6 %collective-permute-start.2 = (bf16[72,512]{1,0:T(8,128)(2,1)S(1)}, bf16[72,512]{1,0:T(8,128)(2,1)S(1)}, u32[]{:S(2)}, u32[]{:S(2)}) collective-permute-start(bf16[72,512]{1,0:T(8,128)(2,1)S(1)} %get-tuple-element.39), channel_id=1, source_target_pairs={{0,4},{1,5},{2,6},{3,7},{4,0},{5,1},{6,2},{7,3},{8,12},{9,13},{10,... | collective-permute-start | bytes 221192 | tf_op jit(solution)/shard_map/ppermute | solution.py:448
  48.9 4.7 %collective-permute-done.2.after_ref.received_ref = bf16[72,512]{1,0:T(8,128)(2,1)S(1)} collective-permute-done((bf16[72,512]{1,0:T(8,128)(2,1)S(1)}, bf16[72,512]{1,0:T(8,128)(2,1)S(1)}, u32[]{:S(2)}, u32[]{:S(2)}) %collective-permute-start.2) | collective-permute-done | bytes 73760 | tf_op jit(solution)/shard_map/ppermute | solution.py:448
  53.7 0.1 collective-permute-start.4
  53.8 1.7 %tail.1 = (f32[512,512]{1,0:T(8,128)}, f32[512,512]{1,0:T(8,128)}, f32[512,512]{1,0:T(8,128)}, f32[1,512]{1,0:T(1,128)}) custom-call(s32[1,128]{1,0:T(1,128)S(1)} %get-tuple-element.33.order_ref, bf16[72,512]{1,0:T(8,128)(2,1)S(1)} %get-tuple-element.38.keep_ref, bf16[72,512]{1,0:T(8,128)(2,1)S(1)} %collective-permute-done.2.after_ref.received_ref, ...), custom_call_target="tpu_custom_call" | custom-call | flops 268435456 | bytes 4194304 | tf_op jit(solution)/shard_map/tail/pallas_call | solution.py:43
  55.5 0.2 collective-permute-done.4.half_ref
  55.7 1.0 %other_half.1 = (f32[512,512]{1,0:T(8,128)}, f32[512,512]{1,0:T(8,128)}) custom-call(bf16[512,512]{1,0:T(8,128)(2,1)S(1)} %collective-permute-done.4.half_ref, f32[512,512]{1,0:T(8,128)} %get-tuple-element.43.self_in, f32[512,512]{1,0:T(8,128)} %get-tuple-element.44.neigh_in), custom_call_target="tpu_custom_call", output_to_operand_aliasing={{0}: (1, {}), {1}: (2, {})} | custom-call | flops 134217728 | bytes 3145728 | tf_op jit(solution)/shard_map/other_half/pallas_call | solution.py:43
  (5 shorter events, 0.0 us)
Async XLA Ops:
  2.6 15.1 %all-to-all-start = ((bf16[32,4,512]{2,1,0:T(4,128)(2,1)}), bf16[32,4,512]{2,1,0:T(4,128)(2,1)S(1)}, u32[]{:S(2)}, u32[]{:S(2)}) async-start(bf16[32,4,512]{2,1,0:T(4,128)(2,1)} %serve.1), calls=%async_computation | async-start | bytes 262144 | tf_op jit(solution)/shard_map/all_to_all | solution.py:389
  9.9 7.7 %copy-start = (bf16[512,512]{1,0:T(8,128)(2,1)S(1)}, bf16[512,512]{1,0:T(8,128)(2,1)}, u32[]{:S(2)}) copy-start(bf16[512,512]{1,0:T(8,128)(2,1)} %w_neigh_ref.3) | copy-start | bytes 1572868
  19.4 2.2 %collective-permute-start = (bf16[512,512]{1,0:T(8,128)(2,1)S(1)}, bf16[512,512]{1,0:T(8,128)(2,1)S(1)}, u32[]{:S(2)}, u32[]{:S(2)}) collective-permute-start(bf16[512,512]{1,0:T(8,128)(2,1)S(1)} %get-tuple-element.34), channel_id=1, source_target_pairs={{0,8},{1,9},{2,10},{3,11},{4,12},{5,13},{6,14},{7,15},{8,0},{9,1},... | collective-permute-start | bytes 1572872 | tf_op jit(solution)/shard_map/ppermute | solution.py:418
  20.2 1.4 %collective-permute-start.1 = (bf16[72,512]{1,0:T(8,128)(2,1)S(1)}, bf16[72,512]{1,0:T(8,128)(2,1)S(1)}, u32[]{:S(2)}, u32[]{:S(2)}) collective-permute-start(bf16[72,512]{1,0:T(8,128)(2,1)S(1)} %get-tuple-element.36), channel_id=1, source_target_pairs={{0,8},{1,9},{2,10},{3,11},{4,12},{5,13},{6,14},{7,15},{8,0},{9,1},... | collective-permute-start | bytes 221192 | tf_op jit(solution)/shard_map/ppermute | solution.py:425
  36.4 6.0 %collective-permute-start.3 = (bf16[64,512]{1,0:T(8,128)(2,1)S(1)}, bf16[64,512]{1,0:T(8,128)(2,1)S(1)}, u32[]{:S(2)}, u32[]{:S(2)}) collective-permute-start(bf16[64,512]{1,0:T(8,128)(2,1)S(1)} %get-tuple-element.41.keep_ref), channel_id=1, source_target_pairs={{0,4},{1,5},{2,6},{3,7},{4,0},{5,1},{6,2},{7,3},{8,12},{9,13},{10,... | collective-permute-start | bytes 196616 | tf_op jit(solution)/shard_map/ppermute | solution.py:447
  43.2 10.5 %all-to-all-start.2 = ((bf16[8,64,512]{2,1,0:T(8,128)(2,1)}), bf16[8,64,512]{2,1,0:T(8,128)(2,1)S(1)}, u32[]{:S(2)}, u32[]{:S(2)}) async-start(bf16[8,64,512]{2,1,0:T(8,128)(2,1)} %total.1), calls=%async_computation.2 | async-start | bytes 1048576 | tf_op jit(solution)/shard_map/all_to_all | solution.py:453
  48.3 5.4 %collective-permute-start.2 = (bf16[72,512]{1,0:T(8,128)(2,1)S(1)}, bf16[72,512]{1,0:T(8,128)(2,1)S(1)}, u32[]{:S(2)}, u32[]{:S(2)}) collective-permute-start(bf16[72,512]{1,0:T(8,128)(2,1)S(1)} %get-tuple-element.39), channel_id=1, source_target_pairs={{0,4},{1,5},{2,6},{3,7},{4,0},{5,1},{6,2},{7,3},{8,12},{9,13},{10,... | collective-permute-start | bytes 221192 | tf_op jit(solution)/shard_map/ppermute | solution.py:448
  53.7 2.0 %collective-permute-start.4 = (bf16[512,512]{1,0:T(8,128)(2,1)S(1)}, bf16[512,512]{1,0:T(8,128)(2,1)S(1)}, u32[]{:S(2)}, u32[]{:S(2)}) collective-permute-start(bf16[512,512]{1,0:T(8,128)(2,1)S(1)} %after_rows.1.mine_ref), channel_id=1, source_target_pairs={{0,8},{1,9},{2,10},{3,11},{4,12},{5,13},{6,14},{7,15},{8,0},{9,1},... | collective-permute-start | bytes 1572872 | tf_op jit(solution)/shard_map/ppermute | solution.py:457

commit v9 on v8

--- a/solution.py
+++ b/solution.py
@@ -251,7 +251,7 @@
 def pack_kernel(dims, order, gather_order, received_ref, keep_ref, received_rows_ref, keep_rows_ref, out_ref):
     across, near, cap = dims
     own_rows, width = keep_ref.shape
-    peers, length = out_ref.shape[0], out_ref.shape[1]
+    peers, length = out_ref.shape[0], out_ref.shape[1] * out_ref.shape[2]
     half = 2 * peers * cap
     share = own_rows // peers
     keep_rows = keep_rows_ref[...].astype(F32)
@@ -266,12 +266,12 @@
             at = ((place // near * 2 + wide) * near + place % near) * cap
             parts += [keep_rows[at : at + cap], other_rows[at : at + cap]]
         parts.append(bias[: length - share - 4 * cap])
-        out_ref[peer] = jnp.concatenate(parts, axis=0).astype(BF16)
+        out_ref[peer] = jnp.concatenate(parts, axis=0).reshape(out_ref.shape[1:]).astype(BF16)
 
 
 def sum_kernel(dims, order, payload_ref, grads_ref, keep_ref, send_ref):
     cap = dims[2]
-    peers, length, width = payload_ref.shape
+    peers, width = payload_ref.shape[0], payload_ref.shape[3]
     pair = 2 * cap
     count = peers * pair
     share = grads_ref.shape[0]
@@ -279,8 +279,9 @@
     bias = jnp.zeros((1, width), F32)
     lower, upper = [None] * peers, [None] * peers
     for peer in range(peers):
-        grads = grads + payload_ref[peer, :share, :].astype(F32)
-        rest = payload_ref[peer, share:, :].astype(F32)
+        block = payload_ref[peer].astype(F32).reshape(-1, width)
+        grads = grads + block[:share]
+        rest = block[share:]
         lower[order[peer]] = rest[:pair]
         upper[order[peer]] = rest[pair : 2 * pair]
         bias = bias + join_two(rest[2 * pair :])
@@ -366,7 +367,7 @@
     cap = slots // devices
     half = slots // 2
     share = own_rows // peers
-    length = -(-(share + 4 * cap + 1) // 8) * 8
+    length = -(-(share + 4 * cap + 2) // 4) * 4
     dims = (across, near, cap)
     chips = [place ^ (place >> 1) for place in reversed(range(peers))]
     gather_chips = list(reversed(range(peers)))
@@ -435,7 +436,7 @@
     )(pre_grad, message, neighbours, neigh_count, serve_rows, w_self)
     (payload,) = call(
         "pack", functools.partial(pack_kernel, dims, chips, gather_chips), (VMEM,) * 4,
-        ((shape((peers, length, width), BF16), VMEM),), flops=work // 4, moved=4 << 20,
+        ((shape((peers, length // 4, 4, width), BF16), VMEM),), flops=work // 4, moved=4 << 20,
     )(received, keep, received_rows, keep_rows)
     arrived = lax.all_to_all(payload, "node", 0, 0, axis_index_groups=cubes, tiled=True)
     grads = shape((share, width), BF16)

time: 57.1 us -> 56.9 us (level)
  no operation moved by 1% of the time
where the time goes in v9:
time: 56.9 us; the launch traced here: 56.5 us
  starting transfers between devices  15.1 us (27%)
  Pallas kernels  15 us (26%)
  blocking collectives  14.2 us (25%)
  waiting for transfers between devices  11.5 us (20%)
  between operations  0.72 us (1%)
    pallas_call x12, Pallas kernels, held(): run(*(pltpu.with_memory_space_constraint(operand, HBM) if memory is HBM e...  15 us
    all_to_all x1, blocking collectives, local(): lax.all_to_all(payload, 'node', 0, 0, axis_index_groups=cubes, tiled=True)  14.2 us
    all_to_all x1, starting transfers between devices, local(): incoming = lax.all_to_all(outgoing, 'node', 0, 0, tiled=True)  7.3 us
    all_to_all x1, starting transfers between devices, local(): lax.all_to_all(total, 'node', 0, 0, axis_index_groups=gather_cubes, tiled...  5.1 us
    ppermute x1, waiting for transfers between devices, local(): received_sum = lax.ppermute(send_sum, 'node', swap_wide)  4.75 us
    all_to_all x1, waiting for transfers between devices, local(): incoming = lax.all_to_all(outgoing, 'node', 0, 0, tiled=True)  4.49 us
    ppermute x1, waiting for transfers between devices, local(): received_grads = lax.ppermute(keep_grads, 'node', swap_wide)  1.62 us
    ppermute x1, starting transfers between devices, local(): received_grads = lax.ppermute(keep_grads, 'node', swap_wide)  1.35 us
  transfers between devices with their start and end apart: 7, of which 5 were waited for; matrix products, arithmetic and copies ran while one was open for 0% of the time, Pallas kernels for 16%

profile of v9, /device:TPU:0, one launch (start us, length us, event | category | flops | bytes accessed | tf_op | source)
XLA Modules:
  0.0 56.5 jit_solution(7766212072498910007)
XLA Ops:
  0.6 2.0 %serve.1 = bf16[32,4,512]{2,1,0:T(4,128)(2,1)} custom-call(s32[1,128]{1,0:T(1,128)} %serve_hbm.3, bf16[512,512]{1,0:T(8,128)(2,1)} %features_hbm.5), custom_call_target="tpu_custom_call" | custom-call | flops 67108864 | bytes 1048576 | tf_op jit(solution)/shard_map/serve/pallas_call | solution.py:43
  2.6 7.3 %all-to-all-start = ((bf16[32,4,512]{2,1,0:T(4,128)(2,1)}), bf16[32,4,512]{2,1,0:T(4,128)(2,1)S(1)}, u32[]{:S(2)}, u32[]{:S(2)}) async-start(bf16[32,4,512]{2,1,0:T(4,128)(2,1)} %serve.1), calls=%async_computation | async-start | bytes 262144 | tf_op jit(solution)/shard_map/all_to_all | solution.py:390
  9.9 3.2 %own_aggregate.1 = (f32[512,512]{1,0:T(8,128)S(1)}, bf16[512,128]{1,0:T(8,128)(2,1)S(1)}, bf16[128,512]{1,0:T(8,128)(2,1)S(1)}, f32[512,128]{1,0:T(8,128)S(1)}, f32[512,512]{1,0:T(8,128)S(1)}) custom-call(s32[16,512]{1,0:T(8,128)} %bitcast.6, s32[1,512]{1,0:T(1,128)} %bitcast.9, bf16[512,512]{1,0:T(8,128)(2,1)} %features_hbm.5, bf16[512,512]{1,0:T(8,128)(2,1)} %w_self_hbm.3, ...), custom_call_target="tpu_custom_call" | custom-call | flops 5368709120 | bytes 4194304 | tf_op jit(solution)/shard_map/own_aggregate/pallas_call | solution.py:43
  13.2 4.5 %all-to-all-done.incoming_ref = bf16[32,4,512]{2,1,0:T(4,128)(2,1)S(1)} async-done(((bf16[32,4,512]{2,1,0:T(4,128)(2,1)}), bf16[32,4,512]{2,1,0:T(4,128)(2,1)S(1)}, u32[]{:S(2)}, u32[]{:S(2)}) %all-to-all-start) | async-done | bytes 131104 | tf_op jit(solution)/shard_map/all_to_all | solution.py:390
  17.7 1.7 %layer_grad.1 = (bf16[512,512]{1,0:T(8,128)(2,1)S(1)}, bf16[2,512,512]{2,1,0:T(8,128)(2,1)S(1)}, bf16[512,512]{1,0:T(8,128)(2,1)S(1)}) custom-call(bf16[32,4,512]{2,1,0:T(4,128)(2,1)S(1)} %all-to-all-done.incoming_ref, f32[512,512]{1,0:T(8,128)S(1)} %get-tuple-element.26.own_sum_ref, bf16[512,128]{1,0:T(8,128)(2,1)S(1)} %get-tuple-element.27.fetch_counts_ref, ...), custom_call_target="tpu_custom_call" | custom-call | flops 1342177280 | bytes 8388608 | tf_op jit(solution)/shard_map/layer_grad/pallas_call | solution.py:43
  19.4 0.2 collective-permute-start
  19.6 0.7 %messages.1 = (bf16[512,512]{1,0:T(8,128)(2,1)S(1)}, bf16[72,512]{1,0:T(8,128)(2,1)S(1)}, bf16[72,512]{1,0:T(8,128)(2,1)S(1)}) custom-call(bf16[512,512]{1,0:T(8,128)(2,1)S(1)} %get-tuple-element.30.pre_grad_ref, bf16[512,512]{1,0:T(8,128)(2,1)S(1)} %copy-done, f32[512,128]{1,0:T(8,128)S(1)} %get-tuple-element.28.inverse_ref, ...), custom_call_target="tpu_custom_call" | custom-call | flops 536870912 | bytes 4194304 | tf_op jit(solution)/shard_map/messages/pallas_call | solution.py:43
  20.2 0.5 collective-permute-start.1
  20.7 0.5 keep_grad.1.keep_ref
  21.2 0.4 collective-permute-done.1.received_rows_ref
  21.6 0.3 pack.1
  21.9 14.2 %all_to_all.15.payload_ref = bf16[8,21,4,512]{3,2,1,0:T(4,128)(2,1)S(1)} all-to-all(bf16[8,21,4,512]{3,2,1,0:T(4,128)(2,1)S(1)} %pack.1), channel_id=1, replica_groups={{16,17,19,18,2,3,1,0},{20,21,23,22,6,7,5,4},{24,25,27,26,10,11,9,8},{28..., dimensions={0} | all-to-all | bytes 1376256 | tf_op jit(solution)/shard_map/all_to_all | solution.py:441
  36.1 0.1 sum_shares.1
  36.3 1.4 %collective-permute-start.3 = (bf16[64,512]{1,0:T(8,128)(2,1)S(1)}, bf16[64,512]{1,0:T(8,128)(2,1)S(1)}, u32[]{:S(2)}, u32[]{:S(2)}) collective-permute-start(bf16[64,512]{1,0:T(8,128)(2,1)S(1)} %get-tuple-element.41.keep_ref), channel_id=1, source_target_pairs={{0,4},{1,5},{2,6},{3,7},{4,0},{5,1},{6,2},{7,3},{8,12},{9,13},{10,... | collective-permute-start | bytes 196616 | tf_op jit(solution)/shard_map/ppermute | solution.py:448
  37.6 3.0 %own_grad.1 = (f32[512,512]{1,0:T(8,128)S(1)}, s32[1,128]{1,0:T(1,128)S(1)}) custom-call(bf16[512,512]{1,0:T(8,128)(2,1)S(1)} %get-tuple-element.30.pre_grad_ref, bf16[512,512]{1,0:T(8,128)(2,1)S(1)} %get-tuple-element.32.message_ref, s32[16,512]{1,0:T(8,128)} %bitcast.7, s32[1,512]{1,0:T(1,128)} %bitcast.10, s32[1,128]{1,0:T(1,128)} %serve_hbm.3, ...), custom_call_target="tpu_custom_call" | custom-call | flops 536870912 | bytes 4194304 | tf_op jit(solution)/shard_map/own_grad/pallas_call | solution.py:43
  40.6 1.6 %collective-permute-done.3.received_ref = bf16[64,512]{1,0:T(8,128)(2,1)S(1)} collective-permute-done((bf16[64,512]{1,0:T(8,128)(2,1)S(1)}, bf16[64,512]{1,0:T(8,128)(2,1)S(1)}, u32[]{:S(2)}, u32[]{:S(2)}) %collective-permute-start.3) | collective-permute-done | bytes 65568 | tf_op jit(solution)/shard_map/ppermute | solution.py:448
  42.2 0.8 %total.1 = bf16[8,64,512]{2,1,0:T(8,128)(2,1)} custom-call(bf16[64,512]{1,0:T(8,128)(2,1)S(1)} %get-tuple-element.41.keep_ref, bf16[64,512]{1,0:T(8,128)(2,1)S(1)} %collective-permute-done.3.received_ref, f32[512,512]{1,0:T(8,128)S(1)} %get-tuple-element.40.after_ref.base_ref), custom_call_target="tpu_custom_call" | custom-call | flops 33554432 | bytes 1048576 | tf_op jit(solution)/shard_map/total/pallas_call | solution.py:43
  43.0 5.1 %all-to-all-start.2 = ((bf16[8,64,512]{2,1,0:T(8,128)(2,1)}), bf16[8,64,512]{2,1,0:T(8,128)(2,1)S(1)}, u32[]{:S(2)}, u32[]{:S(2)}) async-start(bf16[8,64,512]{2,1,0:T(8,128)(2,1)} %total.1), calls=%async_computation.2 | async-start | bytes 1048576 | tf_op jit(solution)/shard_map/all_to_all | solution.py:454
  48.1 0.6 %collective-permute-start.2 = (bf16[72,512]{1,0:T(8,128)(2,1)S(1)}, bf16[72,512]{1,0:T(8,128)(2,1)S(1)}, u32[]{:S(2)}, u32[]{:S(2)}) collective-permute-start(bf16[72,512]{1,0:T(8,128)(2,1)S(1)} %get-tuple-element.39), channel_id=1, source_target_pairs={{0,4},{1,5},{2,6},{3,7},{4,0},{5,1},{6,2},{7,3},{8,12},{9,13},{10,... | collective-permute-start | bytes 221192 | tf_op jit(solution)/shard_map/ppermute | solution.py:449
  48.7 4.8 %collective-permute-done.2.after_ref.received_ref = bf16[72,512]{1,0:T(8,128)(2,1)S(1)} collective-permute-done((bf16[72,512]{1,0:T(8,128)(2,1)S(1)}, bf16[72,512]{1,0:T(8,128)(2,1)S(1)}, u32[]{:S(2)}, u32[]{:S(2)}) %collective-permute-start.2) | collective-permute-done | bytes 73760 | tf_op jit(solution)/shard_map/ppermute | solution.py:449
  53.5 0.1 collective-permute-start.4
  53.6 1.7 %tail.1 = (f32[512,512]{1,0:T(8,128)}, f32[512,512]{1,0:T(8,128)}, f32[512,512]{1,0:T(8,128)}, f32[1,512]{1,0:T(1,128)}) custom-call(s32[1,128]{1,0:T(1,128)S(1)} %get-tuple-element.33.order_ref, bf16[72,512]{1,0:T(8,128)(2,1)S(1)} %get-tuple-element.38.keep_ref, bf16[72,512]{1,0:T(8,128)(2,1)S(1)} %collective-permute-done.2.after_ref.received_ref, ...), custom_call_target="tpu_custom_call" | custom-call | flops 268435456 | bytes 4194304 | tf_op jit(solution)/shard_map/tail/pallas_call | solution.py:43
  55.3 0.2 collective-permute-done.4.half_ref
  55.5 1.0 %other_half.1 = (f32[512,512]{1,0:T(8,128)}, f32[512,512]{1,0:T(8,128)}) custom-call(bf16[512,512]{1,0:T(8,128)(2,1)S(1)} %collective-permute-done.4.half_ref, f32[512,512]{1,0:T(8,128)} %get-tuple-element.43.self_in, f32[512,512]{1,0:T(8,128)} %get-tuple-element.44.neigh_in), custom_call_target="tpu_custom_call", output_to_operand_aliasing={{0}: (1, {}), {1}: (2, {})} | custom-call | flops 134217728 | bytes 3145728 | tf_op jit(solution)/shard_map/other_half/pallas_call | solution.py:43
  (5 shorter events, 0.0 us)
Async XLA Ops:
  2.6 15.1 %all-to-all-start = ((bf16[32,4,512]{2,1,0:T(4,128)(2,1)}), bf16[32,4,512]{2,1,0:T(4,128)(2,1)S(1)}, u32[]{:S(2)}, u32[]{:S(2)}) async-start(bf16[32,4,512]{2,1,0:T(4,128)(2,1)} %serve.1), calls=%async_computation | async-start | bytes 262144 | tf_op jit(solution)/shard_map/all_to_all | solution.py:390
  9.9 7.7 %copy-start = (bf16[512,512]{1,0:T(8,128)(2,1)S(1)}, bf16[512,512]{1,0:T(8,128)(2,1)}, u32[]{:S(2)}) copy-start(bf16[512,512]{1,0:T(8,128)(2,1)} %w_neigh_ref.3) | copy-start | bytes 1572868
  19.4 2.2 %collective-permute-start = (bf16[512,512]{1,0:T(8,128)(2,1)S(1)}, bf16[512,512]{1,0:T(8,128)(2,1)S(1)}, u32[]{:S(2)}, u32[]{:S(2)}) collective-permute-start(bf16[512,512]{1,0:T(8,128)(2,1)S(1)} %get-tuple-element.34), channel_id=1, source_target_pairs={{0,8},{1,9},{2,10},{3,11},{4,12},{5,13},{6,14},{7,15},{8,0},{9,1},... | collective-permute-start | bytes 1572872 | tf_op jit(solution)/shard_map/ppermute | solution.py:419
  20.2 1.4 %collective-permute-start.1 = (bf16[72,512]{1,0:T(8,128)(2,1)S(1)}, bf16[72,512]{1,0:T(8,128)(2,1)S(1)}, u32[]{:S(2)}, u32[]{:S(2)}) collective-permute-start(bf16[72,512]{1,0:T(8,128)(2,1)S(1)} %get-tuple-element.36), channel_id=1, source_target_pairs={{0,8},{1,9},{2,10},{3,11},{4,12},{5,13},{6,14},{7,15},{8,0},{9,1},... | collective-permute-start | bytes 221192 | tf_op jit(solution)/shard_map/ppermute | solution.py:426
  36.3 5.9 %collective-permute-start.3 = (bf16[64,512]{1,0:T(8,128)(2,1)S(1)}, bf16[64,512]{1,0:T(8,128)(2,1)S(1)}, u32[]{:S(2)}, u32[]{:S(2)}) collective-permute-start(bf16[64,512]{1,0:T(8,128)(2,1)S(1)} %get-tuple-element.41.keep_ref), channel_id=1, source_target_pairs={{0,4},{1,5},{2,6},{3,7},{4,0},{5,1},{6,2},{7,3},{8,12},{9,13},{10,... | collective-permute-start | bytes 196616 | tf_op jit(solution)/shard_map/ppermute | solution.py:448
  43.0 10.5 %all-to-all-start.2 = ((bf16[8,64,512]{2,1,0:T(8,128)(2,1)}), bf16[8,64,512]{2,1,0:T(8,128)(2,1)S(1)}, u32[]{:S(2)}, u32[]{:S(2)}) async-start(bf16[8,64,512]{2,1,0:T(8,128)(2,1)} %total.1), calls=%async_computation.2 | async-start | bytes 1048576 | tf_op jit(solution)/shard_map/all_to_all | solution.py:454
  48.1 5.4 %collective-permute-start.2 = (bf16[72,512]{1,0:T(8,128)(2,1)S(1)}, bf16[72,512]{1,0:T(8,128)(2,1)S(1)}, u32[]{:S(2)}, u32[]{:S(2)}) collective-permute-start(bf16[72,512]{1,0:T(8,128)(2,1)S(1)} %get-tuple-element.39), channel_id=1, source_target_pairs={{0,4},{1,5},{2,6},{3,7},{4,0},{5,1},{6,2},{7,3},{8,12},{9,13},{10,... | collective-permute-start | bytes 221192 | tf_op jit(solution)/shard_map/ppermute | solution.py:449
  53.5 2.0 %collective-permute-start.4 = (bf16[512,512]{1,0:T(8,128)(2,1)S(1)}, bf16[512,512]{1,0:T(8,128)(2,1)S(1)}, u32[]{:S(2)}, u32[]{:S(2)}) collective-permute-start(bf16[512,512]{1,0:T(8,128)(2,1)S(1)} %after_rows.1.mine_ref), channel_id=1, source_target_pairs={{0,8},{1,9},{2,10},{3,11},{4,12},{5,13},{6,14},{7,15},{8,0},{9,1},... | collective-permute-start | bytes 1572872 | tf_op jit(solution)/shard_map/ppermute | solution.py:458

commit v10 on v9

--- a/solution.py
+++ b/solution.py
@@ -286,15 +286,15 @@
         upper[order[peer]] = rest[pair : 2 * pair]
         bias = bias + join_two(rest[2 * pair :])
     grads_ref[...] = grads.astype(BF16)
-    bias = split_in_two(bias)
+    bias = split_in_two(bias).astype(F32)
     first = wide_of(dims[1]) == 0
     lower, upper = jnp.concatenate(lower, axis=0), jnp.concatenate(upper, axis=0)
     for ref, rows in (
         (keep_ref, jnp.where(first, lower, upper)),
         (send_ref, jnp.where(first, upper, lower)),
     ):
-        ref[:count, :] = rows.astype(BF16)
-        ref[count:, :] = bias
+        both = jnp.concatenate([rows, bias], axis=0)[: count + 4]
+        ref[...] = both.reshape(ref.shape).astype(BF16)
 
 
 def total_kernel(keep_ref, received_ref, after_ref, out_ref):
@@ -331,10 +331,13 @@
     everything = pl.ds(0, own_rows)
     wide_ref[...] = mine_ref[...].astype(F32) * factor
     send_half(matrix, wide_ref, self_hbm, neigh_hbm, sems.at[0], everything, False)
-    bias_ref[...] = (join_two(keep_ref[half:, :]) + join_two(received_ref[half:, :])) * factor
+    kept, received = (
+        ref[...].astype(F32).reshape(half + 4, -1) for ref in (keep_ref, received_ref)
+    )
+    bias_ref[...] = (join_two(kept[half:]) + join_two(received[half:])) * factor
     copies = [pltpu.make_async_copy(bias_ref, bias_hbm, sems.at[1])]
     copies[0].start()
-    rows = jnp.concatenate([keep_ref[:half, :], received_ref[:half, :]], axis=0)
+    rows = jnp.concatenate([kept[:half], received[:half]], axis=0).astype(BF16)
     row = lax.broadcasted_iota(jnp.int32, (own_rows, slots), 0)
     picks = (row == order_ref[...]).astype(F32).astype(BF16)
     out_ref[...] = base_ref[...] + product(picks, rows, 1, 0)
@@ -440,7 +443,7 @@
     )(received, keep, received_rows, keep_rows)
     arrived = lax.all_to_all(payload, "node", 0, 0, axis_index_groups=cubes, tiled=True)
     grads = shape((share, width), BF16)
-    pairs = shape((half + 8, width), BF16)
+    pairs = shape((half // 4 + 1, 4, width), BF16)
     keep_grads, keep_sum, send_sum = call(
         "sum_shares", functools.partial(sum_kernel, dims, chips), (VMEM,),
         ((grads, VMEM), (pairs, VMEM), (pairs, VMEM)), flops=work // 8, moved=1 << 20,

time: 56.9 us -> 56.9 us (level)
  no operation moved by 1% of the time
where the time goes in v10:
time: 56.9 us; the launch traced here: 56.5 us
  Pallas kernels  15.1 us (27%)
  starting transfers between devices  15.1 us (27%)
  blocking collectives  14.2 us (25%)
  waiting for transfers between devices  11.4 us (20%)
  between operations  0.72 us (1%)
    pallas_call x12, Pallas kernels, held(): run(*(pltpu.with_memory_space_constraint(operand, HBM) if memory is HBM e...  15.1 us
    all_to_all x1, blocking collectives, local(): lax.all_to_all(payload, 'node', 0, 0, axis_index_groups=cubes, tiled=True)  14.2 us
    all_to_all x1, starting transfers between devices, local(): incoming = lax.all_to_all(outgoing, 'node', 0, 0, tiled=True)  7.3 us
    all_to_all x1, starting transfers between devices, local(): lax.all_to_all(total, 'node', 0, 0, axis_index_groups=gather_cubes, tiled...  5.1 us
    ppermute x1, waiting for transfers between devices, local(): received_sum = lax.ppermute(send_sum, 'node', swap_wide)  4.7 us
    all_to_all x1, waiting for transfers between devices, local(): incoming = lax.all_to_all(outgoing, 'node', 0, 0, tiled=True)  4.49 us
    ppermute x1, waiting for transfers between devices, local(): received_grads = lax.ppermute(keep_grads, 'node', swap_wide)  1.62 us
    ppermute x1, starting transfers between devices, local(): received_grads = lax.ppermute(keep_grads, 'node', swap_wide)  1.35 us
  transfers between devices with their start and end apart: 7, of which 5 were waited for; matrix products, arithmetic and copies ran while one was open for 0% of the time, Pallas kernels for 16%

profile of v10, /device:TPU:0, one launch (start us, length us, event | category | flops | bytes accessed | tf_op | source)
XLA Modules:
  0.0 56.5 jit_solution(714462859386103157)
XLA Ops:
  0.6 2.0 %serve.1 = bf16[32,4,512]{2,1,0:T(4,128)(2,1)} custom-call(s32[1,128]{1,0:T(1,128)} %serve_hbm.3, bf16[512,512]{1,0:T(8,128)(2,1)} %features_hbm.5), custom_call_target="tpu_custom_call" | custom-call | flops 67108864 | bytes 1048576 | tf_op jit(solution)/shard_map/serve/pallas_call | solution.py:43
  2.6 7.3 %all-to-all-start = ((bf16[32,4,512]{2,1,0:T(4,128)(2,1)}), bf16[32,4,512]{2,1,0:T(4,128)(2,1)S(1)}, u32[]{:S(2)}, u32[]{:S(2)}) async-start(bf16[32,4,512]{2,1,0:T(4,128)(2,1)} %serve.1), calls=%async_computation | async-start | bytes 262144 | tf_op jit(solution)/shard_map/all_to_all | solution.py:393
  9.9 3.2 %own_aggregate.1 = (f32[512,512]{1,0:T(8,128)S(1)}, bf16[512,128]{1,0:T(8,128)(2,1)S(1)}, bf16[128,512]{1,0:T(8,128)(2,1)S(1)}, f32[512,128]{1,0:T(8,128)S(1)}, f32[512,512]{1,0:T(8,128)S(1)}) custom-call(s32[16,512]{1,0:T(8,128)} %bitcast.6, s32[1,512]{1,0:T(1,128)} %bitcast.9, bf16[512,512]{1,0:T(8,128)(2,1)} %features_hbm.5, bf16[512,512]{1,0:T(8,128)(2,1)} %w_self_hbm.3, ...), custom_call_target="tpu_custom_call" | custom-call | flops 5368709120 | bytes 4194304 | tf_op jit(solution)/shard_map/own_aggregate/pallas_call | solution.py:43
  13.2 4.5 %all-to-all-done.incoming_ref = bf16[32,4,512]{2,1,0:T(4,128)(2,1)S(1)} async-done(((bf16[32,4,512]{2,1,0:T(4,128)(2,1)}), bf16[32,4,512]{2,1,0:T(4,128)(2,1)S(1)}, u32[]{:S(2)}, u32[]{:S(2)}) %all-to-all-start) | async-done | bytes 131104 | tf_op jit(solution)/shard_map/all_to_all | solution.py:393
  17.7 1.7 %layer_grad.1 = (bf16[512,512]{1,0:T(8,128)(2,1)S(1)}, bf16[2,512,512]{2,1,0:T(8,128)(2,1)S(1)}, bf16[512,512]{1,0:T(8,128)(2,1)S(1)}) custom-call(bf16[32,4,512]{2,1,0:T(4,128)(2,1)S(1)} %all-to-all-done.incoming_ref, f32[512,512]{1,0:T(8,128)S(1)} %get-tuple-element.26.own_sum_ref, bf16[512,128]{1,0:T(8,128)(2,1)S(1)} %get-tuple-element.27.fetch_counts_ref, ...), custom_call_target="tpu_custom_call" | custom-call | flops 1342177280 | bytes 8388608 | tf_op jit(solution)/shard_map/layer_grad/pallas_call | solution.py:43
  19.4 0.2 collective-permute-start
  19.6 0.7 %messages.1 = (bf16[512,512]{1,0:T(8,128)(2,1)S(1)}, bf16[72,512]{1,0:T(8,128)(2,1)S(1)}, bf16[72,512]{1,0:T(8,128)(2,1)S(1)}) custom-call(bf16[512,512]{1,0:T(8,128)(2,1)S(1)} %get-tuple-element.30.pre_grad_ref, bf16[512,512]{1,0:T(8,128)(2,1)S(1)} %copy-done, f32[512,128]{1,0:T(8,128)S(1)} %get-tuple-element.28.inverse_ref, ...), custom_call_target="tpu_custom_call" | custom-call | flops 536870912 | bytes 4194304 | tf_op jit(solution)/shard_map/messages/pallas_call | solution.py:43
  20.2 0.5 collective-permute-start.1
  20.7 0.5 keep_grad.1.keep_ref
  21.2 0.4 collective-permute-done.1.received_rows_ref
  21.6 0.3 pack.1
  21.9 14.2 %all_to_all.15.payload_ref = bf16[8,21,4,512]{3,2,1,0:T(4,128)(2,1)S(1)} all-to-all(bf16[8,21,4,512]{3,2,1,0:T(4,128)(2,1)S(1)} %pack.1), channel_id=1, replica_groups={{16,17,19,18,2,3,1,0},{20,21,23,22,6,7,5,4},{24,25,27,26,10,11,9,8},{28..., dimensions={0} | all-to-all | bytes 1376256 | tf_op jit(solution)/shard_map/all_to_all | solution.py:444
  36.1 0.2 sum_shares.1
  36.3 1.4 %collective-permute-start.3 = (bf16[64,512]{1,0:T(8,128)(2,1)S(1)}, bf16[64,512]{1,0:T(8,128)(2,1)S(1)}, u32[]{:S(2)}, u32[]{:S(2)}) collective-permute-start(bf16[64,512]{1,0:T(8,128)(2,1)S(1)} %get-tuple-element.41.keep_ref), channel_id=1, source_target_pairs={{0,4},{1,5},{2,6},{3,7},{4,0},{5,1},{6,2},{7,3},{8,12},{9,13},{10,... | collective-permute-start | bytes 196616 | tf_op jit(solution)/shard_map/ppermute | solution.py:451
  37.6 3.0 %own_grad.1 = (f32[512,512]{1,0:T(8,128)S(1)}, s32[1,128]{1,0:T(1,128)S(1)}) custom-call(bf16[512,512]{1,0:T(8,128)(2,1)S(1)} %get-tuple-element.30.pre_grad_ref, bf16[512,512]{1,0:T(8,128)(2,1)S(1)} %get-tuple-element.32.message_ref, s32[16,512]{1,0:T(8,128)} %bitcast.7, s32[1,512]{1,0:T(1,128)} %bitcast.10, s32[1,128]{1,0:T(1,128)} %serve_hbm.3, ...), custom_call_target="tpu_custom_call" | custom-call | flops 536870912 | bytes 4194304 | tf_op jit(solution)/shard_map/own_grad/pallas_call | solution.py:43
  40.6 1.6 %collective-permute-done.3.received_ref = bf16[64,512]{1,0:T(8,128)(2,1)S(1)} collective-permute-done((bf16[64,512]{1,0:T(8,128)(2,1)S(1)}, bf16[64,512]{1,0:T(8,128)(2,1)S(1)}, u32[]{:S(2)}, u32[]{:S(2)}) %collective-permute-start.3) | collective-permute-done | bytes 65568 | tf_op jit(solution)/shard_map/ppermute | solution.py:451
  42.2 0.8 %total.1 = bf16[8,64,512]{2,1,0:T(8,128)(2,1)} custom-call(bf16[64,512]{1,0:T(8,128)(2,1)S(1)} %get-tuple-element.41.keep_ref, bf16[64,512]{1,0:T(8,128)(2,1)S(1)} %collective-permute-done.3.received_ref, f32[512,512]{1,0:T(8,128)S(1)} %get-tuple-element.40.after_ref.base_ref), custom_call_target="tpu_custom_call" | custom-call | flops 33554432 | bytes 1048576 | tf_op jit(solution)/shard_map/total/pallas_call | solution.py:43
  43.1 5.1 %all-to-all-start.2 = ((bf16[8,64,512]{2,1,0:T(8,128)(2,1)}), bf16[8,64,512]{2,1,0:T(8,128)(2,1)S(1)}, u32[]{:S(2)}, u32[]{:S(2)}) async-start(bf16[8,64,512]{2,1,0:T(8,128)(2,1)} %total.1), calls=%async_computation.2 | async-start | bytes 1048576 | tf_op jit(solution)/shard_map/all_to_all | solution.py:457
  48.2 0.6 %collective-permute-start.2 = (bf16[17,4,512]{2,1,0:T(4,128)(2,1)S(1)}, bf16[17,4,512]{2,1,0:T(4,128)(2,1)S(1)}, u32[]{:S(2)}, u32[]{:S(2)}) collective-permute-start(bf16[17,4,512]{2,1,0:T(4,128)(2,1)S(1)} %get-tuple-element.39), channel_id=1, source_target_pairs={{0,4},{1,5},{2,6},{3,7},{4,0},{5,1},{6,2},{7,3},{8,12},{9,13},{10,... | collective-permute-start | bytes 208904 | tf_op jit(solution)/shard_map/ppermute | solution.py:452
  48.8 4.7 %collective-permute-done.2.after_ref.received_ref = bf16[17,4,512]{2,1,0:T(4,128)(2,1)S(1)} collective-permute-done((bf16[17,4,512]{2,1,0:T(4,128)(2,1)S(1)}, bf16[17,4,512]{2,1,0:T(4,128)(2,1)S(1)}, u32[]{:S(2)}, u32[]{:S(2)}) %collective-permute-start.2) | collective-permute-done | bytes 69664 | tf_op jit(solution)/shard_map/ppermute | solution.py:452
  53.5 0.1 collective-permute-start.4
  53.6 1.7 %tail.1 = (f32[512,512]{1,0:T(8,128)}, f32[512,512]{1,0:T(8,128)}, f32[512,512]{1,0:T(8,128)}, f32[1,512]{1,0:T(1,128)}) custom-call(s32[1,128]{1,0:T(1,128)S(1)} %get-tuple-element.33.order_ref, bf16[17,4,512]{2,1,0:T(4,128)(2,1)S(1)} %get-tuple-element.38.keep_ref, bf16[17,4,512]{2,1,0:T(4,128)(2,1)S(1)} %collective-permute-done.2.after_ref.received_ref, ...), custom_call_target="tpu_custom_call" | custom-call | flops 268435456 | bytes 4194304 | tf_op jit(solution)/shard_map/tail/pallas_call | solution.py:43
  55.3 0.2 collective-permute-done.4.half_ref
  55.5 1.0 %other_half.1 = (f32[512,512]{1,0:T(8,128)}, f32[512,512]{1,0:T(8,128)}) custom-call(bf16[512,512]{1,0:T(8,128)(2,1)S(1)} %collective-permute-done.4.half_ref, f32[512,512]{1,0:T(8,128)} %get-tuple-element.43.self_in, f32[512,512]{1,0:T(8,128)} %get-tuple-element.44.neigh_in), custom_call_target="tpu_custom_call", output_to_operand_aliasing={{0}: (1, {}), {1}: (2, {})} | custom-call | flops 134217728 | bytes 3145728 | tf_op jit(solution)/shard_map/other_half/pallas_call | solution.py:43
  (5 shorter events, 0.0 us)
Async XLA Ops:
  2.6 15.1 %all-to-all-start = ((bf16[32,4,512]{2,1,0:T(4,128)(2,1)}), bf16[32,4,512]{2,1,0:T(4,128)(2,1)S(1)}, u32[]{:S(2)}, u32[]{:S(2)}) async-start(bf16[32,4,512]{2,1,0:T(4,128)(2,1)} %serve.1), calls=%async_computation | async-start | bytes 262144 | tf_op jit(solution)/shard_map/all_to_all | solution.py:393
  9.9 7.7 %copy-start = (bf16[512,512]{1,0:T(8,128)(2,1)S(1)}, bf16[512,512]{1,0:T(8,128)(2,1)}, u32[]{:S(2)}) copy-start(bf16[512,512]{1,0:T(8,128)(2,1)} %w_neigh_ref.3) | copy-start | bytes 1572868
  19.4 2.2 %collective-permute-start = (bf16[512,512]{1,0:T(8,128)(2,1)S(1)}, bf16[512,512]{1,0:T(8,128)(2,1)S(1)}, u32[]{:S(2)}, u32[]{:S(2)}) collective-permute-start(bf16[512,512]{1,0:T(8,128)(2,1)S(1)} %get-tuple-element.34), channel_id=1, source_target_pairs={{0,8},{1,9},{2,10},{3,11},{4,12},{5,13},{6,14},{7,15},{8,0},{9,1},... | collective-permute-start | bytes 1572872 | tf_op jit(solution)/shard_map/ppermute | solution.py:422
  20.2 1.4 %collective-permute-start.1 = (bf16[72,512]{1,0:T(8,128)(2,1)S(1)}, bf16[72,512]{1,0:T(8,128)(2,1)S(1)}, u32[]{:S(2)}, u32[]{:S(2)}) collective-permute-start(bf16[72,512]{1,0:T(8,128)(2,1)S(1)} %get-tuple-element.36), channel_id=1, source_target_pairs={{0,8},{1,9},{2,10},{3,11},{4,12},{5,13},{6,14},{7,15},{8,0},{9,1},... | collective-permute-start | bytes 221192 | tf_op jit(solution)/shard_map/ppermute | solution.py:429
  36.3 5.9 %collective-permute-start.3 = (bf16[64,512]{1,0:T(8,128)(2,1)S(1)}, bf16[64,512]{1,0:T(8,128)(2,1)S(1)}, u32[]{:S(2)}, u32[]{:S(2)}) collective-permute-start(bf16[64,512]{1,0:T(8,128)(2,1)S(1)} %get-tuple-element.41.keep_ref), channel_id=1, source_target_pairs={{0,4},{1,5},{2,6},{3,7},{4,0},{5,1},{6,2},{7,3},{8,12},{9,13},{10,... | collective-permute-start | bytes 196616 | tf_op jit(solution)/shard_map/ppermute | solution.py:451
  43.1 10.4 %all-to-all-start.2 = ((bf16[8,64,512]{2,1,0:T(8,128)(2,1)}), bf16[8,64,512]{2,1,0:T(8,128)(2,1)S(1)}, u32[]{:S(2)}, u32[]{:S(2)}) async-start(bf16[8,64,512]{2,1,0:T(8,128)(2,1)} %total.1), calls=%async_computation.2 | async-start | bytes 1048576 | tf_op jit(solution)/shard_map/all_to_all | solution.py:457
  48.2 5.3 %collective-permute-start.2 = (bf16[17,4,512]{2,1,0:T(4,128)(2,1)S(1)}, bf16[17,4,512]{2,1,0:T(4,128)(2,1)S(1)}, u32[]{:S(2)}, u32[]{:S(2)}) collective-permute-start(bf16[17,4,512]{2,1,0:T(4,128)(2,1)S(1)} %get-tuple-element.39), channel_id=1, source_target_pairs={{0,4},{1,5},{2,6},{3,7},{4,0},{5,1},{6,2},{7,3},{8,12},{9,13},{10,... | collective-permute-start | bytes 208904 | tf_op jit(solution)/shard_map/ppermute | solution.py:452
  53.5 2.0 %collective-permute-start.4 = (bf16[512,512]{1,0:T(8,128)(2,1)S(1)}, bf16[512,512]{1,0:T(8,128)(2,1)S(1)}, u32[]{:S(2)}, u32[]{:S(2)}) collective-permute-start(bf16[512,512]{1,0:T(8,128)(2,1)S(1)} %after_rows.1.mine_ref), channel_id=1, source_target_pairs={{0,8},{1,9},{2,10},{3,11},{4,12},{5,13},{6,14},{7,15},{8,0},{9,1},... | collective-permute-start | bytes 1572872 | tf_op jit(solution)/shard_map/ppermute | solution.py:461

commit v11 on v9

--- a/solution.py
+++ b/solution.py
@@ -347,7 +347,7 @@
 
 def other_kernel(factor, near, half_ref, self_in, neigh_in, self_hbm, neigh_hbm, wide_ref, sems):
     own_rows = half_ref.shape[0]
-    pieces = 4
+    pieces = 1
     length = own_rows // pieces
     matrix = 1 - core_of(near)
     spans = [pl.ds(at * length, length) for at in range(pieces)]

time: 56.9 us -> 57 us (level)
  no operation moved by 1% of the time
where the time goes in v11:
time: 57 us; the launch traced here: 56.6 us
  Pallas kernels  15.1 us (26%)
  starting transfers between devices  15.1 us (26%)
  blocking collectives  14.2 us (25%)
  waiting for transfers between devices  11.5 us (20%)
  between operations  0.72 us (1%)
    pallas_call x12, Pallas kernels, held(): run(*(pltpu.with_memory_space_constraint(operand, HBM) if memory is HBM e...  15.1 us
    all_to_all x1, blocking collectives, local(): lax.all_to_all(payload, 'node', 0, 0, axis_index_groups=cubes, tiled=True)  14.2 us
    all_to_all x1, starting transfers between devices, local(): incoming = lax.all_to_all(outgoing, 'node', 0, 0, tiled=True)  7.3 us
    all_to_all x1, starting transfers between devices, local(): lax.all_to_all(total, 'node', 0, 0, axis_index_groups=gather_cubes, tiled...  5.1 us
    ppermute x1, waiting for transfers between devices, local(): received_sum = lax.ppermute(send_sum, 'node', swap_wide)  4.75 us
    all_to_all x1, waiting for transfers between devices, local(): incoming = lax.all_to_all(outgoing, 'node', 0, 0, tiled=True)  4.49 us
    ppermute x1, waiting for transfers between devices, local(): received_grads = lax.ppermute(keep_grads, 'node', swap_wide)  1.62 us
    ppermute x1, starting transfers between devices, local(): received_grads = lax.ppermute(keep_grads, 'node', swap_wide)  1.35 us
  transfers between devices with their start and end apart: 7, of which 5 were waited for; matrix products, arithmetic and copies ran while one was open for 0% of the time, Pallas kernels for 16%

profile of v11, /device:TPU:0, one launch (start us, length us, event | category | flops | bytes accessed | tf_op | source)
XLA Modules:
  0.0 56.6 jit_solution(10465575429720459749)
XLA Ops:
  0.6 2.0 %serve.1 = bf16[32,4,512]{2,1,0:T(4,128)(2,1)} custom-call(s32[1,128]{1,0:T(1,128)} %serve_hbm.3, bf16[512,512]{1,0:T(8,128)(2,1)} %features_hbm.5), custom_call_target="tpu_custom_call" | custom-call | flops 67108864 | bytes 1048576 | tf_op jit(solution)/shard_map/serve/pallas_call | solution.py:43
  2.6 7.3 %all-to-all-start = ((bf16[32,4,512]{2,1,0:T(4,128)(2,1)}), bf16[32,4,512]{2,1,0:T(4,128)(2,1)S(1)}, u32[]{:S(2)}, u32[]{:S(2)}) async-start(bf16[32,4,512]{2,1,0:T(4,128)(2,1)} %serve.1), calls=%async_computation | async-start | bytes 262144 | tf_op jit(solution)/shard_map/all_to_all | solution.py:390
  9.9 3.2 %own_aggregate.1 = (f32[512,512]{1,0:T(8,128)S(1)}, bf16[512,128]{1,0:T(8,128)(2,1)S(1)}, bf16[128,512]{1,0:T(8,128)(2,1)S(1)}, f32[512,128]{1,0:T(8,128)S(1)}, f32[512,512]{1,0:T(8,128)S(1)}) custom-call(s32[16,512]{1,0:T(8,128)} %bitcast.6, s32[1,512]{1,0:T(1,128)} %bitcast.9, bf16[512,512]{1,0:T(8,128)(2,1)} %features_hbm.5, bf16[512,512]{1,0:T(8,128)(2,1)} %w_self_hbm.3, ...), custom_call_target="tpu_custom_call" | custom-call | flops 5368709120 | bytes 4194304 | tf_op jit(solution)/shard_map/own_aggregate/pallas_call | solution.py:43
  13.2 4.5 %all-to-all-done.incoming_ref = bf16[32,4,512]{2,1,0:T(4,128)(2,1)S(1)} async-done(((bf16[32,4,512]{2,1,0:T(4,128)(2,1)}), bf16[32,4,512]{2,1,0:T(4,128)(2,1)S(1)}, u32[]{:S(2)}, u32[]{:S(2)}) %all-to-all-start) | async-done | bytes 131104 | tf_op jit(solution)/shard_map/all_to_all | solution.py:390
  17.7 1.7 %layer_grad.1 = (bf16[512,512]{1,0:T(8,128)(2,1)S(1)}, bf16[2,512,512]{2,1,0:T(8,128)(2,1)S(1)}, bf16[512,512]{1,0:T(8,128)(2,1)S(1)}) custom-call(bf16[32,4,512]{2,1,0:T(4,128)(2,1)S(1)} %all-to-all-done.incoming_ref, f32[512,512]{1,0:T(8,128)S(1)} %get-tuple-element.26.own_sum_ref, bf16[512,128]{1,0:T(8,128)(2,1)S(1)} %get-tuple-element.27.fetch_counts_ref, ...), custom_call_target="tpu_custom_call" | custom-call | flops 1342177280 | bytes 8388608 | tf_op jit(solution)/shard_map/layer_grad/pallas_call | solution.py:43
  19.4 0.2 collective-permute-start
  19.6 0.7 %messages.1 = (bf16[512,512]{1,0:T(8,128)(2,1)S(1)}, bf16[72,512]{1,0:T(8,128)(2,1)S(1)}, bf16[72,512]{1,0:T(8,128)(2,1)S(1)}) custom-call(bf16[512,512]{1,0:T(8,128)(2,1)S(1)} %get-tuple-element.30.pre_grad_ref, bf16[512,512]{1,0:T(8,128)(2,1)S(1)} %copy-done, f32[512,128]{1,0:T(8,128)S(1)} %get-tuple-element.28.inverse_ref, ...), custom_call_target="tpu_custom_call" | custom-call | flops 536870912 | bytes 4194304 | tf_op jit(solution)/shard_map/messages/pallas_call | solution.py:43
  20.2 0.5 collective-permute-start.1
  20.7 0.5 keep_grad.1.keep_ref
  21.2 0.4 collective-permute-done.1.received_rows_ref
  21.6 0.3 pack.1
  21.9 14.2 %all_to_all.15.payload_ref = bf16[8,21,4,512]{3,2,1,0:T(4,128)(2,1)S(1)} all-to-all(bf16[8,21,4,512]{3,2,1,0:T(4,128)(2,1)S(1)} %pack.1), channel_id=1, replica_groups={{16,17,19,18,2,3,1,0},{20,21,23,22,6,7,5,4},{24,25,27,26,10,11,9,8},{28..., dimensions={0} | all-to-all | bytes 1376256 | tf_op jit(solution)/shard_map/all_to_all | solution.py:441
  36.1 0.1 sum_shares.1
  36.3 1.4 %collective-permute-start.3 = (bf16[64,512]{1,0:T(8,128)(2,1)S(1)}, bf16[64,512]{1,0:T(8,128)(2,1)S(1)}, u32[]{:S(2)}, u32[]{:S(2)}) collective-permute-start(bf16[64,512]{1,0:T(8,128)(2,1)S(1)} %get-tuple-element.41.keep_ref), channel_id=1, source_target_pairs={{0,4},{1,5},{2,6},{3,7},{4,0},{5,1},{6,2},{7,3},{8,12},{9,13},{10,... | collective-permute-start | bytes 196616 | tf_op jit(solution)/shard_map/ppermute | solution.py:448
  37.6 3.0 %own_grad.1 = (f32[512,512]{1,0:T(8,128)S(1)}, s32[1,128]{1,0:T(1,128)S(1)}) custom-call(bf16[512,512]{1,0:T(8,128)(2,1)S(1)} %get-tuple-element.30.pre_grad_ref, bf16[512,512]{1,0:T(8,128)(2,1)S(1)} %get-tuple-element.32.message_ref, s32[16,512]{1,0:T(8,128)} %bitcast.7, s32[1,512]{1,0:T(1,128)} %bitcast.10, s32[1,128]{1,0:T(1,128)} %serve_hbm.3, ...), custom_call_target="tpu_custom_call" | custom-call | flops 536870912 | bytes 4194304 | tf_op jit(solution)/shard_map/own_grad/pallas_call | solution.py:43
  40.6 1.6 %collective-permute-done.3.received_ref = bf16[64,512]{1,0:T(8,128)(2,1)S(1)} collective-permute-done((bf16[64,512]{1,0:T(8,128)(2,1)S(1)}, bf16[64,512]{1,0:T(8,128)(2,1)S(1)}, u32[]{:S(2)}, u32[]{:S(2)}) %collective-permute-start.3) | collective-permute-done | bytes 65568 | tf_op jit(solution)/shard_map/ppermute | solution.py:448
  42.2 0.8 %total.1 = bf16[8,64,512]{2,1,0:T(8,128)(2,1)} custom-call(bf16[64,512]{1,0:T(8,128)(2,1)S(1)} %get-tuple-element.41.keep_ref, bf16[64,512]{1,0:T(8,128)(2,1)S(1)} %collective-permute-done.3.received_ref, f32[512,512]{1,0:T(8,128)S(1)} %get-tuple-element.40.after_ref.base_ref), custom_call_target="tpu_custom_call" | custom-call | flops 33554432 | bytes 1048576 | tf_op jit(solution)/shard_map/total/pallas_call | solution.py:43
  43.0 5.1 %all-to-all-start.2 = ((bf16[8,64,512]{2,1,0:T(8,128)(2,1)}), bf16[8,64,512]{2,1,0:T(8,128)(2,1)S(1)}, u32[]{:S(2)}, u32[]{:S(2)}) async-start(bf16[8,64,512]{2,1,0:T(8,128)(2,1)} %total.1), calls=%async_computation.2 | async-start | bytes 1048576 | tf_op jit(solution)/shard_map/all_to_all | solution.py:454
  48.1 0.6 %collective-permute-start.2 = (bf16[72,512]{1,0:T(8,128)(2,1)S(1)}, bf16[72,512]{1,0:T(8,128)(2,1)S(1)}, u32[]{:S(2)}, u32[]{:S(2)}) collective-permute-start(bf16[72,512]{1,0:T(8,128)(2,1)S(1)} %get-tuple-element.39), channel_id=1, source_target_pairs={{0,4},{1,5},{2,6},{3,7},{4,0},{5,1},{6,2},{7,3},{8,12},{9,13},{10,... | collective-permute-start | bytes 221192 | tf_op jit(solution)/shard_map/ppermute | solution.py:449
  48.7 4.8 %collective-permute-done.2.after_ref.received_ref = bf16[72,512]{1,0:T(8,128)(2,1)S(1)} collective-permute-done((bf16[72,512]{1,0:T(8,128)(2,1)S(1)}, bf16[72,512]{1,0:T(8,128)(2,1)S(1)}, u32[]{:S(2)}, u32[]{:S(2)}) %collective-permute-start.2) | collective-permute-done | bytes 73760 | tf_op jit(solution)/shard_map/ppermute | solution.py:449
  53.5 0.1 collective-permute-start.4
  53.6 1.7 %tail.1 = (f32[512,512]{1,0:T(8,128)}, f32[512,512]{1,0:T(8,128)}, f32[512,512]{1,0:T(8,128)}, f32[1,512]{1,0:T(1,128)}) custom-call(s32[1,128]{1,0:T(1,128)S(1)} %get-tuple-element.33.order_ref, bf16[72,512]{1,0:T(8,128)(2,1)S(1)} %get-tuple-element.38.keep_ref, bf16[72,512]{1,0:T(8,128)(2,1)S(1)} %collective-permute-done.2.after_ref.received_ref, ...), custom_call_target="tpu_custom_call" | custom-call | flops 268435456 | bytes 4194304 | tf_op jit(solution)/shard_map/tail/pallas_call | solution.py:43
  55.3 0.2 collective-permute-done.4.half_ref
  55.5 1.1 %other_half.1 = (f32[512,512]{1,0:T(8,128)}, f32[512,512]{1,0:T(8,128)}) custom-call(bf16[512,512]{1,0:T(8,128)(2,1)S(1)} %collective-permute-done.4.half_ref, f32[512,512]{1,0:T(8,128)} %get-tuple-element.43.self_in, f32[512,512]{1,0:T(8,128)} %get-tuple-element.44.neigh_in), custom_call_target="tpu_custom_call", output_to_operand_aliasing={{0}: (1, {}), {1}: (2, {})} | custom-call | flops 134217728 | bytes 3145728 | tf_op jit(solution)/shard_map/other_half/pallas_call | solution.py:43
  (5 shorter events, 0.0 us)
Async XLA Ops:
  2.6 15.1 %all-to-all-start = ((bf16[32,4,512]{2,1,0:T(4,128)(2,1)}), bf16[32,4,512]{2,1,0:T(4,128)(2,1)S(1)}, u32[]{:S(2)}, u32[]{:S(2)}) async-start(bf16[32,4,512]{2,1,0:T(4,128)(2,1)} %serve.1), calls=%async_computation | async-start | bytes 262144 | tf_op jit(solution)/shard_map/all_to_all | solution.py:390
  9.9 7.7 %copy-start = (bf16[512,512]{1,0:T(8,128)(2,1)S(1)}, bf16[512,512]{1,0:T(8,128)(2,1)}, u32[]{:S(2)}) copy-start(bf16[512,512]{1,0:T(8,128)(2,1)} %w_neigh_ref.3) | copy-start | bytes 1572868
  19.4 2.2 %collective-permute-start = (bf16[512,512]{1,0:T(8,128)(2,1)S(1)}, bf16[512,512]{1,0:T(8,128)(2,1)S(1)}, u32[]{:S(2)}, u32[]{:S(2)}) collective-permute-start(bf16[512,512]{1,0:T(8,128)(2,1)S(1)} %get-tuple-element.34), channel_id=1, source_target_pairs={{0,8},{1,9},{2,10},{3,11},{4,12},{5,13},{6,14},{7,15},{8,0},{9,1},... | collective-permute-start | bytes 1572872 | tf_op jit(solution)/shard_map/ppermute | solution.py:419
  20.2 1.4 %collective-permute-start.1 = (bf16[72,512]{1,0:T(8,128)(2,1)S(1)}, bf16[72,512]{1,0:T(8,128)(2,1)S(1)}, u32[]{:S(2)}, u32[]{:S(2)}) collective-permute-start(bf16[72,512]{1,0:T(8,128)(2,1)S(1)} %get-tuple-element.36), channel_id=1, source_target_pairs={{0,8},{1,9},{2,10},{3,11},{4,12},{5,13},{6,14},{7,15},{8,0},{9,1},... | collective-permute-start | bytes 221192 | tf_op jit(solution)/shard_map/ppermute | solution.py:426
  36.3 5.9 %collective-permute-start.3 = (bf16[64,512]{1,0:T(8,128)(2,1)S(1)}, bf16[64,512]{1,0:T(8,128)(2,1)S(1)}, u32[]{:S(2)}, u32[]{:S(2)}) collective-permute-start(bf16[64,512]{1,0:T(8,128)(2,1)S(1)} %get-tuple-element.41.keep_ref), channel_id=1, source_target_pairs={{0,4},{1,5},{2,6},{3,7},{4,0},{5,1},{6,2},{7,3},{8,12},{9,13},{10,... | collective-permute-start | bytes 196616 | tf_op jit(solution)/shard_map/ppermute | solution.py:448
  43.0 10.5 %all-to-all-start.2 = ((bf16[8,64,512]{2,1,0:T(8,128)(2,1)}), bf16[8,64,512]{2,1,0:T(8,128)(2,1)S(1)}, u32[]{:S(2)}, u32[]{:S(2)}) async-start(bf16[8,64,512]{2,1,0:T(8,128)(2,1)} %total.1), calls=%async_computation.2 | async-start | bytes 1048576 | tf_op jit(solution)/shard_map/all_to_all | solution.py:454
  48.1 5.4 %collective-permute-start.2 = (bf16[72,512]{1,0:T(8,128)(2,1)S(1)}, bf16[72,512]{1,0:T(8,128)(2,1)S(1)}, u32[]{:S(2)}, u32[]{:S(2)}) collective-permute-start(bf16[72,512]{1,0:T(8,128)(2,1)S(1)} %get-tuple-element.39), channel_id=1, source_target_pairs={{0,4},{1,5},{2,6},{3,7},{4,0},{5,1},{6,2},{7,3},{8,12},{9,13},{10,... | collective-permute-start | bytes 221192 | tf_op jit(solution)/shard_map/ppermute | solution.py:449
  53.5 2.0 %collective-permute-start.4 = (bf16[512,512]{1,0:T(8,128)(2,1)S(1)}, bf16[512,512]{1,0:T(8,128)(2,1)S(1)}, u32[]{:S(2)}, u32[]{:S(2)}) collective-permute-start(bf16[512,512]{1,0:T(8,128)(2,1)S(1)} %after_rows.1.mine_ref), channel_id=1, source_target_pairs={{0,8},{1,9},{2,10},{3,11},{4,12},{5,13},{6,14},{7,15},{8,0},{9,1},... | collective-permute-start | bytes 1572872 | tf_op jit(solution)/shard_map/ppermute | solution.py:458
